TPU v7x, 512 devices: a whole 4x4x16 slice. The times are simulated.
512 devices in a mesh: node: 64 (over y, x, z_lo), rel: 8 (over z_hi, core).
Axes of the slice: x: 4, y: 4, z: 16 (z_hi: 4, z_lo: 4; z = z_hi * 4 + z_lo), core: 2. Of those that a mesh axis runs over, the one named last changes fastest.
Arguments:
- features: bfloat16 [8, 1024, 768], P('rel', 'node'), may hold values from -6 to 6
- bases: bfloat16 [30, 768, 1024], P(None, 'node', 'rel'), may hold values from -0.21875 to 0.21875
- coefficients: float32 [6, 30], replicated, may hold values from -0.4375 to 0.4375
- tile_values: bfloat16 [64, 8, 56, 128, 128], P('node', 'rel'), may hold values from -0.03125 to 0.03125
- tile_source: int32 [64, 8, 56], P('node', 'rel'), may hold values from 0 to 7
- tile_relation: int32 [64, 8, 56], P('node', 'rel'), may hold values from 0 to 4
- tile_count: int32 [64, 8], P('node', 'rel'), may hold values from 14 to 56, as said below
Outputs:
- layer_output: bfloat16 [8, 1024, 1024], P('rel', 'node')
Inputs may be any that keep to these rules, and one draw needn't show every extreme that they name: `tile_count`: the live slots of each stretch and group are its first ones; in every draw some stretch and group has all 56 slots live.
All inputs are finite; a program needn't handle non-finite values.
Results may differ from a plain program's by a relative error of at most 0.0054.
Values may be sent and summed in bfloat16 or wider, within the bound.
No kernel may reach another device: no remote copies, remote signals or barrier semaphores. Data moves between devices by JAX's collectives and lax.ppermute only.
A program may use at most 64 MiB of HBM per device.

v0:
```python
import jax
import jax.numpy as jnp
from jax import lax
from jax.sharding import PartitionSpec as P

TILE = 128


batch_tiles = 8


def sent_to_all(shard, axis):
    copies = jnp.broadcast_to(shard, (lax.axis_size(axis), *shard.shape))
    return lax.all_to_all(copies, axis, split_axis=0, concat_axis=0, tiled=True)


def joined_along(pieces, dim):
    lengths = list(pieces.shape[1:])
    lengths[dim] *= pieces.shape[0]
    return jnp.moveaxis(pieces, 0, dim).reshape(lengths)


def gathered_copies(shard, axis, dim):
    pieces = sent_to_all(shard, axis)
    return joined_along(pieces, dim)


def on_device(features, bases, coefficients, tile_values, tile_source, tile_relation, tile_count):
    relations = coefficients.shape[0] - 1
    nbases, din_part, dout_part = bases.shape
    stacked = jnp.dot(
        coefficients,
        bases.reshape(nbases, din_part * dout_part).astype(jnp.float32),
        precision=lax.Precision.HIGHEST,
    )
    weight_part = stacked.astype(jnp.bfloat16).reshape(relations + 1, din_part, dout_part)
    own_rows = features[0]
    row_count, in_width = own_rows.shape
    gathered = gathered_copies(features, "node", 1)[0]
    blocks = gathered.reshape(-1, TILE, in_width)
    values = tile_values[0, 0]
    sources = tile_source[0, 0]
    relation_ids = tile_relation[0, 0]
    live_count = tile_count[0, 0]
    dest_rows = values.shape[1]
    kind_ids = jnp.arange(relations, dtype=jnp.int32)

    def accumulate(step_index, aggregate):
        first_slot = step_index * batch_tiles
        tile_block = lax.dynamic_slice_in_dim(values, first_slot, batch_tiles, 0)
        source_ids = lax.dynamic_slice_in_dim(sources, first_slot, batch_tiles, 0)
        labels = lax.dynamic_slice_in_dim(relation_ids, first_slot, batch_tiles, 0)
        picked = jnp.take(blocks, source_ids, axis=0)
        products = jnp.einsum(
            "sab,sbd->sad", tile_block, picked, preferred_element_type=jnp.float32
        )
        live_slots = first_slot + jnp.arange(batch_tiles, dtype=jnp.int32) < live_count
        select = ((labels[:, None] == kind_ids[None, :]) & live_slots[:, None]).astype(jnp.float32)
        return aggregate + jnp.einsum(
            "sr,sad->ard", select, products, precision=lax.Precision.HIGHEST
        )

    turn_count = (live_count + batch_tiles - 1) // batch_tiles
    aggregate = lax.fori_loop(
        0, turn_count, accumulate, jnp.zeros((dest_rows, relations, in_width), jnp.float32)
    )
    weight_rows = gathered_copies(weight_part, "node", 1)
    group_index = lax.axis_index("rel")
    self_part = lax.dynamic_update_slice(
        jnp.zeros((dest_rows, 1, in_width), jnp.float32),
        own_rows.astype(jnp.float32)[:, None, :],
        (group_index * row_count, 0, 0),
    )
    summed = lax.psum(jnp.concatenate([aggregate, self_part], axis=1), "rel")
    messages = summed.astype(jnp.bfloat16).reshape(dest_rows, -1)
    columns = jnp.dot(
        messages, weight_rows.reshape(-1, dout_part), preferred_element_type=jnp.float32
    )
    local_cols = jnp.maximum(columns, 0.0).astype(jnp.bfloat16)
    return lax.all_to_all(local_cols, "rel", split_axis=0, concat_axis=1, tiled=True)[None]


def solution(mesh):
    return jax.shard_map(
        on_device,
        mesh=mesh,
        in_specs=(
            P("rel", "node", None),
            P(None, "node", "rel"),
            P(),
            P("node", "rel", None, None, None),
            P("node", "rel", None),
            P("node", "rel", None),
            P("node", "rel"),
        ),
        out_specs=P("rel", "node", None),
        check_vma=False,
    )
```

profile of v0, /device:TPU:78, one launch (start us, length us, event | category | flops | bytes accessed | tf_op | source)
XLA Modules:
  0.0 317.2 jit_solution(13572898944553832154)
XLA Ops:
  0.0 0.0 copy-start
  0.0 0.9 copy.17
  1.0 0.0 copy-done
  1.0 0.2 convolution_convert_fusion
  1.2 0.2 broadcast_in_dim.34
  1.5 0.0 copy-start.1
  1.5 47.0 %all_to_all.26 = bf16[64,6,12,128]{3,2,1,0:T(8,128)(2,1)S(1)} all-to-all(bf16[64,6,12,128]{3,2,1,0:T(8,128)(2,1)S(1)} %broadcast_in_dim.34), channel_id=1, replica_groups=mesh['node'=64,'rel'=8] {'node'}, dimensions={0} | all-to-all | bytes 2359296 | tf_op jit(solution)/shard_map/all_to_all | solution.py:14
  48.4 0.0 copy-done.1
  48.4 1.3 broadcast_in_dim.32
  49.7 9.3 %all-to-all-start = ((bf16[64,1,16,768]{3,2,1,0:T(8,128)(2,1)}), bf16[64,1,16,768]{3,2,1,0:T(8,128)(2,1)S(1)}, u32[]{:S(2)}, u32[]{:S(2)}) async-start(bf16[64,1,16,768]{3,2,1,0:T(8,128)(2,1)} %broadcast_in_dim.32), calls=%async_computation | async-start | bytes 3145728 | tf_op jit(solution)/shard_map/all_to_all | solution.py:14
  59.6 0.2 copy.15
  59.8 0.8 bitcast_convert_fusion
  60.6 3.5 %dynamic_update_slice.3 = f32[128,1,768]{0,2,1:T(8,128)S(1)} dynamic-update-slice(f32[128,1,768]{0,2,1:T(8,128)S(1)} %broadcast_in_dim.33, f32[16,1,768]{0,2,1:T(8,128)} %bitcast_convert_fusion, s32[]{:T(128)S(6)} %select_n.23, s32[]{:T(128)} %constant.45.clone.1, s32[]{:T(128)} %constant.45.clone.1) | dynamic-update-slice | bytes 98308 | tf_op jit(solution)/shard_map/dynamic_update_slice | solution.py:69
  64.1 1.4 copy.18
  65.5 3.2 %reshape_reshape.3 = bf16[4608,128]{1,0:T(8,128)(2,1)} reshape(bf16[6,64,12,128]{3,2,1,0:T(8,128)(2,1)} %copy.18) | data formatting | bytes 2359296 | tf_op jit(solution)/shard_map/reshape;reshape | solution.py:77
  68.8 25.5 %all-to-all-done = bf16[64,1,16,768]{3,2,1,0:T(8,128)(2,1)S(1)} async-done(((bf16[64,1,16,768]{3,2,1,0:T(8,128)(2,1)}), bf16[64,1,16,768]{3,2,1,0:T(8,128)(2,1)S(1)}, u32[]{:S(2)}, u32[]{:S(2)}) %all-to-all-start) | async-done | bytes 1572896 | tf_op jit(solution)/shard_map/all_to_all | solution.py:14
  94.3 1.8 broadcast_in_dim.31
  96.1 31.9 %while.11 = (s32[]{:T(128)}, f32[128,5,768]{2,1,0:T(8,128)}, s32[]{:T(128)}, bf16[56,128,128]{2,1,0:T(8,128)(2,1)}, s32[56]{0:T(128)}, /*index=5*/bf16[8,128,768...) while((s32[]{:T(128)}, f32[128,5,768]{2,1,0:T(8,128)}, ...), condition=%wide.region_1.2_spmd.clone, body=%wide.region_0.1_spmd.clone.sunk | while | flops 249791632 | bytes 15209811 | solution.py:64
  96.1 1.4 compare_and_fusion.2
  97.5 0.6 gather_fusion
  98.1 0.0 copy-start.2
  98.2 1.6 fusion.32
  99.7 0.0 copy-done.2
  99.8 0.1 dynamic_slice.19
  99.8 6.9 %bitcast_add_fusion.2 = f32[128,5,768]{2,1,0:T(8,128)} fusion(f32[128,5,768]{2,1,0:T(8,128)} %get-tuple-element.161, f32[8,128,768]{2,1,0:T(8,128)S(1)} %fusion.32, s32[8]{0:T(128)S(1)} %dynamic_slice.19, pred[8]{0:T(512)(128)(4,1)S(1)} %get-tuple-element.147), kind=kOutput, calls=%fused_computation.2.clone.1 | convolution fusion | flops 47677520 | bytes 7077928 | tf_op jit(solution)/shard_map/while/body/sr,sad->ard/dot_general | solution.py:59
  106.7 1.4 compare_and_fusion.2
  108.1 0.6 gather_fusion
  108.8 0.0 copy-start.2
  108.8 1.6 fusion.32
  110.4 0.0 copy-done.2
  110.4 0.1 dynamic_slice.19
  110.5 6.9 %bitcast_add_fusion.2 = f32[128,5,768]{2,1,0:T(8,128)} fusion(f32[128,5,768]{2,1,0:T(8,128)} %get-tuple-element.161, f32[8,128,768]{2,1,0:T(8,128)S(1)} %fusion.32, s32[8]{0:T(128)S(1)} %dynamic_slice.19, pred[8]{0:T(512)(128)(4,1)S(1)} %get-tuple-element.147), kind=kOutput, calls=%fused_computation.2.clone.1 | convolution fusion | flops 47677520 | bytes 7077928 | tf_op jit(solution)/shard_map/while/body/sr,sad->ard/dot_general | solution.py:59
  117.4 1.4 compare_and_fusion.2
  118.8 0.6 gather_fusion
  119.4 0.0 copy-start.2
  119.4 1.6 fusion.32
  121.0 0.0 copy-done.2
  121.0 0.1 dynamic_slice.19
  121.1 6.9 %bitcast_add_fusion.2 = f32[128,5,768]{2,1,0:T(8,128)} fusion(f32[128,5,768]{2,1,0:T(8,128)} %get-tuple-element.161, f32[8,128,768]{2,1,0:T(8,128)S(1)} %fusion.32, s32[8]{0:T(128)S(1)} %dynamic_slice.19, pred[8]{0:T(512)(128)(4,1)S(1)} %get-tuple-element.147), kind=kOutput, calls=%fused_computation.2.clone.1 | convolution fusion | flops 47677520 | bytes 7077928 | tf_op jit(solution)/shard_map/while/body/sr,sad->ard/dot_general | solution.py:59
  128.0 3.2 %copy.16 = f32[128,5,768]{0,2,1:T(8,128)} copy(f32[128,5,768]{2,1,0:T(8,128)} %get-tuple-element.53) | data formatting | bytes 3932160 | tf_op jit(solution)/shard_map/while | solution.py:64
  131.2 1.7 pad_maximum_fusion
  132.9 160.1 %all-reduce.1 = bf16[128,6,768]{0,2,1:T(8,128)(2,1)S(1)} all-reduce(f32[128,6,768]{0,2,1:T(8,128)S(1)} %pad_maximum_fusion), channel_id=1, replica_groups=mesh['node'=64,'rel'=8] {'rel'}, use_global_device_ids=true, to_apply=%region_2.3 | all-reduce | flops 589824 | bytes 3538944 | tf_op jit(solution)/shard_map/psum | solution.py:74
  293.0 1.8 fusion.18
  294.8 21.7 %all_to_all.27 = bf16[8,16,128]{2,1,0:T(8,128)(2,1)S(1)} all-to-all(bf16[8,16,128]{2,1,0:T(8,128)(2,1)S(1)} %bitcast.36), channel_id=1, replica_groups=mesh['node'=64,'rel'=8] {'rel'}, dimensions={0} | all-to-all | bytes 65536 | tf_op jit(solution)/shard_map/all_to_all | solution.py:80
  316.5 0.6 broadcast_in_dim.35
  (8 shorter events, 0.2 us)
Async XLA Ops:
  0.0 1.0 copy-start
  1.5 47.0 %copy-start.1 = (bf16[1,16,768]{2,1,0:T(8,128)(2,1)S(1)}, bf16[1,16,768]{2,1,0:T(8,128)(2,1)}, u32[]{:S(2)}) copy-start(bf16[1,16,768]{2,1,0:T(8,128)(2,1)} %param.9) | copy-start | bytes 73732
  49.7 44.5 %all-to-all-start = ((bf16[64,1,16,768]{3,2,1,0:T(8,128)(2,1)}), bf16[64,1,16,768]{3,2,1,0:T(8,128)(2,1)S(1)}, u32[]{:S(2)}, u32[]{:S(2)}) async-start(bf16[64,1,16,768]{3,2,1,0:T(8,128)(2,1)} %broadcast_in_dim.32), calls=%async_computation | async-start | bytes 3145728 | tf_op jit(solution)/shard_map/all_to_all | solution.py:14
  98.1 1.6 copy-start.2
  108.8 1.6 copy-start.2
  119.4 1.6 copy-start.2
where the time goes:
time: 318 us; the launch traced here: 317 us
  blocking collectives  229 us (72%)
  matrix products  27.4 us (9%)
  waiting for transfers between devices  25.5 us (8%)
  local copies, waits for them, and re-layouts  18.7 us (6%)
  starting transfers between devices  9.27 us (3%)
  other arithmetic  6.63 us (2%)
    psum x1, blocking collectives, on_device(): summed = lax.psum(jnp.concatenate([aggregate, self_part], axis=1), 'rel')  160 us
    all_to_all x1, blocking collectives, sent_to_all(): return lax.all_to_all(copies, axis, split_axis=0, concat_axis=0, tiled=True)  47 us
    all_to_all x1, waiting for transfers between devices, sent_to_all(): return lax.all_to_all(copies, axis, split_axis=0, concat_axis=0, tiled=True)  25.5 us
    all_to_all x1, blocking collectives, on_device(): lax.all_to_all(local_cols, 'rel', split_axis=0, concat_axis=1, tiled=True)  21.7 us
    dot_general x3, matrix products, accumulate(): jnp.einsum('sr,sad->ard', select, products, precision=lax.Precision.HIGHEST)  20.7 us
    all_to_all x1, starting transfers between devices, sent_to_all(): return lax.all_to_all(copies, axis, split_axis=0, concat_axis=0, tiled=True)  9.27 us
  transfers between devices with their start and end apart: 1, of which 1 were waited for; matrix products, arithmetic and copies ran while one was open for 3% of the time, Pallas kernels for 0%

commit v1 on v0

v1 whole, which is shorter than its diff:
```python
import functools

import jax
import jax.numpy as jnp
from jax import lax
from jax.experimental import pallas as pl
from jax.experimental.pallas import tpu as pltpu
from jax.sharding import Mesh
from jax.sharding import PartitionSpec as P

BF = jnp.bfloat16
F32 = jnp.float32
NODE = ("y", "x", "zl")
REL = ("zh", "core")
YX = ("y", "x")
VMEM = pl.BlockSpec(memory_space=pltpu.VMEM)
SMEM = pl.BlockSpec(memory_space=pltpu.SMEM)
PARAMS = pltpu.CompilerParams(vmem_limit_bytes=40 * 1024 * 1024)

RELS = 5
DIN = 768
DOUT = 1024
TILE = 128
SRC = 8
ROWS = 16
NODES = 64
PER = 12
SLOT = 8
SELF = 2
CHUNK = SLOT * NODES


def call(body, outs, ins, scratch=()):
    return pl.pallas_call(
        body,
        out_shape=outs,
        in_specs=ins,
        out_specs=jax.tree.map(lambda _: VMEM, outs),
        scratch_shapes=list(scratch),
        compiler_params=PARAMS,
    )


def shape(dims, kind):
    return jax.ShapeDtypeStruct(dims, kind)


def prepare(coef, own, bases, copies, parcel):
    src = lax.broadcasted_iota(jnp.int32, (DIN, DIN), 0)
    out = lax.broadcasted_iota(jnp.int32, (DIN, DIN), 1)
    swap = jnp.where(src == PER * (out & (NODES - 1)) + (out >> 6), 1.0, 0.0).astype(BF)
    turned = jnp.dot(own[...], swap, preferred_element_type=F32).astype(BF)
    for i in range(4):
        copies[i] = turned
    parcel[...] = jnp.zeros_like(parcel)
    for k in range(DIN // TILE):
        parcel[k, :ROWS] = turned[:, k * TILE : (k + 1) * TILE]
    flat = []
    for r in range(RELS + 1):
        total = jnp.zeros((PER, TILE), F32)
        for b in range(bases.shape[0]):
            total = total + coef[r, b] * bases[b].astype(F32)
        flat.append(total)
    rows = jnp.concatenate(flat[:RELS] + [jnp.zeros((4, TILE), F32)], axis=0)
    for k in range(8):
        parcel[k, ROWS : ROWS + SLOT] = rows[k * SLOT : (k + 1) * SLOT].astype(BF)
    for k in range(PER // SELF):
        parcel[k, ROWS + SLOT : ROWS + SLOT + SELF] = flat[RELS][k * SELF : (k + 1) * SELF].astype(BF)


def densify(count, source, relation, values, dense, acc):
    acc[...] = jnp.zeros_like(acc)

    def add(t, _):
        spot = relation[t] * SRC + source[t]
        acc[spot] = acc[spot] + values[t].astype(F32)
        return 0

    lax.fori_loop(0, count[0], add, 0)
    for r in range(RELS):
        for s in range(SRC):
            dense[r, :, s * TILE : (s + 1) * TILE] = acc[r * SRC + s].astype(BF)


def aggregate(core, dense, feats, send, keep, full):
    for r in range(RELS):
        full[:, r * DIN : (r + 1) * DIN] = jnp.dot(dense[r], feats[...], preferred_element_type=F32)
    full[:, RELS * DIN :] = jnp.zeros((TILE, 8 * CHUNK - RELS * DIN), F32)

    def split(mine):
        for z in range(4):
            a = (2 * z + mine) * CHUNK
            b = (2 * z + 1 - mine) * CHUNK
            keep[z] = full[:, a : a + CHUNK]
            send[z] = full[:, b : b + CHUNK].astype(BF)

    @pl.when(core[0] == 0)
    def _():
        split(0)

    @pl.when(core[0] == 1)
    def _():
        split(1)


def pair_sum(keep, got, out):
    out[...] = (keep[...] + got[...].astype(F32)).astype(BF)


def transform(core, got, own, weights, send, keep):
    src = lax.broadcasted_iota(jnp.int32, (CHUNK + TILE, DIN), 0)
    out = lax.broadcasted_iota(jnp.int32, (CHUNK + TILE, DIN), 1)
    swap = jnp.where(out == PER * (src & (NODES - 1)) + (src >> 6), 1.0, 0.0).astype(BF)
    total = got[0].astype(F32)
    for i in range(1, 4):
        total = total + got[i].astype(F32)
    msgs = jnp.concatenate([total.astype(BF), own[...]], axis=1)
    msgs = jnp.dot(msgs, swap, preferred_element_type=F32).astype(BF)
    part = jnp.dot(msgs, weights[...], preferred_element_type=F32)

    def split(mine):
        for z in range(4):
            a = (2 * z + mine) * ROWS
            b = (2 * z + 1 - mine) * ROWS
            keep[z] = part[a : a + ROWS]
            send[z] = part[b : b + ROWS].astype(BF)

    @pl.when(core[0] == 0)
    def _():
        split(0)

    @pl.when(core[0] == 1)
    def _():
        split(1)


def finish(got, out):
    total = got[0].astype(F32)
    for i in range(1, 4):
        total = total + got[i].astype(F32)
    out[...] = jnp.maximum(total, 0.0).astype(BF)


def exchange(x, axis):
    return lax.all_to_all(x, axis, split_axis=0, concat_axis=0, tiled=True)


def spread(x, axis):
    return exchange(jnp.broadcast_to(x, (lax.axis_size(axis), *x.shape)), axis)


def swap_core(x):
    return lax.ppermute(x, "core", [(0, 1), (1, 0)])


def on_device(features, bases, coefficients, tile_values, tile_source, tile_relation, tile_count):
    core = lax.axis_index("core").astype(jnp.int32).reshape(1)
    copies, parcel = call(
        prepare,
        (shape((4, ROWS, DIN), BF), shape((8, 32, TILE), BF)),
        [SMEM, VMEM, VMEM],
    )(coefficients, features[0], bases)
    feats = exchange(copies, "zl").reshape(NODES, DIN)
    feats = spread(feats, YX).reshape(SRC * TILE, DIN)

    dense = call(
        densify,
        shape((RELS, TILE, SRC * TILE), BF),
        [SMEM, SMEM, SMEM, VMEM],
        [pltpu.VMEM((RELS * SRC, TILE, TILE), F32)],
    )(tile_count[0], tile_source[0, 0], tile_relation[0, 0], tile_values[0, 0])
    send, keep = call(
        aggregate,
        (shape((4, TILE, CHUNK), BF), shape((4, TILE, CHUNK), F32)),
        [SMEM, VMEM, VMEM],
        [pltpu.VMEM((TILE, 8 * CHUNK), F32)],
    )(core, dense, feats)
    pair = call(pair_sum, shape((4, TILE, CHUNK), BF), [VMEM, VMEM])(keep, swap_core(send))

    parcel = exchange(parcel, REL)
    own = parcel[:, :ROWS].reshape(TILE, TILE)
    rows = jnp.moveaxis(parcel[:, ROWS : ROWS + PER], 0, 1).reshape(PER, DOUT)
    rows = spread(rows, "zl").reshape(4 * PER, DOUT)
    weights = spread(rows, YX).reshape(NODES * PER, DOUT)

    sums = exchange(pair, "zh")
    send, keep = call(
        transform,
        (shape((4, ROWS, DOUT), BF), shape((4, ROWS, DOUT), F32)),
        [SMEM, VMEM, VMEM, VMEM],
    )(core, sums, own, weights)
    pair = call(pair_sum, shape((4, ROWS, DOUT), BF), [VMEM, VMEM])(keep, swap_core(send))
    return call(finish, shape((ROWS, DOUT), BF), [VMEM])(exchange(pair, "zh"))[None]


def solution(mesh):
    split = Mesh(mesh.devices.reshape(4, 4, 4, 4, 2), NODE + REL)
    return jax.shard_map(
        on_device,
        mesh=split,
        in_specs=(
            P(REL, NODE, None),
            P(None, NODE, REL),
            P(),
            P(NODE, REL, None, None, None),
            P(NODE, REL, None),
            P(NODE, REL, None),
            P(NODE, REL),
        ),
        out_specs=P(REL, NODE, None),
        check_vma=False,
    )
```

time: 318 us -> 160 us (0.50)
  the two profiles are of different devices: /device:TPU:78 before, /device:TPU:1 now
where the time goes in v1:
time: 160 us; the launch traced here: 157 us
  waiting for transfers between devices  59.1 us (37%)
  blocking collectives  51.3 us (32%)
  starting transfers between devices  32.8 us (20%)
  local copies, waits for them, and re-layouts  6.61 us (4%)
  Pallas kernels  6.29 us (4%)
    all_to_all x4, waiting for transfers between devices, exchange(): return lax.all_to_all(x, axis, split_axis=0, concat_axis=0, tiled=True)  56.6 us
    all_to_all x3, blocking collectives, exchange(): return lax.all_to_all(x, axis, split_axis=0, concat_axis=0, tiled=True)  51.3 us
    all_to_all x4, starting transfers between devices, exchange(): return lax.all_to_all(x, axis, split_axis=0, concat_axis=0, tiled=True)  18.8 us
    ppermute x2, starting transfers between devices, swap_core(): return lax.ppermute(x, 'core', [(0, 1), (1, 0)])  14 us
    unnamed x13, local copies, waits for them, and re-layouts  3.87 us
  transfers between devices with their start and end apart: 6, of which 6 were waited for; matrix products, arithmetic and copies ran while one was open for 0% of the time, Pallas kernels for 2%

profile of v1, /device:TPU:1, one launch (start us, length us, event | category | flops | bytes accessed | tf_op | source)
XLA Modules:
  0.0 156.9 jit_solution(15391301474318871374)
XLA Ops:
  0.0 0.9 copy.9.bases
  0.9 0.0 copy-start.1
  0.9 0.7 copy-done.1
  1.7 0.0 copy-start.2
  1.7 0.7 copy-done.2
  2.4 1.6 %shard_map.74 = (bf16[4,16,768]{2,1,0:T(8,128)(2,1)}, bf16[8,32,128]{2,1,0:T(8,128)(2,1)S(1)}) custom-call(f32[6,30]{1,0:T(8,128)S(1)} %copy-done.2, bf16[16,768]{1,0:T(8,128)(2,1)S(1)} %bitcast.21, bf16[30,12,128]{2,1,0:T(8,128)(2,1)S(1)} %copy.9.bases), custom_call_target="tpu_custom_call" | custom-call | tf_op jit(solution)/shard_map/pallas_call | solution.py:158
  3.9 28.8 %all_to_all.35 = bf16[8,32,128]{2,1,0:T(8,128)(2,1)S(1)} all-to-all(bf16[8,32,128]{2,1,0:T(8,128)(2,1)S(1)} %get-tuple-element.14), channel_id=1, replica_groups=mesh['y'=4,'x'=4,'zl'=4,'zh'=4,'core'=2] {'zh','core'}, dimensions={0} | all-to-all | bytes 131072 | tf_op jit(solution)/shard_map/all_to_all | solution.py:145
  32.7 3.3 %all-to-all-start = ((bf16[4,16,768]{2,1,0:T(8,128)(2,1)}), bf16[4,16,768]{2,1,0:T(8,128)(2,1)S(1)}, u32[]{:S(2)}, u32[]{:S(2)}) async-start(bf16[4,16,768]{2,1,0:T(8,128)(2,1)} %get-tuple-element.11), calls=%async_computation | async-start | bytes 196608 | tf_op jit(solution)/shard_map/all_to_all | solution.py:145
  36.1 4.7 %all-to-all-done = bf16[4,16,768]{2,1,0:T(8,128)(2,1)S(1)} async-done(((bf16[4,16,768]{2,1,0:T(8,128)(2,1)}), bf16[4,16,768]{2,1,0:T(8,128)(2,1)S(1)}, u32[]{:S(2)}, u32[]{:S(2)}) %all-to-all-start) | async-done | bytes 98336 | tf_op jit(solution)/shard_map/all_to_all | solution.py:145
  40.8 7.2 %all_to_all.36 = bf16[4,12,1024]{2,1,0:T(8,128)(2,1)S(1)} all-to-all(bf16[4,12,1024]{2,1,0:T(8,128)(2,1)S(1)} %broadcast_in_dim.13), channel_id=1, replica_groups=mesh['y'=4,'x'=4,'zl'=4,'zh'=4,'core'=2] {'zl'}, dimensions={0} | all-to-all | bytes 196608 | tf_op jit(solution)/shard_map/all_to_all | solution.py:145
  47.9 1.3 broadcast_in_dim.12
  49.3 6.8 %all-to-all-start.1 = ((bf16[16,64,768]{2,1,0:T(8,128)(2,1)}), bf16[16,64,768]{2,1,0:T(8,128)(2,1)S(1)}, u32[]{:S(2)}, u32[]{:S(2)}) async-start(bf16[16,64,768]{2,1,0:T(8,128)(2,1)} %broadcast_in_dim.12), calls=%async_computation.1 | async-start | bytes 3145728 | tf_op jit(solution)/shard_map/all_to_all | solution.py:145
  56.1 19.4 %all-to-all-done.1 = bf16[16,64,768]{2,1,0:T(8,128)(2,1)S(1)} async-done(((bf16[16,64,768]{2,1,0:T(8,128)(2,1)}), bf16[16,64,768]{2,1,0:T(8,128)(2,1)S(1)}, u32[]{:S(2)}, u32[]{:S(2)}) %all-to-all-start.1) | async-done | bytes 1572896 | tf_op jit(solution)/shard_map/all_to_all | solution.py:145
  75.5 1.4 broadcast_in_dim.14
  76.9 0.0 copy-start.3
  76.9 0.0 copy-start.4
  76.9 5.3 %all-to-all-start.5 = ((bf16[16,48,1024]{2,1,0:T(8,128)(2,1)}), bf16[16,48,1024]{2,1,0:T(8,128)(2,1)S(1)}, u32[]{:S(2)}, u32[]{:S(2)}) async-start(bf16[16,48,1024]{2,1,0:T(8,128)(2,1)} %broadcast_in_dim.14), calls=%async_computation.5 | async-start | bytes 3145728 | tf_op jit(solution)/shard_map/all_to_all | solution.py:145
  82.8 0.0 copy-done.3
  82.8 0.0 copy-done.4
  82.9 0.0 copy-start
  82.9 1.5 copy-done
  84.4 1.1 shard_map.73.dense
  85.5 1.3 shard_map.75
  86.8 6.0 %collective-permute-start = (bf16[4,128,512]{2,1,0:T(8,128)(2,1)S(1)}, bf16[4,128,512]{2,1,0:T(8,128)(2,1)S(1)}, u32[]{:S(2)}, u32[]{:S(2)}) collective-permute-start(bf16[4,128,512]{2,1,0:T(8,128)(2,1)S(1)} %get-tuple-element.13), channel_id=1, source_target_pairs={{0,1},{1,0},{2,3},{3,2},{4,5},{5,4},{6,7},{7,6},{8,9},{9,8},{10,11... | collective-permute-start | bytes 1572872 | tf_op jit(solution)/shard_map/ppermute | solution.py:153
  92.8 1.5 collective-permute-done.got
  94.3 0.9 shard_map.76
  95.2 6.1 %all-to-all-done.5 = bf16[16,48,1024]{2,1,0:T(8,128)(2,1)S(1)} async-done(((bf16[16,48,1024]{2,1,0:T(8,128)(2,1)}), bf16[16,48,1024]{2,1,0:T(8,128)(2,1)S(1)}, u32[]{:S(2)}, u32[]{:S(2)}) %all-to-all-start.5) | async-done | bytes 1572896 | tf_op jit(solution)/shard_map/all_to_all | solution.py:145
  101.4 3.5 %all-to-all-start.2 = ((bf16[4,128,512]{2,1,0:T(8,128)(2,1)}), bf16[4,128,512]{2,1,0:T(8,128)(2,1)S(1)}, u32[]{:S(2)}, u32[]{:S(2)}) async-start(bf16[4,128,512]{2,1,0:T(8,128)(2,1)} %shard_map.76), calls=%async_computation.2 | async-start | bytes 1048576 | tf_op jit(solution)/shard_map/all_to_all | solution.py:145
  104.9 26.3 %all-to-all-done.2.got = bf16[4,128,512]{2,1,0:T(8,128)(2,1)S(1)} async-done(((bf16[4,128,512]{2,1,0:T(8,128)(2,1)}), bf16[4,128,512]{2,1,0:T(8,128)(2,1)S(1)}, u32[]{:S(2)}, u32[]{:S(2)}) %all-to-all-start.2) | async-done | bytes 524320 | tf_op jit(solution)/shard_map/all_to_all | solution.py:145
  131.2 0.7 shard_map.77
  131.9 8.0 %collective-permute-start.1 = (bf16[4,16,1024]{2,1,0:T(8,128)(2,1)S(1)}, bf16[4,16,1024]{2,1,0:T(8,128)(2,1)S(1)}, u32[]{:S(2)}, u32[]{:S(2)}) collective-permute-start(bf16[4,16,1024]{2,1,0:T(8,128)(2,1)S(1)} %get-tuple-element.16), channel_id=1, source_target_pairs={{0,1},{1,0},{2,3},{3,2},{4,5},{5,4},{6,7},{7,6},{8,9},{9,8},{10,11... | collective-permute-start | bytes 393224 | tf_op jit(solution)/shard_map/ppermute | solution.py:153
  139.9 1.0 collective-permute-done.1.got
  140.9 15.4 %all_to_all.37.got = bf16[4,16,1024]{2,1,0:T(8,128)(2,1)S(1)} all-to-all(bf16[4,16,1024]{2,1,0:T(8,128)(2,1)S(1)} %shard_map.78), channel_id=1, replica_groups=mesh['y'=4,'x'=4,'zl'=4,'zh'=4,'core'=2] {'zh'}, dimensions={0} | all-to-all | bytes 262144 | tf_op jit(solution)/shard_map/all_to_all | solution.py:145
  156.3 0.6 shard_map.79
  (8 shorter events, 0.1 us)
Async XLA Ops:
  0.9 0.7 copy-start.1
  1.7 0.7 copy-start.2
  32.7 8.1 %all-to-all-start = ((bf16[4,16,768]{2,1,0:T(8,128)(2,1)}), bf16[4,16,768]{2,1,0:T(8,128)(2,1)S(1)}, u32[]{:S(2)}, u32[]{:S(2)}) async-start(bf16[4,16,768]{2,1,0:T(8,128)(2,1)} %get-tuple-element.11), calls=%async_computation | async-start | bytes 196608 | tf_op jit(solution)/shard_map/all_to_all | solution.py:145
  49.3 26.2 %all-to-all-start.1 = ((bf16[16,64,768]{2,1,0:T(8,128)(2,1)}), bf16[16,64,768]{2,1,0:T(8,128)(2,1)S(1)}, u32[]{:S(2)}, u32[]{:S(2)}) async-start(bf16[16,64,768]{2,1,0:T(8,128)(2,1)} %broadcast_in_dim.12), calls=%async_computation.1 | async-start | bytes 3145728 | tf_op jit(solution)/shard_map/all_to_all | solution.py:145
  76.9 6.0 %copy-start.3 = (s32[1,1,56]{2,1,0:T(1,128)S(1)}, s32[1,1,56]{2,1,0:T(1,128)}, u32[]{:S(2)}) copy-start(s32[1,1,56]{2,1,0:T(1,128)} %param.11) | copy-start | bytes 676
  76.9 6.0 %copy-start.4 = (s32[1,1,56]{2,1,0:T(1,128)S(1)}, s32[1,1,56]{2,1,0:T(1,128)}, u32[]{:S(2)}) copy-start(s32[1,1,56]{2,1,0:T(1,128)} %param.12) | copy-start | bytes 676
  76.9 24.5 %all-to-all-start.5 = ((bf16[16,48,1024]{2,1,0:T(8,128)(2,1)}), bf16[16,48,1024]{2,1,0:T(8,128)(2,1)S(1)}, u32[]{:S(2)}, u32[]{:S(2)}) async-start(bf16[16,48,1024]{2,1,0:T(8,128)(2,1)} %broadcast_in_dim.14), calls=%async_computation.5 | async-start | bytes 3145728 | tf_op jit(solution)/shard_map/all_to_all | solution.py:145
  82.9 1.5 copy-start
  86.8 7.5 %collective-permute-start = (bf16[4,128,512]{2,1,0:T(8,128)(2,1)S(1)}, bf16[4,128,512]{2,1,0:T(8,128)(2,1)S(1)}, u32[]{:S(2)}, u32[]{:S(2)}) collective-permute-start(bf16[4,128,512]{2,1,0:T(8,128)(2,1)S(1)} %get-tuple-element.13), channel_id=1, source_target_pairs={{0,1},{1,0},{2,3},{3,2},{4,5},{5,4},{6,7},{7,6},{8,9},{9,8},{10,11... | collective-permute-start | bytes 1572872 | tf_op jit(solution)/shard_map/ppermute | solution.py:153
  101.4 29.8 %all-to-all-start.2 = ((bf16[4,128,512]{2,1,0:T(8,128)(2,1)}), bf16[4,128,512]{2,1,0:T(8,128)(2,1)S(1)}, u32[]{:S(2)}, u32[]{:S(2)}) async-start(bf16[4,128,512]{2,1,0:T(8,128)(2,1)} %shard_map.76), calls=%async_computation.2 | async-start | bytes 1048576 | tf_op jit(solution)/shard_map/all_to_all | solution.py:145
  131.9 9.0 %collective-permute-start.1 = (bf16[4,16,1024]{2,1,0:T(8,128)(2,1)S(1)}, bf16[4,16,1024]{2,1,0:T(8,128)(2,1)S(1)}, u32[]{:S(2)}, u32[]{:S(2)}) collective-permute-start(bf16[4,16,1024]{2,1,0:T(8,128)(2,1)S(1)} %get-tuple-element.16), channel_id=1, source_target_pairs={{0,1},{1,0},{2,3},{3,2},{4,5},{5,4},{6,7},{7,6},{8,9},{9,8},{10,11... | collective-permute-start | bytes 393224 | tf_op jit(solution)/shard_map/ppermute | solution.py:153

commit v2 on v1

v2 whole, which is shorter than its diff:
```python
import jax
import jax.numpy as jnp
from jax import lax
from jax.experimental import pallas as pl
from jax.experimental.pallas import tpu as pltpu
from jax.sharding import Mesh
from jax.sharding import PartitionSpec as P

BF = jnp.bfloat16
F32 = jnp.float32
NODE = ("y", "x", "zl")
REL = ("zh", "core")
YX = ("y", "x")
VMEM = pl.BlockSpec(memory_space=pltpu.VMEM)
SMEM = pl.BlockSpec(memory_space=pltpu.SMEM)
PARAMS = pltpu.CompilerParams(vmem_limit_bytes=40 * 1024 * 1024)

RELS = 5
DIN = 768
DOUT = 1024
TILE = 128
SRC = 8
ROWS = 16
NODES = 64
PER = 12
SLOT = 8
SELF = 2
CHUNK = SLOT * NODES
HALF = TILE // 2


def call(body, outs, ins, scratch=()):
    return pl.pallas_call(
        body,
        out_shape=outs,
        in_specs=ins,
        out_specs=jax.tree.map(lambda _: VMEM, outs),
        scratch_shapes=list(scratch),
        compiler_params=PARAMS,
    )


def shape(kind, *dims):
    return jax.ShapeDtypeStruct(dims, kind)


def turn(own, turned, copies):
    src = lax.broadcasted_iota(jnp.int32, (DIN, DIN), 0)
    out = lax.broadcasted_iota(jnp.int32, (DIN, DIN), 1)
    swap = jnp.where(src == PER * (out & (NODES - 1)) + (out >> 6), 1.0, 0.0).astype(BF)
    value = jnp.dot(own[...], swap, preferred_element_type=F32).astype(BF)
    turned[...] = value
    for i in range(4):
        copies[i] = value


def weigh(place, coef, turned, bases, send, keep, parcel):
    parcel[...] = jnp.zeros_like(parcel)
    for k in range(DIN // TILE):
        parcel[k, :ROWS] = turned[:, k * TILE : (k + 1) * TILE]
    flat = []
    for r in range(RELS + 1):
        total = jnp.zeros((PER, TILE), F32)
        for b in range(bases.shape[0]):
            total = total + coef[r, b] * bases[b].astype(F32)
        flat.append(total)
    rows = jnp.concatenate(flat[:RELS] + [jnp.zeros((4, TILE), F32)], axis=0)
    for k in range(8):
        parcel[k, ROWS : ROWS + SLOT] = rows[k * SLOT : (k + 1) * SLOT].astype(BF)
    for k in range(PER // SELF):
        parcel[k, ROWS + SLOT : ROWS + SLOT + SELF] = flat[RELS][k * SELF : (k + 1) * SELF].astype(BF)
    zh, core = place[1], place[2]
    for d in range(4):
        z = 2 * lax.rem(zh + d, 4)
        keep[d] = parcel[z + core]
        send[d] = parcel[z + 1 - core]


def join_cores(place, keep, got, *outs):
    core = place[2]
    for d in range(4):
        outs[d][core] = keep[d]
        outs[d][1 - core] = got[d]


def join_groups(place, *refs):
    ins, (own, rows) = refs[:4], refs[4:]
    for d in range(4):
        z = lax.rem(place[1] + 4 - d, 4)
        for c in range(2):
            g = 2 * z + c
            own[g] = ins[d][c, :ROWS]
            rows[:, pl.ds(pl.multiple_of(g * TILE, TILE), TILE)] = ins[d][c, ROWS:]


def stack(a, b, c, d, out):
    out[...] = jnp.concatenate([x[:PER].astype(F32) for x in (a, b, c, d)], axis=0).astype(BF)


def densify(count, source, relation, values, dense, acc):
    acc[...] = jnp.zeros_like(acc)

    def add(t, _):
        spot = relation[t] * SRC + source[t]
        acc[spot] = acc[spot] + values[t].astype(F32)
        return 0

    lax.fori_loop(0, count[0], add, 0)
    for r in range(RELS):
        for s in range(SRC):
            dense[r, :, s * TILE : (s + 1) * TILE] = acc[r * SRC + s].astype(BF)


def aggregate(place, dense, feats, send, keep, full):
    for r in range(RELS):
        full[:, r * DIN : (r + 1) * DIN] = jnp.dot(dense[r], feats[...], preferred_element_type=F32)
    full[:, RELS * DIN :] = jnp.zeros((TILE, 8 * CHUNK - RELS * DIN), F32)
    zh, core = place[1], place[2]
    for e in range(4):
        z = 2 * (zh ^ e)
        keep[e] = full[:, pl.ds(pl.multiple_of((z + core) * CHUNK, CHUNK), CHUNK)]
        send[e] = full[:, pl.ds(pl.multiple_of((z + 1 - core) * CHUNK, CHUNK), CHUNK)].astype(BF)


def first_half(keep, got, send_a, send_b, keep_a, keep_b):
    def total(e, rows):
        return keep[e, rows] + got[e, rows].astype(F32)

    a, b = slice(0, HALF), slice(HALF, TILE)
    send_a[0] = total(1, a).astype(BF)
    send_a[1] = total(2, a).astype(BF)
    send_b[0] = total(3, b).astype(BF)
    send_b[1] = total(2, b).astype(BF)
    keep_a[0] = total(0, a)
    keep_a[1] = total(3, a)
    keep_b[0] = total(0, b)
    keep_b[1] = total(1, b)


def second_half(keep_a, keep_b, got_a, got_b, send_a, send_b, hold):
    hold[:HALF] = keep_a[0] + got_a[0].astype(F32)
    hold[HALF:] = keep_b[0] + got_b[0].astype(F32)
    send_a[...] = (keep_a[1] + got_a[1].astype(F32)).astype(BF)
    send_b[...] = (keep_b[1] + got_b[1].astype(F32)).astype(BF)


def transform(place, hold, got_a, got_b, own, weights, send, keep, part):
    zl, core = place[0], place[2]
    src = lax.broadcasted_iota(jnp.int32, (CHUNK + TILE, DIN), 0)
    out = lax.broadcasted_iota(jnp.int32, (CHUNK + TILE, DIN), 1)
    node = src & (NODES - 1)
    spot = 4 * PER * (node >> 2) + PER * ((zl - node) & 3) + (src >> 6)
    swap = jnp.where(out == spot, 1.0, 0.0).astype(BF)
    top = (hold[:HALF] + got_a[...].astype(F32)).astype(BF)
    low = (hold[HALF:] + got_b[...].astype(F32)).astype(BF)
    msgs = jnp.concatenate([jnp.concatenate([top, low], axis=0), own[...]], axis=1)
    msgs = jnp.dot(msgs, swap, preferred_element_type=F32).astype(BF)
    part[...] = jnp.dot(msgs, weights[...], preferred_element_type=F32)
    for z in range(4):
        keep[z] = part[pl.ds(pl.multiple_of((2 * z + core) * ROWS, ROWS), ROWS)]
        send[z] = part[pl.ds(pl.multiple_of((2 * z + 1 - core) * ROWS, ROWS), ROWS)].astype(BF)


def pair_sum(keep, got, out):
    out[...] = (keep[...] + got[...].astype(F32)).astype(BF)


def finish(got, out):
    total = got[0].astype(F32)
    for i in range(1, 4):
        total = total + got[i].astype(F32)
    out[...] = jnp.maximum(total, 0.0).astype(BF)


def exchange(x, axis):
    return lax.all_to_all(x, axis, split_axis=0, concat_axis=0, tiled=True)


def spread(x, axis):
    return exchange(jnp.broadcast_to(x, (lax.axis_size(axis), *x.shape)), axis)


def shift(x, axis, step):
    return lax.ppermute(x, axis, [(i, (i + step) % 4) for i in range(4)])


def partner(x, axis, mask):
    return lax.ppermute(x, axis, [(i, i ^ mask) for i in range(lax.axis_size(axis))])


def on_device(features, bases, coefficients, tile_values, tile_source, tile_relation, tile_count):
    place = jnp.stack([lax.axis_index(a) for a in ("zl", "zh", "core")]).astype(jnp.int32)
    turned, copies = call(
        turn, (shape(BF, ROWS, DIN), shape(BF, 4, ROWS, DIN)), [VMEM]
    )(features[0])
    feats = exchange(copies, "zl").reshape(NODES, DIN)

    send, keep = call(
        weigh,
        (shape(BF, 4, 32, TILE), shape(BF, 4, 32, TILE)),
        [SMEM, SMEM, VMEM, VMEM],
        [pltpu.VMEM((8, 32, TILE), BF)],
    )(place, coefficients, turned, bases)
    block = shape(BF, 2, 32, TILE)
    parts = call(join_cores, (block,) * 4, [SMEM, VMEM, VMEM])(place, keep, partner(send, "core", 1))
    parts = [parts[0]] + [shift(parts[d], "zh", d) for d in (1, 2, 3)]

    feats = spread(feats, YX).reshape(SRC * TILE, DIN)

    own, rows = call(
        join_groups,
        (shape(BF, 8, ROWS, TILE), shape(BF, ROWS, DOUT)),
        [SMEM] + [VMEM] * 4,
    )(place, *parts)
    own = own.reshape(TILE, TILE)
    rows = [rows] + [shift(rows, "zl", d) for d in (1, 2, 3)]
    rows = call(stack, shape(BF, 4 * PER, DOUT), [VMEM] * 4)(*rows)
    weights = spread(rows, YX).reshape(NODES * PER, DOUT)

    dense = call(
        densify,
        shape(BF, RELS, TILE, SRC * TILE),
        [SMEM, SMEM, SMEM, VMEM],
        [pltpu.VMEM((RELS * SRC, TILE, TILE), F32)],
    )(tile_count[0], tile_source[0, 0], tile_relation[0, 0], tile_values[0, 0])
    send, keep = call(
        aggregate,
        (shape(BF, 4, TILE, CHUNK), shape(F32, 4, TILE, CHUNK)),
        [SMEM, VMEM, VMEM],
        [pltpu.VMEM((TILE, 8 * CHUNK), F32)],
    )(place, dense, feats)
    two = shape(BF, 2, HALF, CHUNK)
    wide = shape(F32, 2, HALF, CHUNK)
    send_a, send_b, keep_a, keep_b = call(first_half, (two, two, wide, wide), [VMEM] * 2)(
        keep, partner(send, "core", 1)
    )
    one = shape(BF, HALF, CHUNK)
    send_a, send_b, hold = call(second_half, (one, one, shape(F32, TILE, CHUNK)), [VMEM] * 4)(
        keep_a, keep_b, partner(send_a, "zh", 1), partner(send_b, "zh", 3)
    )
    send, keep = call(
        transform,
        (shape(BF, 4, ROWS, DOUT), shape(F32, 4, ROWS, DOUT)),
        [SMEM] + [VMEM] * 5,
        [pltpu.VMEM((TILE, DOUT), F32)],
    )(place, hold, partner(send_a, "zh", 3), partner(send_b, "zh", 1), own, weights)
    pair = call(pair_sum, shape(BF, 4, ROWS, DOUT), [VMEM] * 2)(keep, partner(send, "core", 1))
    return call(finish, shape(BF, ROWS, DOUT), [VMEM])(exchange(pair, "zh"))[None]


def solution(mesh):
    split = Mesh(mesh.devices.reshape(4, 4, 4, 4, 2), NODE + REL)
    return jax.shard_map(
        on_device,
        mesh=split,
        in_specs=(
            P(REL, NODE, None),
            P(None, NODE, REL),
            P(),
            P(NODE, REL, None, None, None),
            P(NODE, REL, None),
            P(NODE, REL, None),
            P(NODE, REL),
        ),
        out_specs=P(REL, NODE, None),
        check_vma=False,
    )
```

time: 160 us -> 150 us (0.938)
  starting transfers between devices: 32.8 us -> 87.2 us
  waiting for transfers between devices: 59.1 us -> 17.9 us
  blocking collectives: 51.3 us -> 29.7 us
    ppermute x2 -> x13, starting transfers between devices: 14 us -> 73.2 us  [the longest x7 42.3 us: partner(): lax.ppermute(x, axis, [(i, i ^ mask) for i in range(lax.axis_size(axis))])]
    all_to_all x4 -> x2, waiting for transfers between devices: 56.6 us -> 0.01 us  [exchange(): return lax.all_to_all(x, axis, split_axis=0, concat_axis=0, tiled=True)]
    all_to_all x3 -> x2, blocking collectives: 51.3 us -> 29.7 us  [exchange(): return lax.all_to_all(x, axis, split_axis=0, concat_axis=0, tiled=True)]
    ppermute x2 -> x13, waiting for transfers between devices: 2.48 us -> 17.9 us  [the longest x7 13.1 us: partner(): lax.ppermute(x, axis, [(i, i ^ mask) for i in range(lax.axis_size(axis))])]
    all_to_all x4 -> x2, starting transfers between devices: 18.8 us -> 13.9 us  [exchange(): return lax.all_to_all(x, axis, split_axis=0, concat_axis=0, tiled=True)]
    pallas_call x7 -> x12, Pallas kernels: 6.29 us -> 7.3 us  [the longest x1 1.86 us: on_device(): call(aggregate, (shape(BF, 4, TILE, CHUNK), shape(F32, 4, TILE, CHUNK)),...]
  transfers between devices with their start and end apart: 6 -> 15, of which waited for: 6 -> 9; matrix products, arithmetic and copies ran while one was open for 0% -> 0% of each run, Pallas kernels for 2% -> 3%
where the time goes in v2:
time: 150 us; the launch traced here: 148 us
  starting transfers between devices  87.2 us (58%)
  blocking collectives  29.7 us (20%)
  waiting for transfers between devices  17.9 us (12%)
  Pallas kernels  7.3 us (5%)
  local copies, waits for them, and re-layouts  5.04 us (3%)
    ppermute x7, starting transfers between devices, partner(): lax.ppermute(x, axis, [(i, i ^ mask) for i in range(lax.axis_size(axis))])  42.3 us
    ppermute x6, starting transfers between devices, shift(): return lax.ppermute(x, axis, [(i, (i + step) % 4) for i in range(4)])  30.9 us
    all_to_all x2, blocking collectives, exchange(): return lax.all_to_all(x, axis, split_axis=0, concat_axis=0, tiled=True)  29.7 us
    all_to_all x2, starting transfers between devices, exchange(): return lax.all_to_all(x, axis, split_axis=0, concat_axis=0, tiled=True)  13.9 us
    ppermute x7, waiting for transfers between devices, partner(): lax.ppermute(x, axis, [(i, i ^ mask) for i in range(lax.axis_size(axis))])  13.1 us
    ppermute x6, waiting for transfers between devices, shift(): return lax.ppermute(x, axis, [(i, (i + step) % 4) for i in range(4)])  4.77 us
  transfers between devices with their start and end apart: 15, of which 9 were waited for; matrix products, arithmetic and copies ran while one was open for 0% of the time, Pallas kernels for 3%

profile of v2, /device:TPU:1, one launch (start us, length us, event | category | flops | bytes accessed | tf_op | source)
XLA Modules:
  0.0 148.2 jit_solution(6467538737312493810)
XLA Ops:
  0.0 0.0 copy-start.1
  0.0 0.7 copy-done.1
  0.7 0.3 shard_map.74
  1.0 10.9 %all_to_all.20 = bf16[4,16,768]{2,1,0:T(8,128)(2,1)S(1)} all-to-all(bf16[4,16,768]{2,1,0:T(8,128)(2,1)S(1)} %get-tuple-element.26), channel_id=1, replica_groups=mesh['y'=4,'x'=4,'zl'=4,'zh'=4,'core'=2] {'zl'}, dimensions={0} | all-to-all | bytes 196608 | tf_op jit(solution)/shard_map/all_to_all | solution.py:176
  11.9 1.4 broadcast_in_dim.9
  13.3 0.0 copy-start.5
  13.3 0.0 copy-start.2
  13.3 6.9 %all-to-all-start.1 = ((bf16[16,64,768]{2,1,0:T(8,128)(2,1)}), bf16[16,64,768]{2,1,0:T(8,128)(2,1)S(1)}, u32[]{:S(2)}, u32[]{:S(2)}) async-start(bf16[16,64,768]{2,1,0:T(8,128)(2,1)} %broadcast_in_dim.9), calls=%async_computation.1 | async-start | bytes 3145728 | tf_op jit(solution)/shard_map/all_to_all | solution.py:176
  20.2 0.0 copy-done.5
  20.3 0.1 pad_add_fusion.place
  20.4 0.0 copy-done.2
  20.4 0.8 shard_map.78
  21.1 4.3 %collective-permute-start.5 = (bf16[4,32,128]{2,1,0:T(8,128)(2,1)S(1)}, bf16[4,32,128]{2,1,0:T(8,128)(2,1)S(1)}, u32[]{:S(2)}, u32[]{:S(2)}) collective-permute-start(bf16[4,32,128]{2,1,0:T(8,128)(2,1)S(1)} %get-tuple-element.38), channel_id=1, source_target_pairs={{0,1},{1,0},{2,3},{3,2},{4,5},{5,4},{6,7},{7,6},{8,9},{9,8},{10,11... | collective-permute-start | bytes 98312 | tf_op jit(solution)/shard_map/ppermute | solution.py:188
  25.4 0.8 collective-permute-done.5.got
  26.2 0.5 shard_map.79
  26.8 8.8 %collective-permute-start.6 = (bf16[2,32,128]{2,1,0:T(8,128)(2,1)S(1)}, bf16[2,32,128]{2,1,0:T(8,128)(2,1)S(1)}, u32[]{:S(2)}, u32[]{:S(2)}) collective-permute-start(bf16[2,32,128]{2,1,0:T(8,128)(2,1)S(1)} %get-tuple-element.40), channel_id=1, source_target_pairs={{0,2},{2,4},{4,6},{6,0},{1,3},{3,5},{5,7},{7,1},{8,10},{10,12},{12... | collective-permute-start | bytes 49160 | tf_op jit(solution)/shard_map/ppermute | solution.py:184
  35.6 7.9 %collective-permute-start.7 = (bf16[2,32,128]{2,1,0:T(8,128)(2,1)S(1)}, bf16[2,32,128]{2,1,0:T(8,128)(2,1)S(1)}, u32[]{:S(2)}, u32[]{:S(2)}) collective-permute-start(bf16[2,32,128]{2,1,0:T(8,128)(2,1)S(1)} %get-tuple-element.41), channel_id=1, source_target_pairs={{0,4},{2,6},{4,0},{6,2},{1,5},{3,7},{5,1},{7,3},{8,12},{10,14},{12... | collective-permute-start | bytes 49160 | tf_op jit(solution)/shard_map/ppermute | solution.py:184
  43.6 5.2 %collective-permute-start.8 = (bf16[2,32,128]{2,1,0:T(8,128)(2,1)S(1)}, bf16[2,32,128]{2,1,0:T(8,128)(2,1)S(1)}, u32[]{:S(2)}, u32[]{:S(2)}) collective-permute-start(bf16[2,32,128]{2,1,0:T(8,128)(2,1)S(1)} %get-tuple-element.42), channel_id=1, source_target_pairs={{0,6},{2,0},{4,2},{6,4},{1,7},{3,1},{5,3},{7,5},{8,14},{10,8},{12,... | collective-permute-start | bytes 49160 | tf_op jit(solution)/shard_map/ppermute | solution.py:184
  48.8 0.0 collective-permute-done.6.refs_1_
  48.8 0.2 collective-permute-done.7.refs_2_
  48.9 3.0 %collective-permute-done.8.refs_3_ = bf16[2,32,128]{2,1,0:T(8,128)(2,1)S(1)} collective-permute-done((bf16[2,32,128]{2,1,0:T(8,128)(2,1)S(1)}, bf16[2,32,128]{2,1,0:T(8,128)(2,1)S(1)}, u32[]{:S(2)}, u32[]{:S(2)}) %collective-permute-start.8) | collective-permute-done | bytes 16416 | tf_op jit(solution)/shard_map/ppermute | solution.py:184
  52.0 0.6 shard_map.80
  52.6 2.7 %collective-permute-start.9 = (bf16[16,1024]{1,0:T(8,128)(2,1)S(1)}, bf16[16,1024]{1,0:T(8,128)(2,1)S(1)}, u32[]{:S(2)}, u32[]{:S(2)}) collective-permute-start(bf16[16,1024]{1,0:T(8,128)(2,1)S(1)} %get-tuple-element.44.a), channel_id=1, source_target_pairs={{0,8},{8,16},{16,24},{24,0},{1,9},{9,17},{17,25},{25,1},{2,10},{10... | collective-permute-start | bytes 98312 | tf_op jit(solution)/shard_map/ppermute | solution.py:184
  55.3 2.4 %collective-permute-start.10 = (bf16[16,1024]{1,0:T(8,128)(2,1)S(1)}, bf16[16,1024]{1,0:T(8,128)(2,1)S(1)}, u32[]{:S(2)}, u32[]{:S(2)}) collective-permute-start(bf16[16,1024]{1,0:T(8,128)(2,1)S(1)} %get-tuple-element.44.a), channel_id=1, source_target_pairs={{0,16},{8,24},{16,0},{24,8},{1,17},{9,25},{17,1},{25,9},{2,18},{10... | collective-permute-start | bytes 98312 | tf_op jit(solution)/shard_map/ppermute | solution.py:184
  57.6 3.9 %collective-permute-start.11 = (bf16[16,1024]{1,0:T(8,128)(2,1)S(1)}, bf16[16,1024]{1,0:T(8,128)(2,1)S(1)}, u32[]{:S(2)}, u32[]{:S(2)}) collective-permute-start(bf16[16,1024]{1,0:T(8,128)(2,1)S(1)} %get-tuple-element.44.a), channel_id=1, source_target_pairs={{0,24},{8,0},{16,8},{24,16},{1,25},{9,1},{17,9},{25,17},{2,26},{10... | collective-permute-start | bytes 98312 | tf_op jit(solution)/shard_map/ppermute | solution.py:184
  61.6 0.0 collective-permute-done.9.b
  61.6 0.2 collective-permute-done.10.c
  61.8 1.3 collective-permute-done.11.d
  63.2 0.0 all-to-all-done.1
  63.2 1.4 broadcast_in_dim.10
  64.6 0.0 copy-start.3
  64.6 0.0 copy-start.4
  64.6 7.1 %all-to-all-start.2 = ((bf16[16,48,1024]{2,1,0:T(8,128)(2,1)}), bf16[16,48,1024]{2,1,0:T(8,128)(2,1)S(1)}, u32[]{:S(2)}, u32[]{:S(2)}) async-start(bf16[16,48,1024]{2,1,0:T(8,128)(2,1)} %broadcast_in_dim.10), calls=%async_computation.2 | async-start | bytes 3145728 | tf_op jit(solution)/shard_map/all_to_all | solution.py:176
  72.3 0.0 copy-done.3
  72.3 0.0 copy-done.4
  72.3 0.0 copy-start
  72.3 1.5 %copy-done = bf16[1,1,56,128,128]{4,3,2,1,0:T(8,128)(2,1)S(1)} copy-done((bf16[1,1,56,128,128]{4,3,2,1,0:T(8,128)(2,1)S(1)}, bf16[1,1,56,128,128]{4,3,2,1,0:T(8,128)(2,1)}, u32[]{:S(2)}) %copy-start) | copy-done | bytes 1835032
  73.8 1.2 shard_map.73.dense
  75.0 1.9 %shard_map.75 = (bf16[4,128,512]{2,1,0:T(8,128)(2,1)S(1)}, f32[4,128,512]{2,1,0:T(8,128)S(1)}) custom-call(s32[3]{0:T(128)S(1)} %pad_add_fusion.place, bf16[5,128,1024]{2,1,0:T(8,128)(2,1)S(1)} %shard_map.73.dense, bf16[1024,768]{1,0:T(8,128)(2,1)S(1)} %bitcast.14), custom_call_target="tpu_custom_call" | custom-call | tf_op jit(solution)/shard_map/pallas_call | solution.py:226
  76.9 5.7 %collective-permute-start = (bf16[4,128,512]{2,1,0:T(8,128)(2,1)S(1)}, bf16[4,128,512]{2,1,0:T(8,128)(2,1)S(1)}, u32[]{:S(2)}, u32[]{:S(2)}) collective-permute-start(bf16[4,128,512]{2,1,0:T(8,128)(2,1)S(1)} %get-tuple-element.28), channel_id=1, source_target_pairs={{0,1},{1,0},{2,3},{3,2},{4,5},{5,4},{6,7},{7,6},{8,9},{9,8},{10,11... | collective-permute-start | bytes 1572872 | tf_op jit(solution)/shard_map/ppermute | solution.py:188
  82.6 1.5 %collective-permute-done.got = bf16[4,128,512]{2,1,0:T(8,128)(2,1)S(1)} collective-permute-done((bf16[4,128,512]{2,1,0:T(8,128)(2,1)S(1)}, bf16[4,128,512]{2,1,0:T(8,128)(2,1)S(1)}, u32[]{:S(2)}, u32[]{:S(2)}) %collective-permute-start) | collective-permute-done | bytes 524320 | tf_op jit(solution)/shard_map/ppermute | solution.py:188
  84.1 0.1 shard_map.76
  84.2 2.7 %collective-permute-start.1 = (bf16[2,64,512]{2,1,0:T(8,128)(2,1)S(1)}, bf16[2,64,512]{2,1,0:T(8,128)(2,1)S(1)}, u32[]{:S(2)}, u32[]{:S(2)}) collective-permute-start(bf16[2,64,512]{2,1,0:T(8,128)(2,1)S(1)} %get-tuple-element.31), channel_id=1, source_target_pairs={{0,2},{2,0},{4,6},{6,4},{1,3},{3,1},{5,7},{7,5},{8,10},{10,8},{12,... | collective-permute-start | bytes 393224 | tf_op jit(solution)/shard_map/ppermute | solution.py:188
  86.9 5.5 %collective-permute-start.2 = (bf16[2,64,512]{2,1,0:T(8,128)(2,1)S(1)}, bf16[2,64,512]{2,1,0:T(8,128)(2,1)S(1)}, u32[]{:S(2)}, u32[]{:S(2)}) collective-permute-start(bf16[2,64,512]{2,1,0:T(8,128)(2,1)S(1)} %get-tuple-element.32), channel_id=1, source_target_pairs={{0,6},{2,4},{4,2},{6,0},{1,7},{3,5},{5,3},{7,1},{8,14},{10,12},{12... | collective-permute-start | bytes 393224 | tf_op jit(solution)/shard_map/ppermute | solution.py:188
  92.5 8.2 %collective-permute-done.1.got_a = bf16[2,64,512]{2,1,0:T(8,128)(2,1)S(1)} collective-permute-done((bf16[2,64,512]{2,1,0:T(8,128)(2,1)S(1)}, bf16[2,64,512]{2,1,0:T(8,128)(2,1)S(1)}, u32[]{:S(2)}, u32[]{:S(2)}) %collective-permute-start.1) | collective-permute-done | bytes 131104 | tf_op jit(solution)/shard_map/ppermute | solution.py:188
  100.7 0.0 collective-permute-done.2.got_b
  100.7 6.7 %collective-permute-start.3 = (bf16[64,512]{1,0:T(8,128)(2,1)S(1)}, bf16[64,512]{1,0:T(8,128)(2,1)S(1)}, u32[]{:S(2)}, u32[]{:S(2)}) collective-permute-start(bf16[64,512]{1,0:T(8,128)(2,1)S(1)} %get-tuple-element.34), channel_id=1, source_target_pairs={{0,6},{2,4},{4,2},{6,0},{1,7},{3,5},{5,3},{7,1},{8,14},{10,12},{12... | collective-permute-start | bytes 196616 | tf_op jit(solution)/shard_map/ppermute | solution.py:188
  107.4 8.4 %collective-permute-start.4 = (bf16[64,512]{1,0:T(8,128)(2,1)S(1)}, bf16[64,512]{1,0:T(8,128)(2,1)S(1)}, u32[]{:S(2)}, u32[]{:S(2)}) collective-permute-start(bf16[64,512]{1,0:T(8,128)(2,1)S(1)} %get-tuple-element.35), channel_id=1, source_target_pairs={{0,2},{2,0},{4,6},{6,4},{1,3},{3,1},{5,7},{7,5},{8,10},{10,8},{12,... | collective-permute-start | bytes 196616 | tf_op jit(solution)/shard_map/ppermute | solution.py:188
  115.8 0.0 all-to-all-done.2
  115.8 0.0 collective-permute-done.3.got_a
  115.8 1.6 %collective-permute-done.4.got_b = bf16[64,512]{1,0:T(8,128)(2,1)S(1)} collective-permute-done((bf16[64,512]{1,0:T(8,128)(2,1)S(1)}, bf16[64,512]{1,0:T(8,128)(2,1)S(1)}, u32[]{:S(2)}, u32[]{:S(2)}) %collective-permute-start.4) | collective-permute-done | bytes 65568 | tf_op jit(solution)/shard_map/ppermute | solution.py:188
  117.5 1.3 shard_map.82
  118.7 9.0 %collective-permute-start.12 = (bf16[4,16,1024]{2,1,0:T(8,128)(2,1)S(1)}, bf16[4,16,1024]{2,1,0:T(8,128)(2,1)S(1)}, u32[]{:S(2)}, u32[]{:S(2)}) collective-permute-start(bf16[4,16,1024]{2,1,0:T(8,128)(2,1)S(1)} %get-tuple-element.46), channel_id=1, source_target_pairs={{0,1},{1,0},{2,3},{3,2},{4,5},{5,4},{6,7},{7,6},{8,9},{9,8},{10,11... | collective-permute-start | bytes 393224 | tf_op jit(solution)/shard_map/ppermute | solution.py:188
  127.7 1.0 collective-permute-done.12.got
  128.7 18.8 %all_to_all.21.got = bf16[4,16,1024]{2,1,0:T(8,128)(2,1)S(1)} all-to-all(bf16[4,16,1024]{2,1,0:T(8,128)(2,1)S(1)} %shard_map.83), channel_id=1, replica_groups=mesh['y'=4,'x'=4,'zl'=4,'zh'=4,'core'=2] {'zh'}, dimensions={0} | all-to-all | bytes 262144 | tf_op jit(solution)/shard_map/all_to_all | solution.py:176
  147.5 0.6 shard_map.84
  (4 shorter events, 0.1 us)
Async XLA Ops:
  0.0 0.7 copy-start.1
  13.3 6.9 %copy-start.5 = (bf16[30,12,128]{2,0,1:T(8,128)(2,1)S(1)}, bf16[30,12,128]{2,0,1:T(8,128)(2,1)}, u32[]{:S(2)}) copy-start(bf16[30,12,128]{2,0,1:T(8,128)(2,1)} %param.8) | copy-start | bytes 276484
  13.3 7.0 %copy-start.2 = (f32[6,30]{1,0:T(8,128)S(1)}, f32[6,30]{1,0:T(8,128)}, u32[]{:S(2)}) copy-start(f32[6,30]{1,0:T(8,128)} %coef.1) | copy-start | bytes 2164
  13.3 49.9 %all-to-all-start.1 = ((bf16[16,64,768]{2,1,0:T(8,128)(2,1)}), bf16[16,64,768]{2,1,0:T(8,128)(2,1)S(1)}, u32[]{:S(2)}, u32[]{:S(2)}) async-start(bf16[16,64,768]{2,1,0:T(8,128)(2,1)} %broadcast_in_dim.9), calls=%async_computation.1 | async-start | bytes 3145728 | tf_op jit(solution)/shard_map/all_to_all | solution.py:176
  21.1 5.1 %collective-permute-start.5 = (bf16[4,32,128]{2,1,0:T(8,128)(2,1)S(1)}, bf16[4,32,128]{2,1,0:T(8,128)(2,1)S(1)}, u32[]{:S(2)}, u32[]{:S(2)}) collective-permute-start(bf16[4,32,128]{2,1,0:T(8,128)(2,1)S(1)} %get-tuple-element.38), channel_id=1, source_target_pairs={{0,1},{1,0},{2,3},{3,2},{4,5},{5,4},{6,7},{7,6},{8,9},{9,8},{10,11... | collective-permute-start | bytes 98312 | tf_op jit(solution)/shard_map/ppermute | solution.py:188
  26.8 22.0 %collective-permute-start.6 = (bf16[2,32,128]{2,1,0:T(8,128)(2,1)S(1)}, bf16[2,32,128]{2,1,0:T(8,128)(2,1)S(1)}, u32[]{:S(2)}, u32[]{:S(2)}) collective-permute-start(bf16[2,32,128]{2,1,0:T(8,128)(2,1)S(1)} %get-tuple-element.40), channel_id=1, source_target_pairs={{0,2},{2,4},{4,6},{6,0},{1,3},{3,5},{5,7},{7,1},{8,10},{10,12},{12... | collective-permute-start | bytes 49160 | tf_op jit(solution)/shard_map/ppermute | solution.py:184
  35.6 13.3 %collective-permute-start.7 = (bf16[2,32,128]{2,1,0:T(8,128)(2,1)S(1)}, bf16[2,32,128]{2,1,0:T(8,128)(2,1)S(1)}, u32[]{:S(2)}, u32[]{:S(2)}) collective-permute-start(bf16[2,32,128]{2,1,0:T(8,128)(2,1)S(1)} %get-tuple-element.41), channel_id=1, source_target_pairs={{0,4},{2,6},{4,0},{6,2},{1,5},{3,7},{5,1},{7,3},{8,12},{10,14},{12... | collective-permute-start | bytes 49160 | tf_op jit(solution)/shard_map/ppermute | solution.py:184
  43.6 8.4 %collective-permute-start.8 = (bf16[2,32,128]{2,1,0:T(8,128)(2,1)S(1)}, bf16[2,32,128]{2,1,0:T(8,128)(2,1)S(1)}, u32[]{:S(2)}, u32[]{:S(2)}) collective-permute-start(bf16[2,32,128]{2,1,0:T(8,128)(2,1)S(1)} %get-tuple-element.42), channel_id=1, source_target_pairs={{0,6},{2,0},{4,2},{6,4},{1,7},{3,1},{5,3},{7,5},{8,14},{10,8},{12,... | collective-permute-start | bytes 49160 | tf_op jit(solution)/shard_map/ppermute | solution.py:184
  52.6 9.0 %collective-permute-start.9 = (bf16[16,1024]{1,0:T(8,128)(2,1)S(1)}, bf16[16,1024]{1,0:T(8,128)(2,1)S(1)}, u32[]{:S(2)}, u32[]{:S(2)}) collective-permute-start(bf16[16,1024]{1,0:T(8,128)(2,1)S(1)} %get-tuple-element.44.a), channel_id=1, source_target_pairs={{0,8},{8,16},{16,24},{24,0},{1,9},{9,17},{17,25},{25,1},{2,10},{10... | collective-permute-start | bytes 98312 | tf_op jit(solution)/shard_map/ppermute | solution.py:184
  55.3 6.5 %collective-permute-start.10 = (bf16[16,1024]{1,0:T(8,128)(2,1)S(1)}, bf16[16,1024]{1,0:T(8,128)(2,1)S(1)}, u32[]{:S(2)}, u32[]{:S(2)}) collective-permute-start(bf16[16,1024]{1,0:T(8,128)(2,1)S(1)} %get-tuple-element.44.a), channel_id=1, source_target_pairs={{0,16},{8,24},{16,0},{24,8},{1,17},{9,25},{17,1},{25,9},{2,18},{10... | collective-permute-start | bytes 98312 | tf_op jit(solution)/shard_map/ppermute | solution.py:184
  57.6 5.5 %collective-permute-start.11 = (bf16[16,1024]{1,0:T(8,128)(2,1)S(1)}, bf16[16,1024]{1,0:T(8,128)(2,1)S(1)}, u32[]{:S(2)}, u32[]{:S(2)}) collective-permute-start(bf16[16,1024]{1,0:T(8,128)(2,1)S(1)} %get-tuple-element.44.a), channel_id=1, source_target_pairs={{0,24},{8,0},{16,8},{24,16},{1,25},{9,1},{17,9},{25,17},{2,26},{10... | collective-permute-start | bytes 98312 | tf_op jit(solution)/shard_map/ppermute | solution.py:184
  64.6 7.7 %copy-start.3 = (s32[1,1,56]{2,1,0:T(1,128)S(1)}, s32[1,1,56]{2,1,0:T(1,128)}, u32[]{:S(2)}) copy-start(s32[1,1,56]{2,1,0:T(1,128)} %param.11) | copy-start | bytes 676
  64.6 7.7 %copy-start.4 = (s32[1,1,56]{2,1,0:T(1,128)S(1)}, s32[1,1,56]{2,1,0:T(1,128)}, u32[]{:S(2)}) copy-start(s32[1,1,56]{2,1,0:T(1,128)} %param.12) | copy-start | bytes 676
  64.6 51.2 %all-to-all-start.2 = ((bf16[16,48,1024]{2,1,0:T(8,128)(2,1)}), bf16[16,48,1024]{2,1,0:T(8,128)(2,1)S(1)}, u32[]{:S(2)}, u32[]{:S(2)}) async-start(bf16[16,48,1024]{2,1,0:T(8,128)(2,1)} %broadcast_in_dim.10), calls=%async_computation.2 | async-start | bytes 3145728 | tf_op jit(solution)/shard_map/all_to_all | solution.py:176
  72.3 1.5 %copy-start = (bf16[1,1,56,128,128]{4,3,2,1,0:T(8,128)(2,1)S(1)}, bf16[1,1,56,128,128]{4,3,2,1,0:T(8,128)(2,1)}, u32[]{:S(2)}) copy-start(bf16[1,1,56,128,128]{4,3,2,1,0:T(8,128)(2,1)} %param.10) | copy-start | bytes 5505028
  76.9 7.2 %collective-permute-start = (bf16[4,128,512]{2,1,0:T(8,128)(2,1)S(1)}, bf16[4,128,512]{2,1,0:T(8,128)(2,1)S(1)}, u32[]{:S(2)}, u32[]{:S(2)}) collective-permute-start(bf16[4,128,512]{2,1,0:T(8,128)(2,1)S(1)} %get-tuple-element.28), channel_id=1, source_target_pairs={{0,1},{1,0},{2,3},{3,2},{4,5},{5,4},{6,7},{7,6},{8,9},{9,8},{10,11... | collective-permute-start | bytes 1572872 | tf_op jit(solution)/shard_map/ppermute | solution.py:188
  84.2 16.5 %collective-permute-start.1 = (bf16[2,64,512]{2,1,0:T(8,128)(2,1)S(1)}, bf16[2,64,512]{2,1,0:T(8,128)(2,1)S(1)}, u32[]{:S(2)}, u32[]{:S(2)}) collective-permute-start(bf16[2,64,512]{2,1,0:T(8,128)(2,1)S(1)} %get-tuple-element.31), channel_id=1, source_target_pairs={{0,2},{2,0},{4,6},{6,4},{1,3},{3,1},{5,7},{7,5},{8,10},{10,8},{12,... | collective-permute-start | bytes 393224 | tf_op jit(solution)/shard_map/ppermute | solution.py:188
  86.9 13.7 %collective-permute-start.2 = (bf16[2,64,512]{2,1,0:T(8,128)(2,1)S(1)}, bf16[2,64,512]{2,1,0:T(8,128)(2,1)S(1)}, u32[]{:S(2)}, u32[]{:S(2)}) collective-permute-start(bf16[2,64,512]{2,1,0:T(8,128)(2,1)S(1)} %get-tuple-element.32), channel_id=1, source_target_pairs={{0,6},{2,4},{4,2},{6,0},{1,7},{3,5},{5,3},{7,1},{8,14},{10,12},{12... | collective-permute-start | bytes 393224 | tf_op jit(solution)/shard_map/ppermute | solution.py:188
  100.7 15.1 %collective-permute-start.3 = (bf16[64,512]{1,0:T(8,128)(2,1)S(1)}, bf16[64,512]{1,0:T(8,128)(2,1)S(1)}, u32[]{:S(2)}, u32[]{:S(2)}) collective-permute-start(bf16[64,512]{1,0:T(8,128)(2,1)S(1)} %get-tuple-element.34), channel_id=1, source_target_pairs={{0,6},{2,4},{4,2},{6,0},{1,7},{3,5},{5,3},{7,1},{8,14},{10,12},{12... | collective-permute-start | bytes 196616 | tf_op jit(solution)/shard_map/ppermute | solution.py:188
  107.4 10.1 %collective-permute-start.4 = (bf16[64,512]{1,0:T(8,128)(2,1)S(1)}, bf16[64,512]{1,0:T(8,128)(2,1)S(1)}, u32[]{:S(2)}, u32[]{:S(2)}) collective-permute-start(bf16[64,512]{1,0:T(8,128)(2,1)S(1)} %get-tuple-element.35), channel_id=1, source_target_pairs={{0,2},{2,0},{4,6},{6,4},{1,3},{3,1},{5,7},{7,5},{8,10},{10,8},{12,... | collective-permute-start | bytes 196616 | tf_op jit(solution)/shard_map/ppermute | solution.py:188
  118.7 10.0 %collective-permute-start.12 = (bf16[4,16,1024]{2,1,0:T(8,128)(2,1)S(1)}, bf16[4,16,1024]{2,1,0:T(8,128)(2,1)S(1)}, u32[]{:S(2)}, u32[]{:S(2)}) collective-permute-start(bf16[4,16,1024]{2,1,0:T(8,128)(2,1)S(1)} %get-tuple-element.46), channel_id=1, source_target_pairs={{0,1},{1,0},{2,3},{3,2},{4,5},{5,4},{6,7},{7,6},{8,9},{9,8},{10,11... | collective-permute-start | bytes 393224 | tf_op jit(solution)/shard_map/ppermute | solution.py:188

commit v3 on v2

--- a/solution.py
+++ b/solution.py
@@ -12,8 +12,10 @@
 REL = ("zh", "core")
 YX = ("y", "x")
 VMEM = pl.BlockSpec(memory_space=pltpu.VMEM)
+ANY = pl.BlockSpec(memory_space=pl.ANY)
+HBM = pl.BlockSpec(memory_space=pltpu.HBM)
 SMEM = pl.BlockSpec(memory_space=pltpu.SMEM)
-PARAMS = pltpu.CompilerParams(vmem_limit_bytes=40 * 1024 * 1024)
+PARAMS = pltpu.CompilerParams(vmem_limit_bytes=16 * 1024 * 1024)
 
 RELS = 5
 DIN = 768
@@ -29,12 +31,12 @@
 HALF = TILE // 2
 
 
-def call(body, outs, ins, scratch=()):
+def call(body, outs, ins, scratch=(), where=VMEM):
     return pl.pallas_call(
         body,
         out_shape=outs,
         in_specs=ins,
-        out_specs=jax.tree.map(lambda _: VMEM, outs),
+        out_specs=jax.tree.map(lambda _: where, outs),
         scratch_shapes=list(scratch),
         compiler_params=PARAMS,
     )
@@ -44,40 +46,62 @@
     return jax.ShapeDtypeStruct(dims, kind)
 
 
-def turn(own, turned, copies):
+def start(own, coef, bases, padded, copies, rows):
     src = lax.broadcasted_iota(jnp.int32, (DIN, DIN), 0)
     out = lax.broadcasted_iota(jnp.int32, (DIN, DIN), 1)
     swap = jnp.where(src == PER * (out & (NODES - 1)) + (out >> 6), 1.0, 0.0).astype(BF)
     value = jnp.dot(own[...], swap, preferred_element_type=F32).astype(BF)
-    turned[...] = value
+    padded[:, :DIN] = value
+    padded[:, DIN:] = jnp.zeros((ROWS, 8 * TILE - DIN), BF)
+    rows[...] = jnp.zeros_like(rows)
+    for d in range(PER):
+        part = jnp.dot(
+            coef[...], bases[d].astype(F32), precision=lax.Precision.HIGHEST, preferred_element_type=F32
+        )
+        for r in range(RELS):
+            j = r * PER + d
+            rows[j // SLOT, j % SLOT : j % SLOT + 1] = part[r : r + 1]
+        rows[d // SELF, SLOT + d % SELF : SLOT + d % SELF + 1] = part[RELS :]
     for i in range(4):
-        copies[i] = value
-
-
-def weigh(place, coef, turned, bases, send, keep, parcel):
-    parcel[...] = jnp.zeros_like(parcel)
-    for k in range(DIN // TILE):
-        parcel[k, :ROWS] = turned[:, k * TILE : (k + 1) * TILE]
-    flat = []
-    for r in range(RELS + 1):
-        total = jnp.zeros((PER, TILE), F32)
-        for b in range(bases.shape[0]):
-            total = total + coef[r, b] * bases[b].astype(F32)
-        flat.append(total)
-    rows = jnp.concatenate(flat[:RELS] + [jnp.zeros((4, TILE), F32)], axis=0)
-    for k in range(8):
-        parcel[k, ROWS : ROWS + SLOT] = rows[k * SLOT : (k + 1) * SLOT].astype(BF)
-    for k in range(PER // SELF):
-        parcel[k, ROWS + SLOT : ROWS + SLOT + SELF] = flat[RELS][k * SELF : (k + 1) * SELF].astype(BF)
-    zh, core = place[1], place[2]
+        copies[i, :, :DIN] = value
+        for k in range(8):
+            copies[i, :, DIN + k * TILE : DIN + (k + 1) * TILE] = rows[k].astype(BF)
+
+
+def repeat(block, copies, sems):
+    moves = [pltpu.make_async_copy(block, copies.at[i], sems.at[i]) for i in range(copies.shape[0])]
+    for move in moves:
+        move.start()
+    for move in moves:
+        move.wait()
+
+
+def fan(after, gathered, copies, block, sems):
+    block[...] = gathered[:, :, :DIN].reshape(NODES, DIN)
+    repeat(block, copies, sems)
+
+
+def fan_rows(after, rows, copies, sems):
+    repeat(rows, copies, sems)
+
+
+def sort(place, padded, gathered, send, keep):
+    zh, core = place[0], place[1]
+
+    def fill(ref, d, k):
+        ref[d, :ROWS] = padded[:, pl.ds(pl.multiple_of(k * TILE, TILE), TILE)]
+        spot = pl.ds(pl.multiple_of(DIN + k * TILE, TILE), TILE)
+        rows = [gathered[z, :, spot].astype(F32)[:PER] for z in range(4)]
+        ref[d, ROWS:] = jnp.concatenate(rows, axis=0).astype(BF)
+
     for d in range(4):
         z = 2 * lax.rem(zh + d, 4)
-        keep[d] = parcel[z + core]
-        send[d] = parcel[z + 1 - core]
+        fill(keep, d, z + core)
+        fill(send, d, z + 1 - core)
 
 
 def join_cores(place, keep, got, *outs):
-    core = place[2]
+    core = place[1]
     for d in range(4):
         outs[d][core] = keep[d]
         outs[d][1 - core] = got[d]
@@ -86,17 +110,13 @@
 def join_groups(place, *refs):
     ins, (own, rows) = refs[:4], refs[4:]
     for d in range(4):
-        z = lax.rem(place[1] + 4 - d, 4)
+        z = lax.rem(place[0] + 4 - d, 4)
         for c in range(2):
             g = 2 * z + c
             own[g] = ins[d][c, :ROWS]
             rows[:, pl.ds(pl.multiple_of(g * TILE, TILE), TILE)] = ins[d][c, ROWS:]
 
 
-def stack(a, b, c, d, out):
-    out[...] = jnp.concatenate([x[:PER].astype(F32) for x in (a, b, c, d)], axis=0).astype(BF)
-
-
 def densify(count, source, relation, values, dense, acc):
     acc[...] = jnp.zeros_like(acc)
 
@@ -111,11 +131,11 @@
             dense[r, :, s * TILE : (s + 1) * TILE] = acc[r * SRC + s].astype(BF)
 
 
-def aggregate(place, dense, feats, send, keep, full):
+def aggregate(place, dense, feats, after, send, keep, full):
     for r in range(RELS):
         full[:, r * DIN : (r + 1) * DIN] = jnp.dot(dense[r], feats[...], preferred_element_type=F32)
     full[:, RELS * DIN :] = jnp.zeros((TILE, 8 * CHUNK - RELS * DIN), F32)
-    zh, core = place[1], place[2]
+    zh, core = place[0], place[1]
     for e in range(4):
         z = 2 * (zh ^ e)
         keep[e] = full[:, pl.ds(pl.multiple_of((z + core) * CHUNK, CHUNK), CHUNK)]
@@ -145,12 +165,10 @@
 
 
 def transform(place, hold, got_a, got_b, own, weights, send, keep, part):
-    zl, core = place[0], place[2]
+    core = place[1]
     src = lax.broadcasted_iota(jnp.int32, (CHUNK + TILE, DIN), 0)
     out = lax.broadcasted_iota(jnp.int32, (CHUNK + TILE, DIN), 1)
-    node = src & (NODES - 1)
-    spot = 4 * PER * (node >> 2) + PER * ((zl - node) & 3) + (src >> 6)
-    swap = jnp.where(out == spot, 1.0, 0.0).astype(BF)
+    swap = jnp.where(out == PER * (src & (NODES - 1)) + (src >> 6), 1.0, 0.0).astype(BF)
     top = (hold[:HALF] + got_a[...].astype(F32)).astype(BF)
     low = (hold[HALF:] + got_b[...].astype(F32)).astype(BF)
     msgs = jnp.concatenate([jnp.concatenate([top, low], axis=0), own[...]], axis=1)
@@ -176,10 +194,6 @@
     return lax.all_to_all(x, axis, split_axis=0, concat_axis=0, tiled=True)
 
 
-def spread(x, axis):
-    return exchange(jnp.broadcast_to(x, (lax.axis_size(axis), *x.shape)), axis)
-
-
 def shift(x, axis, step):
     return lax.ppermute(x, axis, [(i, (i + step) % 4) for i in range(4)])
 
@@ -189,46 +203,55 @@
 
 
 def on_device(features, bases, coefficients, tile_values, tile_source, tile_relation, tile_count):
-    place = jnp.stack([lax.axis_index(a) for a in ("zl", "zh", "core")]).astype(jnp.int32)
-    turned, copies = call(
-        turn, (shape(BF, ROWS, DIN), shape(BF, 4, ROWS, DIN)), [VMEM]
-    )(features[0])
-    feats = exchange(copies, "zl").reshape(NODES, DIN)
-
-    send, keep = call(
-        weigh,
-        (shape(BF, 4, 32, TILE), shape(BF, 4, 32, TILE)),
-        [SMEM, SMEM, VMEM, VMEM],
-        [pltpu.VMEM((8, 32, TILE), BF)],
-    )(place, coefficients, turned, bases)
-    block = shape(BF, 2, 32, TILE)
-    parts = call(join_cores, (block,) * 4, [SMEM, VMEM, VMEM])(place, keep, partner(send, "core", 1))
-    parts = [parts[0]] + [shift(parts[d], "zh", d) for d in (1, 2, 3)]
-
-    feats = spread(feats, YX).reshape(SRC * TILE, DIN)
-
-    own, rows = call(
-        join_groups,
-        (shape(BF, 8, ROWS, TILE), shape(BF, ROWS, DOUT)),
-        [SMEM] + [VMEM] * 4,
-    )(place, *parts)
-    own = own.reshape(TILE, TILE)
-    rows = [rows] + [shift(rows, "zl", d) for d in (1, 2, 3)]
-    rows = call(stack, shape(BF, 4 * PER, DOUT), [VMEM] * 4)(*rows)
-    weights = spread(rows, YX).reshape(NODES * PER, DOUT)
-
+    place = jnp.stack([lax.axis_index(a) for a in REL]).astype(jnp.int32)
+    padded, copies = call(
+        start,
+        (shape(BF, ROWS, 8 * TILE), shape(BF, 4, ROWS, DIN + 8 * TILE)),
+        [VMEM] * 3,
+        [pltpu.VMEM((8, ROWS, TILE), F32)],
+    )(features[0], coefficients, jnp.swapaxes(bases, 0, 1))
+    gathered = exchange(copies, "zl")
     dense = call(
         densify,
         shape(BF, RELS, TILE, SRC * TILE),
         [SMEM, SMEM, SMEM, VMEM],
         [pltpu.VMEM((RELS * SRC, TILE, TILE), F32)],
     )(tile_count[0], tile_source[0, 0], tile_relation[0, 0], tile_values[0, 0])
+    feats = call(
+        fan,
+        shape(BF, 16, NODES, DIN),
+        [ANY, VMEM],
+        [pltpu.VMEM((NODES, DIN), BF), pltpu.SemaphoreType.DMA((16,))],
+        HBM,
+    )(dense, gathered)
+    feats = exchange(feats, YX).reshape(SRC * TILE, DIN)
+
+    parcel = shape(BF, 4, ROWS + 4 * PER, TILE)
+    send, keep = call(sort, (parcel, parcel), [SMEM, VMEM, VMEM])(place, padded, gathered)
+    block = shape(BF, 2, ROWS + 4 * PER, TILE)
+    parts = call(join_cores, (block,) * 4, [SMEM, VMEM, VMEM])(place, keep, partner(send, "core", 1))
+    parts = [parts[0]] + [shift(parts[d], "zh", d) for d in (1, 2, 3)]
+    own, rows = call(
+        join_groups,
+        (shape(BF, 8, ROWS, TILE), shape(BF, 4 * PER, DOUT)),
+        [SMEM] + [VMEM] * 4,
+    )(place, *parts)
+    own = own.reshape(TILE, TILE)
+
     send, keep = call(
         aggregate,
         (shape(BF, 4, TILE, CHUNK), shape(F32, 4, TILE, CHUNK)),
-        [SMEM, VMEM, VMEM],
+        [SMEM, VMEM, VMEM, ANY],
         [pltpu.VMEM((TILE, 8 * CHUNK), F32)],
-    )(place, dense, feats)
+    )(place, dense, feats, rows)
+    weights = call(
+        fan_rows,
+        shape(BF, 16, 4 * PER, DOUT),
+        [ANY, VMEM],
+        [pltpu.SemaphoreType.DMA((16,))],
+        HBM,
+    )(send, rows)
+    weights = exchange(weights, YX).reshape(NODES * PER, DOUT)
     two = shape(BF, 2, HALF, CHUNK)
     wide = shape(F32, 2, HALF, CHUNK)
     send_a, send_b, keep_a, keep_b = call(first_half, (two, two, wide, wide), [VMEM] * 2)(

time: 150 us -> 141 us (0.940)
  the two profiles are of different devices: /device:TPU:1 before, /device:TPU:66 now
where the time goes in v3:
time: 141 us; the launch traced here: 140 us
  starting transfers between devices  72.6 us (51%)
  waiting for transfers between devices  24.9 us (18%)
  blocking collectives  22.9 us (16%)
  Pallas kernels  11.5 us (8%)
  local copies, waits for them, and re-layouts  7.3 us (5%)
    ppermute x7, starting transfers between devices, partner(): lax.ppermute(x, axis, [(i, i ^ mask) for i in range(lax.axis_size(axis))])  29 us
    ppermute x3, starting transfers between devices, shift(): return lax.ppermute(x, axis, [(i, (i + step) % 4) for i in range(4)])  23.2 us
    all_to_all x1, blocking collectives, exchange(): return lax.all_to_all(x, axis, split_axis=0, concat_axis=0, tiled=True)  22.9 us
    all_to_all x3, starting transfers between devices, exchange(): return lax.all_to_all(x, axis, split_axis=0, concat_axis=0, tiled=True)  20.4 us
    ppermute x7, waiting for transfers between devices, partner(): lax.ppermute(x, axis, [(i, i ^ mask) for i in range(lax.axis_size(axis))])  19.1 us
    unnamed x18, local copies, waits for them, and re-layouts  7.3 us
    ppermute x3, waiting for transfers between devices, shift(): return lax.ppermute(x, axis, [(i, (i + step) % 4) for i in range(4)])  5.29 us
  transfers between devices with their start and end apart: 13, of which 9 were waited for; matrix products, arithmetic and copies ran while one was open for 0% of the time, Pallas kernels for 2%

profile of v3, /device:TPU:66, one launch (start us, length us, event | category | flops | bytes accessed | tf_op | source)
XLA Modules:
  0.0 140.2 jit_solution(7652958516661953639)
XLA Ops:
  0.0 0.0 copy-start.4
  0.0 0.9 copy-done.4
  0.9 0.0 copy-start.5
  0.9 0.7 copy-done.5
  1.6 0.0 copy-start.6
  1.6 0.7 copy-done.6
  2.3 1.2 shard_map.74
  3.5 5.5 %all-to-all-start = ((bf16[4,16,1792]{2,1,0:T(8,128)(2,1)}), bf16[4,16,1792]{2,1,0:T(8,128)(2,1)S(1)}, u32[]{:S(2)}, u32[]{:S(2)}) async-start(bf16[4,16,1792]{2,1,0:T(8,128)(2,1)} %get-tuple-element.26), calls=%async_computation | async-start | bytes 458752 | tf_op jit(solution)/shard_map/all_to_all | solution.py:194
  9.7 0.0 copy-start.1
  9.7 1.5 %copy-done.1 = bf16[1,1,56,128,128]{4,3,2,1,0:T(8,128)(2,1)S(1)} copy-done((bf16[1,1,56,128,128]{4,3,2,1,0:T(8,128)(2,1)S(1)}, bf16[1,1,56,128,128]{4,3,2,1,0:T(8,128)(2,1)}, u32[]{:S(2)}) %copy-start.1) | copy-done | bytes 1835032
  11.2 0.0 copy-start.7
  11.2 0.7 copy-done.7
  11.9 0.0 copy-start.8
  11.9 0.7 copy-done.8
  12.5 1.2 shard_map.73.after.dense
  13.8 0.5 all-to-all-done.gathered
  14.3 2.2 %shard_map.75 = bf16[16,64,768]{2,1,0:T(8,128)(2,1)S(1)} custom-call(bf16[5,128,1024]{2,1,0:T(8,128)(2,1)S(1)} %shard_map.73.after.dense, bf16[4,16,1792]{2,1,0:T(8,128)(2,1)S(1)} %all-to-all-done.gathered), custom_call_target="tpu_custom_call" | custom-call | tf_op jit(solution)/shard_map/pallas_call | solution.py:220
  16.5 0.0 copy-start
  16.5 1.2 copy-done
  17.7 7.5 %all-to-all-start.1 = ((bf16[16,64,768]{2,1,0:T(8,128)(2,1)}), bf16[16,64,768]{2,1,0:T(8,128)(2,1)S(1)}, u32[]{:S(2)}, u32[]{:S(2)}) async-start(bf16[16,64,768]{2,1,0:T(8,128)(2,1)} %copy-done), calls=%async_computation.1 | async-start | bytes 3145728 | tf_op jit(solution)/shard_map/all_to_all | solution.py:194
  25.1 0.1 pad_add_fusion.place
  25.2 0.6 shard_map.76
  25.8 1.9 %collective-permute-start = (bf16[4,64,128]{2,1,0:T(8,128)(2,1)S(1)}, bf16[4,64,128]{2,1,0:T(8,128)(2,1)S(1)}, u32[]{:S(2)}, u32[]{:S(2)}) collective-permute-start(bf16[4,64,128]{2,1,0:T(8,128)(2,1)S(1)} %get-tuple-element.29), channel_id=1, source_target_pairs={{0,1},{1,0},{2,3},{3,2},{4,5},{5,4},{6,7},{7,6},{8,9},{9,8},{10,11... | collective-permute-start | bytes 196616 | tf_op jit(solution)/shard_map/ppermute | solution.py:202
  27.7 1.2 collective-permute-done.got
  29.0 0.6 shard_map.77
  29.5 9.1 %collective-permute-start.1 = (bf16[2,64,128]{2,1,0:T(8,128)(2,1)S(1)}, bf16[2,64,128]{2,1,0:T(8,128)(2,1)S(1)}, u32[]{:S(2)}, u32[]{:S(2)}) collective-permute-start(bf16[2,64,128]{2,1,0:T(8,128)(2,1)S(1)} %get-tuple-element.31), channel_id=1, source_target_pairs={{0,2},{2,4},{4,6},{6,0},{1,3},{3,5},{5,7},{7,1},{8,10},{10,12},{12... | collective-permute-start | bytes 98312 | tf_op jit(solution)/shard_map/ppermute | solution.py:198
  38.6 8.7 %collective-permute-start.2 = (bf16[2,64,128]{2,1,0:T(8,128)(2,1)S(1)}, bf16[2,64,128]{2,1,0:T(8,128)(2,1)S(1)}, u32[]{:S(2)}, u32[]{:S(2)}) collective-permute-start(bf16[2,64,128]{2,1,0:T(8,128)(2,1)S(1)} %get-tuple-element.32), channel_id=1, source_target_pairs={{0,4},{2,6},{4,0},{6,2},{1,5},{3,7},{5,1},{7,3},{8,12},{10,14},{12... | collective-permute-start | bytes 98312 | tf_op jit(solution)/shard_map/ppermute | solution.py:198
  47.3 5.5 %collective-permute-start.3 = (bf16[2,64,128]{2,1,0:T(8,128)(2,1)S(1)}, bf16[2,64,128]{2,1,0:T(8,128)(2,1)S(1)}, u32[]{:S(2)}, u32[]{:S(2)}) collective-permute-start(bf16[2,64,128]{2,1,0:T(8,128)(2,1)S(1)} %get-tuple-element.33), channel_id=1, source_target_pairs={{0,6},{2,0},{4,2},{6,4},{1,7},{3,1},{5,3},{7,5},{8,14},{10,8},{12,... | collective-permute-start | bytes 98312 | tf_op jit(solution)/shard_map/ppermute | solution.py:198
  52.8 0.0 collective-permute-done.1.refs_1_
  52.8 0.7 collective-permute-done.2.refs_2_
  53.5 4.6 %collective-permute-done.3.refs_3_ = bf16[2,64,128]{2,1,0:T(8,128)(2,1)S(1)} collective-permute-done((bf16[2,64,128]{2,1,0:T(8,128)(2,1)S(1)}, bf16[2,64,128]{2,1,0:T(8,128)(2,1)S(1)}, u32[]{:S(2)}, u32[]{:S(2)}) %collective-permute-start.3) | collective-permute-done | bytes 32800 | tf_op jit(solution)/shard_map/ppermute | solution.py:198
  58.0 0.6 shard_map.78
  58.6 0.0 all-to-all-done.1
  58.6 1.9 %shard_map.79 = (bf16[4,128,512]{2,1,0:T(8,128)(2,1)S(1)}, f32[4,128,512]{2,1,0:T(8,128)S(1)}) custom-call(s32[2]{0:T(128)S(1)} %pad_add_fusion.place, bf16[5,128,1024]{2,1,0:T(8,128)(2,1)S(1)} %shard_map.73.after.dense, bf16[1024,768]{1,0:T(8,128)(2,1)S(1)} %bitcast.13, bf16[48,1024]{1,0:T(8,128)(2,1)S(1)} %get-tuple-element.34.after.rows), custom_call_target="tpu_custom_call" | custom-call | tf_op jit(solution)/shard_map/pallas_call | solution.py:241
  60.5 0.0 copy-start.2
  60.5 1.0 copy-done.2
  61.5 1.3 shard_map.82
  62.8 0.0 copy-start.3
  62.8 7.4 %all-to-all-start.2 = ((bf16[16,48,1024]{2,1,0:T(8,128)(2,1)}), bf16[16,48,1024]{2,1,0:T(8,128)(2,1)S(1)}, u32[]{:S(2)}, u32[]{:S(2)}) async-start(bf16[16,48,1024]{2,1,0:T(8,128)(2,1)} %shard_map.82), calls=%async_computation.2 | async-start | bytes 3145728 | tf_op jit(solution)/shard_map/all_to_all | solution.py:194
  70.2 1.9 %collective-permute-start.4 = (bf16[4,128,512]{2,1,0:T(8,128)(2,1)S(1)}, bf16[4,128,512]{2,1,0:T(8,128)(2,1)S(1)}, u32[]{:S(2)}, u32[]{:S(2)}) collective-permute-start(bf16[4,128,512]{2,1,0:T(8,128)(2,1)S(1)} %get-tuple-element.36.after), channel_id=1, source_target_pairs={{0,1},{1,0},{2,3},{3,2},{4,5},{5,4},{6,7},{7,6},{8,9},{9,8},{10,11... | collective-permute-start | bytes 1572872 | tf_op jit(solution)/shard_map/ppermute | solution.py:202
  72.1 1.9 %collective-permute-done.4.got = bf16[4,128,512]{2,1,0:T(8,128)(2,1)S(1)} collective-permute-done((bf16[4,128,512]{2,1,0:T(8,128)(2,1)S(1)}, bf16[4,128,512]{2,1,0:T(8,128)(2,1)S(1)}, u32[]{:S(2)}, u32[]{:S(2)}) %collective-permute-start.4) | collective-permute-done | bytes 524320 | tf_op jit(solution)/shard_map/ppermute | solution.py:202
  74.0 0.0 copy-done.3
  74.0 0.1 shard_map.80
  74.1 1.9 %collective-permute-start.5 = (bf16[2,64,512]{2,1,0:T(8,128)(2,1)S(1)}, bf16[2,64,512]{2,1,0:T(8,128)(2,1)S(1)}, u32[]{:S(2)}, u32[]{:S(2)}) collective-permute-start(bf16[2,64,512]{2,1,0:T(8,128)(2,1)S(1)} %get-tuple-element.39), channel_id=1, source_target_pairs={{0,2},{2,0},{4,6},{6,4},{1,3},{3,1},{5,7},{7,5},{8,10},{10,8},{12,... | collective-permute-start | bytes 393224 | tf_op jit(solution)/shard_map/ppermute | solution.py:202
  76.1 6.6 %collective-permute-start.6 = (bf16[2,64,512]{2,1,0:T(8,128)(2,1)S(1)}, bf16[2,64,512]{2,1,0:T(8,128)(2,1)S(1)}, u32[]{:S(2)}, u32[]{:S(2)}) collective-permute-start(bf16[2,64,512]{2,1,0:T(8,128)(2,1)S(1)} %get-tuple-element.40), channel_id=1, source_target_pairs={{0,6},{2,4},{4,2},{6,0},{1,7},{3,5},{5,3},{7,1},{8,14},{10,12},{12... | collective-permute-start | bytes 393224 | tf_op jit(solution)/shard_map/ppermute | solution.py:202
  82.6 5.9 %collective-permute-done.5.got_a = bf16[2,64,512]{2,1,0:T(8,128)(2,1)S(1)} collective-permute-done((bf16[2,64,512]{2,1,0:T(8,128)(2,1)S(1)}, bf16[2,64,512]{2,1,0:T(8,128)(2,1)S(1)}, u32[]{:S(2)}, u32[]{:S(2)}) %collective-permute-start.5) | collective-permute-done | bytes 131104 | tf_op jit(solution)/shard_map/ppermute | solution.py:202
  88.6 4.8 %collective-permute-done.6.got_b = bf16[2,64,512]{2,1,0:T(8,128)(2,1)S(1)} collective-permute-done((bf16[2,64,512]{2,1,0:T(8,128)(2,1)S(1)}, bf16[2,64,512]{2,1,0:T(8,128)(2,1)S(1)}, u32[]{:S(2)}, u32[]{:S(2)}) %collective-permute-start.6) | collective-permute-done | bytes 131104 | tf_op jit(solution)/shard_map/ppermute | solution.py:202
  93.4 8.4 %collective-permute-start.7 = (bf16[64,512]{1,0:T(8,128)(2,1)S(1)}, bf16[64,512]{1,0:T(8,128)(2,1)S(1)}, u32[]{:S(2)}, u32[]{:S(2)}) collective-permute-start(bf16[64,512]{1,0:T(8,128)(2,1)S(1)} %get-tuple-element.42), channel_id=1, source_target_pairs={{0,6},{2,4},{4,2},{6,0},{1,7},{3,5},{5,3},{7,1},{8,14},{10,12},{12... | collective-permute-start | bytes 196616 | tf_op jit(solution)/shard_map/ppermute | solution.py:202
  101.8 6.4 %collective-permute-start.8 = (bf16[64,512]{1,0:T(8,128)(2,1)S(1)}, bf16[64,512]{1,0:T(8,128)(2,1)S(1)}, u32[]{:S(2)}, u32[]{:S(2)}) collective-permute-start(bf16[64,512]{1,0:T(8,128)(2,1)S(1)} %get-tuple-element.43), channel_id=1, source_target_pairs={{0,2},{2,0},{4,6},{6,4},{1,3},{3,1},{5,7},{7,5},{8,10},{10,8},{12,... | collective-permute-start | bytes 196616 | tf_op jit(solution)/shard_map/ppermute | solution.py:202
  108.2 0.0 collective-permute-done.7.got_a
  108.2 4.0 %collective-permute-done.8.got_b = bf16[64,512]{1,0:T(8,128)(2,1)S(1)} collective-permute-done((bf16[64,512]{1,0:T(8,128)(2,1)S(1)}, bf16[64,512]{1,0:T(8,128)(2,1)S(1)}, u32[]{:S(2)}, u32[]{:S(2)}) %collective-permute-start.8) | collective-permute-done | bytes 65568 | tf_op jit(solution)/shard_map/ppermute | solution.py:202
  112.2 0.0 all-to-all-done.2
  112.2 1.2 shard_map.83
  113.4 1.9 %collective-permute-start.9 = (bf16[4,16,1024]{2,1,0:T(8,128)(2,1)S(1)}, bf16[4,16,1024]{2,1,0:T(8,128)(2,1)S(1)}, u32[]{:S(2)}, u32[]{:S(2)}) collective-permute-start(bf16[4,16,1024]{2,1,0:T(8,128)(2,1)S(1)} %get-tuple-element.46), channel_id=1, source_target_pairs={{0,1},{1,0},{2,3},{3,2},{4,5},{5,4},{6,7},{7,6},{8,9},{9,8},{10,11... | collective-permute-start | bytes 393224 | tf_op jit(solution)/shard_map/ppermute | solution.py:202
  115.3 1.3 collective-permute-done.9.got
  116.7 22.9 %all_to_all.20.got = bf16[4,16,1024]{2,1,0:T(8,128)(2,1)S(1)} all-to-all(bf16[4,16,1024]{2,1,0:T(8,128)(2,1)S(1)} %shard_map.84), channel_id=1, replica_groups=mesh['y'=4,'x'=4,'zl'=4,'zh'=4,'core'=2] {'zh'}, dimensions={0} | all-to-all | bytes 262144 | tf_op jit(solution)/shard_map/all_to_all | solution.py:194
  139.5 0.6 shard_map.85
  (2 shorter events, 0.1 us)
Async XLA Ops:
  0.0 0.9 copy-start.4
  0.9 0.7 copy-start.5
  1.6 0.7 copy-start.6
  3.5 10.7 %all-to-all-start = ((bf16[4,16,1792]{2,1,0:T(8,128)(2,1)}), bf16[4,16,1792]{2,1,0:T(8,128)(2,1)S(1)}, u32[]{:S(2)}, u32[]{:S(2)}) async-start(bf16[4,16,1792]{2,1,0:T(8,128)(2,1)} %get-tuple-element.26), calls=%async_computation | async-start | bytes 458752 | tf_op jit(solution)/shard_map/all_to_all | solution.py:194
  9.7 1.5 %copy-start.1 = (bf16[1,1,56,128,128]{4,3,2,1,0:T(8,128)(2,1)S(1)}, bf16[1,1,56,128,128]{4,3,2,1,0:T(8,128)(2,1)}, u32[]{:S(2)}) copy-start(bf16[1,1,56,128,128]{4,3,2,1,0:T(8,128)(2,1)} %param.10) | copy-start | bytes 5505028
  11.2 0.7 copy-start.7
  11.9 0.7 copy-start.8
  16.5 1.2 copy-start
  17.7 41.0 %all-to-all-start.1 = ((bf16[16,64,768]{2,1,0:T(8,128)(2,1)}), bf16[16,64,768]{2,1,0:T(8,128)(2,1)S(1)}, u32[]{:S(2)}, u32[]{:S(2)}) async-start(bf16[16,64,768]{2,1,0:T(8,128)(2,1)} %copy-done), calls=%async_computation.1 | async-start | bytes 3145728 | tf_op jit(solution)/shard_map/all_to_all | solution.py:194
  25.8 3.1 %collective-permute-start = (bf16[4,64,128]{2,1,0:T(8,128)(2,1)S(1)}, bf16[4,64,128]{2,1,0:T(8,128)(2,1)S(1)}, u32[]{:S(2)}, u32[]{:S(2)}) collective-permute-start(bf16[4,64,128]{2,1,0:T(8,128)(2,1)S(1)} %get-tuple-element.29), channel_id=1, source_target_pairs={{0,1},{1,0},{2,3},{3,2},{4,5},{5,4},{6,7},{7,6},{8,9},{9,8},{10,11... | collective-permute-start | bytes 196616 | tf_op jit(solution)/shard_map/ppermute | solution.py:202
  29.5 23.2 %collective-permute-start.1 = (bf16[2,64,128]{2,1,0:T(8,128)(2,1)S(1)}, bf16[2,64,128]{2,1,0:T(8,128)(2,1)S(1)}, u32[]{:S(2)}, u32[]{:S(2)}) collective-permute-start(bf16[2,64,128]{2,1,0:T(8,128)(2,1)S(1)} %get-tuple-element.31), channel_id=1, source_target_pairs={{0,2},{2,4},{4,6},{6,0},{1,3},{3,5},{5,7},{7,1},{8,10},{10,12},{12... | collective-permute-start | bytes 98312 | tf_op jit(solution)/shard_map/ppermute | solution.py:198
  38.6 14.9 %collective-permute-start.2 = (bf16[2,64,128]{2,1,0:T(8,128)(2,1)S(1)}, bf16[2,64,128]{2,1,0:T(8,128)(2,1)S(1)}, u32[]{:S(2)}, u32[]{:S(2)}) collective-permute-start(bf16[2,64,128]{2,1,0:T(8,128)(2,1)S(1)} %get-tuple-element.32), channel_id=1, source_target_pairs={{0,4},{2,6},{4,0},{6,2},{1,5},{3,7},{5,1},{7,3},{8,12},{10,14},{12... | collective-permute-start | bytes 98312 | tf_op jit(solution)/shard_map/ppermute | solution.py:198
  47.3 10.8 %collective-permute-start.3 = (bf16[2,64,128]{2,1,0:T(8,128)(2,1)S(1)}, bf16[2,64,128]{2,1,0:T(8,128)(2,1)S(1)}, u32[]{:S(2)}, u32[]{:S(2)}) collective-permute-start(bf16[2,64,128]{2,1,0:T(8,128)(2,1)S(1)} %get-tuple-element.33), channel_id=1, source_target_pairs={{0,6},{2,0},{4,2},{6,4},{1,7},{3,1},{5,3},{7,5},{8,14},{10,8},{12,... | collective-permute-start | bytes 98312 | tf_op jit(solution)/shard_map/ppermute | solution.py:198
  60.5 1.0 copy-start.2
  62.8 11.2 %copy-start.3 = (f32[4,128,512]{2,1,0:T(8,128)S(1)}, f32[4,128,512]{2,1,0:T(8,128)}, u32[]{:S(2)}) copy-start(f32[4,128,512]{2,1,0:T(8,128)} %copy-done.2) | copy-start | bytes 3145732
  62.8 49.3 %all-to-all-start.2 = ((bf16[16,48,1024]{2,1,0:T(8,128)(2,1)}), bf16[16,48,1024]{2,1,0:T(8,128)(2,1)S(1)}, u32[]{:S(2)}, u32[]{:S(2)}) async-start(bf16[16,48,1024]{2,1,0:T(8,128)(2,1)} %shard_map.82), calls=%async_computation.2 | async-start | bytes 3145728 | tf_op jit(solution)/shard_map/all_to_all | solution.py:194
  70.2 3.8 %collective-permute-start.4 = (bf16[4,128,512]{2,1,0:T(8,128)(2,1)S(1)}, bf16[4,128,512]{2,1,0:T(8,128)(2,1)S(1)}, u32[]{:S(2)}, u32[]{:S(2)}) collective-permute-start(bf16[4,128,512]{2,1,0:T(8,128)(2,1)S(1)} %get-tuple-element.36.after), channel_id=1, source_target_pairs={{0,1},{1,0},{2,3},{3,2},{4,5},{5,4},{6,7},{7,6},{8,9},{9,8},{10,11... | collective-permute-start | bytes 1572872 | tf_op jit(solution)/shard_map/ppermute | solution.py:202
  74.1 14.5 %collective-permute-start.5 = (bf16[2,64,512]{2,1,0:T(8,128)(2,1)S(1)}, bf16[2,64,512]{2,1,0:T(8,128)(2,1)S(1)}, u32[]{:S(2)}, u32[]{:S(2)}) collective-permute-start(bf16[2,64,512]{2,1,0:T(8,128)(2,1)S(1)} %get-tuple-element.39), channel_id=1, source_target_pairs={{0,2},{2,0},{4,6},{6,4},{1,3},{3,1},{5,7},{7,5},{8,10},{10,8},{12,... | collective-permute-start | bytes 393224 | tf_op jit(solution)/shard_map/ppermute | solution.py:202
  76.1 17.3 %collective-permute-start.6 = (bf16[2,64,512]{2,1,0:T(8,128)(2,1)S(1)}, bf16[2,64,512]{2,1,0:T(8,128)(2,1)S(1)}, u32[]{:S(2)}, u32[]{:S(2)}) collective-permute-start(bf16[2,64,512]{2,1,0:T(8,128)(2,1)S(1)} %get-tuple-element.40), channel_id=1, source_target_pairs={{0,6},{2,4},{4,2},{6,0},{1,7},{3,5},{5,3},{7,1},{8,14},{10,12},{12... | collective-permute-start | bytes 393224 | tf_op jit(solution)/shard_map/ppermute | solution.py:202
  93.4 14.8 %collective-permute-start.7 = (bf16[64,512]{1,0:T(8,128)(2,1)S(1)}, bf16[64,512]{1,0:T(8,128)(2,1)S(1)}, u32[]{:S(2)}, u32[]{:S(2)}) collective-permute-start(bf16[64,512]{1,0:T(8,128)(2,1)S(1)} %get-tuple-element.42), channel_id=1, source_target_pairs={{0,6},{2,4},{4,2},{6,0},{1,7},{3,5},{5,3},{7,1},{8,14},{10,12},{12... | collective-permute-start | bytes 196616 | tf_op jit(solution)/shard_map/ppermute | solution.py:202
  101.8 10.4 %collective-permute-start.8 = (bf16[64,512]{1,0:T(8,128)(2,1)S(1)}, bf16[64,512]{1,0:T(8,128)(2,1)S(1)}, u32[]{:S(2)}, u32[]{:S(2)}) collective-permute-start(bf16[64,512]{1,0:T(8,128)(2,1)S(1)} %get-tuple-element.43), channel_id=1, source_target_pairs={{0,2},{2,0},{4,6},{6,4},{1,3},{3,1},{5,7},{7,5},{8,10},{10,8},{12,... | collective-permute-start | bytes 196616 | tf_op jit(solution)/shard_map/ppermute | solution.py:202
  113.4 3.2 %collective-permute-start.9 = (bf16[4,16,1024]{2,1,0:T(8,128)(2,1)S(1)}, bf16[4,16,1024]{2,1,0:T(8,128)(2,1)S(1)}, u32[]{:S(2)}, u32[]{:S(2)}) collective-permute-start(bf16[4,16,1024]{2,1,0:T(8,128)(2,1)S(1)} %get-tuple-element.46), channel_id=1, source_target_pairs={{0,1},{1,0},{2,3},{3,2},{4,5},{5,4},{6,7},{7,6},{8,9},{9,8},{10,11... | collective-permute-start | bytes 393224 | tf_op jit(solution)/shard_map/ppermute | solution.py:202

commit v4 on v1

v4 whole, which is shorter than its diff:
```python
import jax
import jax.numpy as jnp
from jax import lax
from jax.experimental import pallas as pl
from jax.experimental.pallas import tpu as pltpu
from jax.sharding import Mesh
from jax.sharding import PartitionSpec as P

BF = jnp.bfloat16
F32 = jnp.float32
NODE = ("y", "x", "zl")
REL = ("zh", "core")
YX = ("y", "x")
VMEM = pl.BlockSpec(memory_space=pltpu.VMEM)
ANY = pl.BlockSpec(memory_space=pl.ANY)
SMEM = pl.BlockSpec(memory_space=pltpu.SMEM)
PARAMS = pltpu.CompilerParams(vmem_limit_bytes=16 * 1024 * 1024)

RELS = 5
DIN = 768
DOUT = 1024
TILE = 128
SRC = 8
ROWS = 16
NODES = 64
PER = 12
SLOT = 8
SELF = 2
CHUNK = SLOT * NODES
WEIGHT = 10**11


def call(body, outs, ins, scratch=(), cost=None):
    return pl.pallas_call(
        body,
        cost_estimate=cost,
        out_shape=outs,
        in_specs=ins,
        out_specs=jax.tree.map(lambda _: VMEM, outs),
        scratch_shapes=list(scratch),
        compiler_params=PARAMS,
    )


def shape(kind, *dims):
    return jax.ShapeDtypeStruct(dims, kind)


def start(own, turned, copies):
    src = lax.broadcasted_iota(jnp.int32, (DIN, DIN), 0)
    out = lax.broadcasted_iota(jnp.int32, (DIN, DIN), 1)
    swap = jnp.where(src == PER * (out & (NODES - 1)) + (out >> 6), 1.0, 0.0).astype(BF)
    value = jnp.dot(own[...], swap, preferred_element_type=F32).astype(BF)
    turned[...] = value
    for i in range(4):
        copies[i] = value


def weigh(place, coef, turned, bases, send, keep, rows, parcel):
    rows[...] = jnp.zeros_like(rows)
    for d in range(PER):
        part = jnp.dot(
            coef[...], bases[d].astype(F32), precision=lax.Precision.HIGHEST, preferred_element_type=F32
        )
        for r in range(RELS):
            j = r * PER + d
            rows[j // SLOT, j % SLOT : j % SLOT + 1] = part[r : r + 1]
        rows[d // SELF, SLOT + d % SELF : SLOT + d % SELF + 1] = part[RELS:]
    for k in range(8):
        if k < DIN // TILE:
            parcel[k, :ROWS] = turned[:, k * TILE : (k + 1) * TILE]
        else:
            parcel[k, :ROWS] = jnp.zeros((ROWS, TILE), BF)
        parcel[k, ROWS:] = rows[k].astype(BF)
    core = place[0]
    for z in range(4):
        keep[z] = parcel[2 * z + core]
        send[z] = parcel[2 * z + 1 - core]


def join_cores(place, after, keep, got, out):
    core = place[0]
    mine = pl.ds(pl.multiple_of(core * TILE, TILE), TILE)
    other = pl.ds(pl.multiple_of((1 - core) * TILE, TILE), TILE)
    for z in range(4):
        for i in range(4):
            out[4 * z + i, :, mine] = keep[z]
            out[4 * z + i, :, other] = got[z]


def join_groups(place, got, own, rows):
    zl = place[1]
    for z in range(4):
        for c in range(2):
            own[2 * z + c] = got[4 * z + zl, :ROWS, c * TILE : (c + 1) * TILE]
        part = [got[4 * z + i, ROWS:].astype(F32)[:PER] for i in range(4)]
        rows[:, 2 * z * TILE : 2 * (z + 1) * TILE] = jnp.concatenate(part, axis=0).astype(BF)


def densify(count, source, relation, values, dense, acc):
    acc[...] = jnp.zeros_like(acc)

    def add(t, _):
        spot = relation[t] * SRC + source[t]
        acc[spot] = acc[spot] + values[t].astype(F32)
        return 0

    lax.fori_loop(0, count[0], add, 0)
    for r in range(RELS):
        for s in range(SRC):
            dense[r, :, s * TILE : (s + 1) * TILE] = acc[r * SRC + s].astype(BF)


def aggregate(place, dense, feats, send, keep, full):
    for r in range(RELS):
        full[:, r * DIN : (r + 1) * DIN] = jnp.dot(dense[r], feats[...], preferred_element_type=F32)
    full[:, RELS * DIN :] = jnp.zeros((TILE, 8 * CHUNK - RELS * DIN), F32)
    core = place[0]
    for z in range(4):
        keep[z] = full[:, pl.ds(pl.multiple_of((2 * z + core) * CHUNK, CHUNK), CHUNK)]
        send[z] = full[:, pl.ds(pl.multiple_of((2 * z + 1 - core) * CHUNK, CHUNK), CHUNK)].astype(BF)


def arrange(sums, own, msgs):
    src = lax.broadcasted_iota(jnp.int32, (CHUNK + TILE, DIN), 0)
    out = lax.broadcasted_iota(jnp.int32, (CHUNK + TILE, DIN), 1)
    swap = jnp.where(out == PER * (src & (NODES - 1)) + (src >> 6), 1.0, 0.0).astype(BF)
    value = jnp.concatenate([sums[...], own[...]], axis=1)
    msgs[...] = jnp.dot(value, swap, preferred_element_type=F32).astype(BF)


def transform(place, msgs, weights, send, keep, part):
    core = place[0]
    part[...] = jnp.dot(msgs[...], weights[...], preferred_element_type=F32)
    for z in range(4):
        keep[z] = part[pl.ds(pl.multiple_of((2 * z + core) * ROWS, ROWS), ROWS)]
        send[z] = part[pl.ds(pl.multiple_of((2 * z + 1 - core) * ROWS, ROWS), ROWS)].astype(BF)


def pair_sum(keep, got, out):
    out[...] = (keep[...] + got[...].astype(F32)).astype(BF)


def finish(got, out):
    total = got[0].astype(F32)
    for i in range(1, 4):
        total = total + got[i].astype(F32)
    out[...] = jnp.maximum(total, 0.0).astype(BF)


def exchange(x, axis):
    return lax.all_to_all(x, axis, split_axis=0, concat_axis=0, tiled=True)


def spread(x, axis):
    return exchange(jnp.broadcast_to(x, (lax.axis_size(axis), *x.shape)), axis)


def partner(x):
    return lax.ppermute(x, "core", [(0, 1), (1, 0)])


def on_device(features, bases, coefficients, tile_values, tile_source, tile_relation, tile_count):
    place = jnp.stack([lax.axis_index(a) for a in ("core", "zl")]).astype(jnp.int32)
    turned, copies = call(
        start, (shape(BF, ROWS, DIN), shape(BF, 4, ROWS, DIN)), [VMEM]
    )(features[0])
    feats = exchange(copies, "zl").reshape(NODES, DIN)
    feats = spread(feats, YX).reshape(SRC * TILE, DIN)

    dense = call(
        densify,
        shape(BF, RELS, TILE, SRC * TILE),
        [SMEM, SMEM, SMEM, VMEM],
        [pltpu.VMEM((RELS * SRC, TILE, TILE), F32)],
    )(tile_count[0], tile_source[0, 0], tile_relation[0, 0], tile_values[0, 0])
    part = shape(F32, 4, TILE, CHUNK)
    send, keep = call(
        aggregate,
        (shape(BF, 4, TILE, CHUNK), part),
        [SMEM, VMEM, VMEM],
        [pltpu.VMEM((TILE, 8 * CHUNK), F32)],
    )(place, dense, feats)
    pair = call(pair_sum, shape(BF, 4, TILE, CHUNK), [VMEM] * 2)(keep, partner(send))
    sums = lax.psum_scatter(pair.reshape(4 * TILE, CHUNK), "zh", scatter_dimension=0, tiled=True)

    parcel = shape(BF, 4, 2 * ROWS, TILE)
    send, keep = call(
        weigh,
        (parcel, parcel),
        [SMEM] + [VMEM] * 3,
        [pltpu.VMEM((8, ROWS, TILE), F32), pltpu.VMEM((8, 2 * ROWS, TILE), BF)],
    )(place, coefficients, turned, jnp.swapaxes(bases, 0, 1))
    joined = call(join_cores, shape(BF, 16, 2 * ROWS, 2 * TILE), [SMEM, ANY, VMEM, VMEM])(
        place, pair, keep, partner(send)
    )
    own, rows = call(
        join_groups,
        (shape(BF, 8, ROWS, TILE), shape(BF, 4 * PER, DOUT)),
        [SMEM, VMEM],
    )(place, exchange(joined, ("zh", "zl")))
    weights = spread(rows, YX).reshape(NODES * PER, DOUT)
    msgs = call(
        arrange,
        shape(BF, TILE, DIN),
        [VMEM] * 2,
        cost=pl.CostEstimate(flops=WEIGHT, bytes_accessed=1 << 20, transcendentals=0),
    )(sums, own.reshape(TILE, TILE))

    send, keep = call(
        transform,
        (shape(BF, 4, ROWS, DOUT), shape(F32, 4, ROWS, DOUT)),
        [SMEM] + [VMEM] * 2,
        [pltpu.VMEM((TILE, DOUT), F32)],
    )(place, msgs, weights)
    pair = call(pair_sum, shape(BF, 4, ROWS, DOUT), [VMEM] * 2)(keep, partner(send))
    return call(finish, shape(BF, ROWS, DOUT), [VMEM])(exchange(pair, "zh"))[None]


def solution(mesh):
    split = Mesh(mesh.devices.reshape(4, 4, 4, 4, 2), NODE + REL)
    return jax.shard_map(
        on_device,
        mesh=split,
        in_specs=(
            P(REL, NODE, None),
            P(None, NODE, REL),
            P(),
            P(NODE, REL, None, None, None),
            P(NODE, REL, None),
            P(NODE, REL, None),
            P(NODE, REL),
        ),
        out_specs=P(REL, NODE, None),
        check_vma=False,
    )
```

time: 160 us -> 167 us (1.044)
  waiting for transfers between devices: 59.1 us -> 37.4 us
  blocking collectives: 51.3 us -> 71.8 us
  between operations: 0.82 us -> 14.2 us
  starting transfers between devices: 32.8 us -> 27.4 us
  Pallas kernels: 6.29 us -> 8.3 us
    all_to_all x4 -> x2, waiting for transfers between devices: 56.6 us -> 29.7 us  [exchange(): return lax.all_to_all(x, axis, split_axis=0, concat_axis=0, tiled=True)]
    all_to_all x3, blocking collectives: 51.3 us -> 71.8 us  [exchange(): return lax.all_to_all(x, axis, split_axis=0, concat_axis=0, tiled=True)]
    all_to_all x4 -> x2, starting transfers between devices: 18.8 us -> 10.6 us  [exchange(): return lax.all_to_all(x, axis, split_axis=0, concat_axis=0, tiled=True)]
    reduce_scatter x0 -> x1, waiting for transfers between devices: none -> 4.4 us  [on_device(): lax.psum_scatter(pair.reshape(4 * TILE, CHUNK), 'zh', scatter_dimension=0...]
    ppermute x2 -> x3, starting transfers between devices: 14 us -> 16.8 us  [partner(): return lax.ppermute(x, 'core', [(0, 1), (1, 0)])]
    pallas_call x7 -> x11, Pallas kernels: 6.29 us -> 8.3 us  [the longest x1 1.88 us: on_device(): call(aggregate, (shape(BF, 4, TILE, CHUNK), part), [SMEM, VMEM, VMEM], [p...]
    unnamed x13 -> x14, local copies, waits for them, and re-layouts: 3.87 us -> 3.16 us
  transfers between devices with their start and end apart: 6 -> 6, of which waited for: 6 -> 6; matrix products, arithmetic and copies ran while one was open for 0% -> 1% of each run, Pallas kernels for 2% -> 2%
where the time goes in v4:
time: 167 us; the launch traced here: 165 us
  blocking collectives  71.8 us (43%)
  waiting for transfers between devices  37.4 us (22%)
  starting transfers between devices  27.4 us (16%)
  between operations  14.2 us (9%)
  Pallas kernels  8.3 us (5%)
  local copies, waits for them, and re-layouts  5.86 us (4%)
    all_to_all x3, blocking collectives, exchange(): return lax.all_to_all(x, axis, split_axis=0, concat_axis=0, tiled=True)  71.8 us
    all_to_all x2, waiting for transfers between devices, exchange(): return lax.all_to_all(x, axis, split_axis=0, concat_axis=0, tiled=True)  29.7 us
    ppermute x3, starting transfers between devices, partner(): return lax.ppermute(x, 'core', [(0, 1), (1, 0)])  16.8 us
    all_to_all x2, starting transfers between devices, exchange(): return lax.all_to_all(x, axis, split_axis=0, concat_axis=0, tiled=True)  10.6 us
    reduce_scatter x1, waiting for transfers between devices, on_device(): lax.psum_scatter(pair.reshape(4 * TILE, CHUNK), 'zh', scatter_dimension=0...  4.4 us
  transfers between devices with their start and end apart: 6, of which 6 were waited for; matrix products, arithmetic and copies ran while one was open for 1% of the time, Pallas kernels for 2%

profile of v4, /device:TPU:1, one launch (start us, length us, event | category | flops | bytes accessed | tf_op | source)
XLA Modules:
  0.0 165.1 jit_solution(10981682380432232817)
XLA Ops:
  6.5 0.0 copy-start.2
  6.5 0.7 copy-done.2
  7.3 0.3 shard_map.74
  7.6 10.9 %all_to_all.25 = bf16[4,16,768]{2,1,0:T(8,128)(2,1)S(1)} all-to-all(bf16[4,16,768]{2,1,0:T(8,128)(2,1)S(1)} %get-tuple-element.15), channel_id=1, replica_groups=mesh['y'=4,'x'=4,'zl'=4,'zh'=4,'core'=2] {'zl'}, dimensions={0} | all-to-all | bytes 196608 | tf_op jit(solution)/shard_map/all_to_all | solution.py:152
  18.5 1.3 broadcast_in_dim.9
  19.8 0.0 copy-start.4
  19.8 0.0 copy-start.5
  19.8 6.9 %all-to-all-start.1 = ((bf16[16,64,768]{2,1,0:T(8,128)(2,1)}), bf16[16,64,768]{2,1,0:T(8,128)(2,1)S(1)}, u32[]{:S(2)}, u32[]{:S(2)}) async-start(bf16[16,64,768]{2,1,0:T(8,128)(2,1)} %broadcast_in_dim.9), calls=%async_computation.1 | async-start | bytes 3145728 | tf_op jit(solution)/shard_map/all_to_all | solution.py:152
  26.7 0.0 reduce-scatter.2.cloned.1.call-start
  27.4 0.0 copy-done.4
  27.4 0.0 copy-done.5
  27.4 0.0 copy-start
  27.5 1.5 copy-done
  28.9 1.2 shard_map.73.dense
  30.2 0.1 pad_add_fusion.place
  30.2 16.6 %all-to-all-done.1 = bf16[16,64,768]{2,1,0:T(8,128)(2,1)S(1)} async-done(((bf16[16,64,768]{2,1,0:T(8,128)(2,1)}), bf16[16,64,768]{2,1,0:T(8,128)(2,1)S(1)}, u32[]{:S(2)}, u32[]{:S(2)}) %all-to-all-start.1) | async-done | bytes 1572896 | tf_op jit(solution)/shard_map/all_to_all | solution.py:152
  46.9 1.9 %shard_map.75 = (bf16[4,128,512]{2,1,0:T(8,128)(2,1)S(1)}, f32[4,128,512]{2,1,0:T(8,128)S(1)}) custom-call(s32[2]{0:T(128)S(1)} %pad_add_fusion.place, bf16[5,128,1024]{2,1,0:T(8,128)(2,1)S(1)} %shard_map.73.dense, bf16[1024,768]{1,0:T(8,128)(2,1)S(1)} %bitcast.15), custom_call_target="tpu_custom_call" | custom-call | tf_op jit(solution)/shard_map/pallas_call | solution.py:178
  48.8 0.0 copy-start.1
  48.8 0.0 copy-start.3
  48.8 6.3 %collective-permute-start = (bf16[4,128,512]{2,1,0:T(8,128)(2,1)S(1)}, bf16[4,128,512]{2,1,0:T(8,128)(2,1)S(1)}, u32[]{:S(2)}, u32[]{:S(2)}) collective-permute-start(bf16[4,128,512]{2,1,0:T(8,128)(2,1)S(1)} %get-tuple-element.17), channel_id=1, source_target_pairs={{0,1},{1,0},{2,3},{3,2},{4,5},{5,4},{6,7},{7,6},{8,9},{9,8},{10,11... | collective-permute-start | bytes 1572872 | tf_op jit(solution)/shard_map/ppermute | solution.py:160
  55.1 1.5 collective-permute-done.got
  56.6 0.9 shard_map.76.after
  57.5 0.0 reduce-scatter.2.cloned.1.call-update
  57.6 0.0 copy-done.1
  57.6 0.0 copy-done.3
  57.6 0.9 shard_map.77
  58.5 2.3 %collective-permute-start.1 = (bf16[4,32,128]{2,1,0:T(8,128)(2,1)S(1)}, bf16[4,32,128]{2,1,0:T(8,128)(2,1)S(1)}, u32[]{:S(2)}, u32[]{:S(2)}) collective-permute-start(bf16[4,32,128]{2,1,0:T(8,128)(2,1)S(1)} %get-tuple-element.20), channel_id=1, source_target_pairs={{0,1},{1,0},{2,3},{3,2},{4,5},{5,4},{6,7},{7,6},{8,9},{9,8},{10,11... | collective-permute-start | bytes 98312 | tf_op jit(solution)/shard_map/ppermute | solution.py:160
  60.8 0.8 collective-permute-done.1.got
  61.6 0.6 shard_map.78
  62.2 39.6 %all_to_all.26.got = bf16[16,32,256]{2,1,0:T(8,128)(2,1)S(1)} all-to-all(bf16[16,32,256]{2,1,0:T(8,128)(2,1)S(1)} %shard_map.78), channel_id=1, replica_groups=mesh['y'=4,'x'=4,'zl'=4,'zh'=4,'core'=2] {'zh','zl'}, dimensions={0} | all-to-all | bytes 524288 | tf_op jit(solution)/shard_map/all_to_all | solution.py:152
  101.7 0.6 shard_map.79
  102.3 1.4 broadcast_in_dim.10
  103.7 3.7 %all-to-all-start.3 = ((bf16[16,48,1024]{2,1,0:T(8,128)(2,1)}), bf16[16,48,1024]{2,1,0:T(8,128)(2,1)S(1)}, u32[]{:S(2)}, u32[]{:S(2)}) async-start(bf16[16,48,1024]{2,1,0:T(8,128)(2,1)} %broadcast_in_dim.10), calls=%async_computation.4 | async-start | bytes 3145728 | tf_op jit(solution)/shard_map/all_to_all | solution.py:152
  107.4 4.4 %reduce-scatter.2.cloned.1.call-done.sums = bf16[128,512]{1,0:T(8,128)(2,1)} async-done(((bf16[512,512]{1,0:T(8,128)(2,1)}), bf16[128,512]{1,0:T(8,128)(2,1)}) %reduce-scatter.2.cloned.1.call-update) | async-done | bytes 131088 | tf_op jit(solution)/shard_map/reduce_scatter | solution.py:185
  111.8 0.0 copy-start.6
  111.8 0.9 copy-done.6
  112.7 0.4 shard_map.80.msgs
  113.1 13.0 %all-to-all-done.3 = bf16[16,48,1024]{2,1,0:T(8,128)(2,1)S(1)} async-done(((bf16[16,48,1024]{2,1,0:T(8,128)(2,1)}), bf16[16,48,1024]{2,1,0:T(8,128)(2,1)S(1)}, u32[]{:S(2)}, u32[]{:S(2)}) %all-to-all-start.3) | async-done | bytes 1572896 | tf_op jit(solution)/shard_map/all_to_all | solution.py:152
  126.1 1.0 shard_map.81
  127.1 8.2 %collective-permute-start.2 = (bf16[4,16,1024]{2,1,0:T(8,128)(2,1)S(1)}, bf16[4,16,1024]{2,1,0:T(8,128)(2,1)S(1)}, u32[]{:S(2)}, u32[]{:S(2)}) collective-permute-start(bf16[4,16,1024]{2,1,0:T(8,128)(2,1)S(1)} %get-tuple-element.24), channel_id=1, source_target_pairs={{0,1},{1,0},{2,3},{3,2},{4,5},{5,4},{6,7},{7,6},{8,9},{9,8},{10,11... | collective-permute-start | bytes 393224 | tf_op jit(solution)/shard_map/ppermute | solution.py:160
  135.3 1.0 collective-permute-done.2.got
  136.3 21.3 %all_to_all.27.got = bf16[4,16,1024]{2,1,0:T(8,128)(2,1)S(1)} all-to-all(bf16[4,16,1024]{2,1,0:T(8,128)(2,1)S(1)} %shard_map.82), channel_id=1, replica_groups=mesh['y'=4,'x'=4,'zl'=4,'zh'=4,'core'=2] {'zh'}, dimensions={0} | all-to-all | bytes 262144 | tf_op jit(solution)/shard_map/all_to_all | solution.py:152
  157.6 0.6 shard_map.83
  (1 shorter events, 0.0 us)
Async XLA Ops:
  6.5 0.7 copy-start.2
  19.8 7.6 %copy-start.4 = (s32[1,1,56]{2,1,0:T(1,128)S(1)}, s32[1,1,56]{2,1,0:T(1,128)}, u32[]{:S(2)}) copy-start(s32[1,1,56]{2,1,0:T(1,128)} %param.11) | copy-start | bytes 676
  19.8 7.6 %copy-start.5 = (s32[1,1,56]{2,1,0:T(1,128)S(1)}, s32[1,1,56]{2,1,0:T(1,128)}, u32[]{:S(2)}) copy-start(s32[1,1,56]{2,1,0:T(1,128)} %param.12) | copy-start | bytes 676
  19.8 27.1 %all-to-all-start.1 = ((bf16[16,64,768]{2,1,0:T(8,128)(2,1)}), bf16[16,64,768]{2,1,0:T(8,128)(2,1)S(1)}, u32[]{:S(2)}, u32[]{:S(2)}) async-start(bf16[16,64,768]{2,1,0:T(8,128)(2,1)} %broadcast_in_dim.9), calls=%async_computation.1 | async-start | bytes 3145728 | tf_op jit(solution)/shard_map/all_to_all | solution.py:152
  26.7 85.1 %reduce-scatter.2.cloned.1.call-start = ((), (), s32[]{:S(2)}) async-start(), calls=%async_computation.6 | async-start | bytes 655360 | tf_op jit(solution)/shard_map/reduce_scatter | solution.py:185
  27.4 1.5 copy-start
  48.8 8.8 %copy-start.1 = (bf16[30,12,128]{2,0,1:T(8,128)(2,1)S(1)}, bf16[30,12,128]{2,0,1:T(8,128)(2,1)}, u32[]{:S(2)}) copy-start(bf16[30,12,128]{2,0,1:T(8,128)(2,1)} %param.8) | copy-start | bytes 276484
  48.8 8.8 %copy-start.3 = (f32[6,30]{1,0:T(8,128)S(1)}, f32[6,30]{1,0:T(8,128)}, u32[]{:S(2)}) copy-start(f32[6,30]{1,0:T(8,128)} %coef.1) | copy-start | bytes 2164
  48.8 7.8 %collective-permute-start = (bf16[4,128,512]{2,1,0:T(8,128)(2,1)S(1)}, bf16[4,128,512]{2,1,0:T(8,128)(2,1)S(1)}, u32[]{:S(2)}, u32[]{:S(2)}) collective-permute-start(bf16[4,128,512]{2,1,0:T(8,128)(2,1)S(1)} %get-tuple-element.17), channel_id=1, source_target_pairs={{0,1},{1,0},{2,3},{3,2},{4,5},{5,4},{6,7},{7,6},{8,9},{9,8},{10,11... | collective-permute-start | bytes 1572872 | tf_op jit(solution)/shard_map/ppermute | solution.py:160
  58.5 3.1 %collective-permute-start.1 = (bf16[4,32,128]{2,1,0:T(8,128)(2,1)S(1)}, bf16[4,32,128]{2,1,0:T(8,128)(2,1)S(1)}, u32[]{:S(2)}, u32[]{:S(2)}) collective-permute-start(bf16[4,32,128]{2,1,0:T(8,128)(2,1)S(1)} %get-tuple-element.20), channel_id=1, source_target_pairs={{0,1},{1,0},{2,3},{3,2},{4,5},{5,4},{6,7},{7,6},{8,9},{9,8},{10,11... | collective-permute-start | bytes 98312 | tf_op jit(solution)/shard_map/ppermute | solution.py:160
  103.7 22.5 %all-to-all-start.3 = ((bf16[16,48,1024]{2,1,0:T(8,128)(2,1)}), bf16[16,48,1024]{2,1,0:T(8,128)(2,1)S(1)}, u32[]{:S(2)}, u32[]{:S(2)}) async-start(bf16[16,48,1024]{2,1,0:T(8,128)(2,1)} %broadcast_in_dim.10), calls=%async_computation.4 | async-start | bytes 3145728 | tf_op jit(solution)/shard_map/all_to_all | solution.py:152
  111.8 0.9 copy-start.6
  127.1 9.2 %collective-permute-start.2 = (bf16[4,16,1024]{2,1,0:T(8,128)(2,1)S(1)}, bf16[4,16,1024]{2,1,0:T(8,128)(2,1)S(1)}, u32[]{:S(2)}, u32[]{:S(2)}) collective-permute-start(bf16[4,16,1024]{2,1,0:T(8,128)(2,1)S(1)} %get-tuple-element.24), channel_id=1, source_target_pairs={{0,1},{1,0},{2,3},{3,2},{4,5},{5,4},{6,7},{7,6},{8,9},{9,8},{10,11... | collective-permute-start | bytes 393224 | tf_op jit(solution)/shard_map/ppermute | solution.py:160
Sparse Core Ops, SparseCore 0:
  57.7 54.0 reduce-scatter.1

commit v5 on v4

v5 whole, which is shorter than its diff:
```python
import jax
import jax.numpy as jnp
from jax import lax
from jax.experimental import pallas as pl
from jax.experimental.pallas import tpu as pltpu
from jax.sharding import Mesh
from jax.sharding import PartitionSpec as P

BF = jnp.bfloat16
F32 = jnp.float32
NODE = ("y", "x", "zl")
REL = ("zh", "core")
YX = ("y", "x")
VMEM = pl.BlockSpec(memory_space=pltpu.VMEM)
ANY = pl.BlockSpec(memory_space=pl.ANY)
SMEM = pl.BlockSpec(memory_space=pltpu.SMEM)
PARAMS = pltpu.CompilerParams(vmem_limit_bytes=16 * 1024 * 1024)

RELS = 5
DIN = 768
DOUT = 1024
TILE = 128
SRC = 8
ROWS = 16
NODES = 64
PER = 12
SLOT = 8
SELF = 2
CHUNK = SLOT * NODES
WEIGHT = 10**11


def call(body, outs, ins, scratch=(), cost=None):
    return pl.pallas_call(
        body,
        cost_estimate=cost,
        out_shape=outs,
        in_specs=ins,
        out_specs=jax.tree.map(lambda _: VMEM, outs),
        scratch_shapes=list(scratch),
        compiler_params=PARAMS,
    )


def shape(kind, *dims):
    return jax.ShapeDtypeStruct(dims, kind)


def start(own, coef, bases, padded, copies, rows):
    src = lax.broadcasted_iota(jnp.int32, (DIN, DIN), 0)
    out = lax.broadcasted_iota(jnp.int32, (DIN, DIN), 1)
    swap = jnp.where(src == PER * (out & (NODES - 1)) + (out >> 6), 1.0, 0.0).astype(BF)
    value = jnp.dot(own[...], swap, preferred_element_type=F32).astype(BF)
    padded[:, :DIN] = value
    padded[:, DIN:] = jnp.zeros((ROWS, 8 * TILE - DIN), BF)
    rows[...] = jnp.zeros_like(rows)
    for d in range(PER):
        part = jnp.dot(
            coef[...], bases[d].astype(F32), precision=lax.Precision.HIGHEST, preferred_element_type=F32
        )
        for r in range(RELS):
            j = r * PER + d
            rows[j // SLOT, j % SLOT : j % SLOT + 1] = part[r : r + 1]
        rows[d // SELF, SLOT + d % SELF : SLOT + d % SELF + 1] = part[RELS :]
    for i in range(4):
        copies[i, :, :DIN] = value
        for k in range(8):
            copies[i, :, DIN + k * TILE : DIN + (k + 1) * TILE] = rows[k].astype(BF)


def sort(place, padded, gathered, send, keep):
    core = place[1]

    def fill(ref, z, k):
        ref[z, :ROWS] = padded[:, pl.ds(pl.multiple_of(k * TILE, TILE), TILE)]
        spot = pl.ds(pl.multiple_of(DIN + k * TILE, TILE), TILE)
        rows = [gathered[i, :, spot].astype(F32)[:PER] for i in range(4)]
        ref[z, ROWS:] = jnp.concatenate(rows, axis=0).astype(BF)

    for z in range(4):
        fill(keep, z, 2 * z + core)
        fill(send, z, 2 * z + 1 - core)


def join_cores(place, keep, got, send, mine, relay):
    zh, core = place[0], place[1]
    for e, ref in ((1, send.at[0]), (2, send.at[1]), (0, mine), (3, relay)):
        z = zh ^ e
        ref[core] = keep[z]
        ref[1 - core] = got[z]


def pass_on(relay, got, send):
    send[0] = relay[...]
    send[1] = got[1]


def join_groups(place, mine, first, second, own, rows):
    for e, ref in ((0, mine), (1, first.at[0]), (3, second.at[0]), (2, second.at[1])):
        z = place[0] ^ e
        for c in range(2):
            g = 2 * z + c
            own[g] = ref[c, :ROWS]
            rows[:, pl.ds(pl.multiple_of(g * TILE, TILE), TILE)] = ref[c, ROWS:]


def densify(count, source, relation, values, dense, acc):
    acc[...] = jnp.zeros_like(acc)

    def add(t, _):
        spot = relation[t] * SRC + source[t]
        acc[spot] = acc[spot] + values[t].astype(F32)
        return 0

    lax.fori_loop(0, count[0], add, 0)
    for r in range(RELS):
        for s in range(SRC):
            dense[r, :, s * TILE : (s + 1) * TILE] = acc[r * SRC + s].astype(BF)


def aggregate(place, dense, feats, after, send, keep, full):
    for r in range(RELS):
        full[:, r * DIN : (r + 1) * DIN] = jnp.dot(dense[r], feats[...], preferred_element_type=F32)
    full[:, RELS * DIN :] = jnp.zeros((TILE, 8 * CHUNK - RELS * DIN), F32)
    core = place[1]
    for z in range(4):
        keep[z] = full[:, pl.ds(pl.multiple_of((2 * z + core) * CHUNK, CHUNK), CHUNK)]
        send[z] = full[:, pl.ds(pl.multiple_of((2 * z + 1 - core) * CHUNK, CHUNK), CHUNK)].astype(BF)


def arrange(sums, own, msgs):
    src = lax.broadcasted_iota(jnp.int32, (CHUNK + TILE, DIN), 0)
    out = lax.broadcasted_iota(jnp.int32, (CHUNK + TILE, DIN), 1)
    swap = jnp.where(out == PER * (src & (NODES - 1)) + (src >> 6), 1.0, 0.0).astype(BF)
    value = jnp.concatenate([sums[...], own[...]], axis=1)
    msgs[...] = jnp.dot(value, swap, preferred_element_type=F32).astype(BF)


def transform(place, msgs, weights, send, keep, part):
    core = place[1]
    part[...] = jnp.dot(msgs[...], weights[...], preferred_element_type=F32)
    for z in range(4):
        keep[z] = part[pl.ds(pl.multiple_of((2 * z + core) * ROWS, ROWS), ROWS)]
        send[z] = part[pl.ds(pl.multiple_of((2 * z + 1 - core) * ROWS, ROWS), ROWS)].astype(BF)


def pair_sum(keep, got, out):
    out[...] = (keep[...] + got[...].astype(F32)).astype(BF)


def finish(got, out):
    total = got[0].astype(F32)
    for i in range(1, 4):
        total = total + got[i].astype(F32)
    out[...] = jnp.maximum(total, 0.0).astype(BF)


def exchange(x, axis):
    return lax.all_to_all(x, axis, split_axis=0, concat_axis=0, tiled=True)


def spread(x, axis):
    return exchange(jnp.broadcast_to(x, (lax.axis_size(axis), *x.shape)), axis)


def partner(x, axis, mask):
    return lax.ppermute(x, axis, [(i, i ^ mask) for i in range(lax.axis_size(axis))])


def on_device(features, bases, coefficients, tile_values, tile_source, tile_relation, tile_count):
    place = jnp.stack([lax.axis_index(a) for a in REL]).astype(jnp.int32)
    padded, copies = call(
        start,
        (shape(BF, ROWS, 8 * TILE), shape(BF, 4, ROWS, DIN + 8 * TILE)),
        [VMEM] * 3,
        [pltpu.VMEM((8, ROWS, TILE), F32)],
    )(features[0], coefficients, jnp.swapaxes(bases, 0, 1))
    gathered = exchange(copies, "zl")
    dense = call(
        densify,
        shape(BF, RELS, TILE, SRC * TILE),
        [SMEM, SMEM, SMEM, VMEM],
        [pltpu.VMEM((RELS * SRC, TILE, TILE), F32)],
        pl.CostEstimate(flops=1 << 20, bytes_accessed=1 << 23, transcendentals=0),
    )(tile_count[0], tile_source[0, 0], tile_relation[0, 0], tile_values[0, 0])
    feats = spread(gathered[:, :, :DIN].reshape(NODES, DIN), YX).reshape(SRC * TILE, DIN)

    parcel = shape(BF, 4, ROWS + 4 * PER, TILE)
    send, keep = call(sort, (parcel, parcel), [SMEM, VMEM, VMEM])(place, padded, gathered)
    block = shape(BF, 2, ROWS + 4 * PER, TILE)
    blocks = shape(BF, 2, 2, ROWS + 4 * PER, TILE)
    send, mine, relay = call(join_cores, (blocks, block, block), [SMEM, VMEM, VMEM])(
        place, keep, partner(send, "core", 1)
    )
    first = partner(send, "zh", 1)
    relay = call(pass_on, blocks, [VMEM] * 2)(relay, first)
    second = partner(relay, "zh", 3)
    own, rows = call(
        join_groups,
        (shape(BF, 8, ROWS, TILE), shape(BF, 4 * PER, DOUT)),
        [SMEM] + [VMEM] * 3,
    )(place, mine, first, second)

    send, keep = call(
        aggregate,
        (shape(BF, 4, TILE, CHUNK), shape(F32, 4, TILE, CHUNK)),
        [SMEM, VMEM, VMEM, ANY],
        [pltpu.VMEM((TILE, 8 * CHUNK), F32)],
    )(place, dense, feats, relay)
    pair = call(pair_sum, shape(BF, 4, TILE, CHUNK), [VMEM] * 2)(keep, partner(send, "core", 1))
    sums = lax.psum_scatter(pair.reshape(4 * TILE, CHUNK), "zh", scatter_dimension=0, tiled=True)
    weights = spread(rows, YX).reshape(NODES * PER, DOUT)
    msgs = call(
        arrange,
        shape(BF, TILE, DIN),
        [VMEM] * 2,
        cost=pl.CostEstimate(flops=WEIGHT, bytes_accessed=1 << 20, transcendentals=0),
    )(sums, own.reshape(TILE, TILE))
    send, keep = call(
        transform,
        (shape(BF, 4, ROWS, DOUT), shape(F32, 4, ROWS, DOUT)),
        [SMEM] + [VMEM] * 2,
        [pltpu.VMEM((TILE, DOUT), F32)],
    )(place, msgs, weights)
    pair = call(pair_sum, shape(BF, 4, ROWS, DOUT), [VMEM] * 2)(keep, partner(send, "core", 1))
    return call(finish, shape(BF, ROWS, DOUT), [VMEM])(exchange(pair, "zh"))[None]


def solution(mesh):
    split = Mesh(mesh.devices.reshape(4, 4, 4, 4, 2), NODE + REL)
    return jax.shard_map(
        on_device,
        mesh=split,
        in_specs=(
            P(REL, NODE, None),
            P(None, NODE, REL),
            P(),
            P(NODE, REL, None, None, None),
            P(NODE, REL, None),
            P(NODE, REL, None),
            P(NODE, REL),
        ),
        out_specs=P(REL, NODE, None),
        check_vma=False,
    )
```

time: 167 us -> 141 us (0.84)
  the two profiles are of different devices: /device:TPU:1 before, /device:TPU:96 now
where the time goes in v5:
time: 141 us
  waiting for transfers between devices  41.1 us (29%)
  starting transfers between devices  35 us (25%)
  blocking collectives  34.7 us (25%)
  between operations  14.2 us (10%)
  Pallas kernels  8.15 us (6%)
  local copies, waits for them, and re-layouts  7.41 us (5%)
    all_to_all x2, blocking collectives, exchange(): return lax.all_to_all(x, axis, split_axis=0, concat_axis=0, tiled=True)  34.7 us
    ppermute x5, starting transfers between devices, partner(): lax.ppermute(x, axis, [(i, i ^ mask) for i in range(lax.axis_size(axis))])  24.9 us
    reduce_scatter x1, waiting for transfers between devices, on_device(): lax.psum_scatter(pair.reshape(4 * TILE, CHUNK), 'zh', scatter_dimension=0...  20.1 us
    ppermute x5, waiting for transfers between devices, partner(): lax.ppermute(x, axis, [(i, i ^ mask) for i in range(lax.axis_size(axis))])  12.1 us
    all_to_all x2, starting transfers between devices, exchange(): return lax.all_to_all(x, axis, split_axis=0, concat_axis=0, tiled=True)  10.1 us
    all_to_all x2, waiting for transfers between devices, exchange(): return lax.all_to_all(x, axis, split_axis=0, concat_axis=0, tiled=True)  8.89 us
    unnamed x14, local copies, waits for them, and re-layouts  4.72 us
  transfers between devices with their start and end apart: 8, of which 8 were waited for; matrix products, arithmetic and copies ran while one was open for 1% of the time, Pallas kernels for 2%

profile of v5, /device:TPU:96, one launch (start us, length us, event | category | flops | bytes accessed | tf_op | source)
XLA Modules:
  0.0 140.5 jit_solution(1112734945327750613)
XLA Ops:
  6.5 0.0 copy-start.1
  6.5 0.9 copy-done.1
  7.4 0.0 copy-start.2
  7.4 0.7 copy-done.2
  8.2 0.0 copy-start.3
  8.2 0.7 copy-done.3
  8.9 0.5 shard_map.74
  9.4 11.5 %all_to_all.20.gathered = bf16[4,16,1792]{2,1,0:T(8,128)(2,1)S(1)} all-to-all(bf16[4,16,1792]{2,1,0:T(8,128)(2,1)S(1)} %get-tuple-element.18), channel_id=1, replica_groups=mesh['y'=4,'x'=4,'zl'=4,'zh'=4,'core'=2] {'zl'}, dimensions={0} | all-to-all | bytes 458752 | tf_op jit(solution)/shard_map/all_to_all | solution.py:159
  20.9 1.3 broadcast_in_dim.9
  22.2 0.0 copy-start.4
  22.2 0.0 copy-start.5
  22.2 6.3 %all-to-all-start.1 = ((bf16[16,64,768]{2,1,0:T(8,128)(2,1)}), bf16[16,64,768]{2,1,0:T(8,128)(2,1)S(1)}, u32[]{:S(2)}, u32[]{:S(2)}) async-start(bf16[16,64,768]{2,1,0:T(8,128)(2,1)} %broadcast_in_dim.9), calls=%async_computation.1 | async-start | bytes 3145728 | tf_op jit(solution)/shard_map/all_to_all | solution.py:159
  28.6 0.0 reduce-scatter.2.cloned.1.call-start
  28.6 0.1 pad_add_fusion.place
  28.7 0.6 shard_map.75
  29.3 1.9 %collective-permute-start = (bf16[4,64,128]{2,1,0:T(8,128)(2,1)S(1)}, bf16[4,64,128]{2,1,0:T(8,128)(2,1)S(1)}, u32[]{:S(2)}, u32[]{:S(2)}) collective-permute-start(bf16[4,64,128]{2,1,0:T(8,128)(2,1)S(1)} %get-tuple-element.21), channel_id=1, source_target_pairs={{0,1},{1,0},{2,3},{3,2},{4,5},{5,4},{6,7},{7,6},{8,9},{9,8},{10,11... | collective-permute-start | bytes 196616 | tf_op jit(solution)/shard_map/ppermute | solution.py:167
  31.2 1.2 collective-permute-done.got
  32.4 0.6 shard_map.76
  33.0 9.1 %collective-permute-start.1 = (bf16[2,2,64,128]{3,2,1,0:T(8,128)(2,1)S(1)}, bf16[2,2,64,128]{3,2,1,0:T(8,128)(2,1)S(1)}, u32[]{:S(2)}, u32[]{:S(2)}) collective-permute-start(bf16[2,2,64,128]{3,2,1,0:T(8,128)(2,1)S(1)} %get-tuple-element.23), channel_id=1, source_target_pairs={{0,2},{2,0},{4,6},{6,4},{1,3},{3,1},{5,7},{7,5},{8,10},{10,8},{12,... | collective-permute-start | bytes 196616 | tf_op jit(solution)/shard_map/ppermute | solution.py:167
  42.8 0.0 copy-done.4
  42.8 0.0 copy-done.5
  42.8 0.0 copy-start
  42.8 1.5 %copy-done = bf16[1,1,56,128,128]{4,3,2,1,0:T(8,128)(2,1)S(1)} copy-done((bf16[1,1,56,128,128]{4,3,2,1,0:T(8,128)(2,1)S(1)}, bf16[1,1,56,128,128]{4,3,2,1,0:T(8,128)(2,1)}, u32[]{:S(2)}) %copy-start) | copy-done | bytes 1835032
  44.3 1.2 shard_map.73.dense
  45.5 2.2 %collective-permute-done.1.got.first = bf16[2,2,64,128]{3,2,1,0:T(8,128)(2,1)S(1)} collective-permute-done((bf16[2,2,64,128]{3,2,1,0:T(8,128)(2,1)S(1)}, bf16[2,2,64,128]{3,2,1,0:T(8,128)(2,1)S(1)}, u32[]{:S(2)}, u32[]{:S(2)}) %collective-permute-start.1) | collective-permute-done | bytes 65568 | tf_op jit(solution)/shard_map/ppermute | solution.py:167
  47.7 4.6 %all-to-all-done.1 = bf16[16,64,768]{2,1,0:T(8,128)(2,1)S(1)} async-done(((bf16[16,64,768]{2,1,0:T(8,128)(2,1)}), bf16[16,64,768]{2,1,0:T(8,128)(2,1)S(1)}, u32[]{:S(2)}, u32[]{:S(2)}) %all-to-all-start.1) | async-done | bytes 1572896 | tf_op jit(solution)/shard_map/all_to_all | solution.py:159
  52.3 1.9 %shard_map.78 = (bf16[4,128,512]{2,1,0:T(8,128)(2,1)S(1)}, f32[4,128,512]{2,1,0:T(8,128)S(1)}) custom-call(s32[2]{0:T(128)S(1)} %pad_add_fusion.place, bf16[5,128,1024]{2,1,0:T(8,128)(2,1)S(1)} %shard_map.73.dense, bf16[1024,768]{1,0:T(8,128)(2,1)S(1)} %bitcast.15, bf16[2,2,64,128]{3,2,1,0:T(8,128)(2,1)S(1)} %shard_map.77.after), custom_call_target="tpu_custom_call" | custom-call | tf_op jit(solution)/shard_map/pallas_call | solution.py:204
  54.2 1.9 %collective-permute-start.2 = (bf16[4,128,512]{2,1,0:T(8,128)(2,1)S(1)}, bf16[4,128,512]{2,1,0:T(8,128)(2,1)S(1)}, u32[]{:S(2)}, u32[]{:S(2)}) collective-permute-start(bf16[4,128,512]{2,1,0:T(8,128)(2,1)S(1)} %get-tuple-element.25), channel_id=1, source_target_pairs={{0,1},{1,0},{2,3},{3,2},{4,5},{5,4},{6,7},{7,6},{8,9},{9,8},{10,11... | collective-permute-start | bytes 1572872 | tf_op jit(solution)/shard_map/ppermute | solution.py:167
  56.1 1.9 %collective-permute-done.2.got = bf16[4,128,512]{2,1,0:T(8,128)(2,1)S(1)} collective-permute-done((bf16[4,128,512]{2,1,0:T(8,128)(2,1)S(1)}, bf16[4,128,512]{2,1,0:T(8,128)(2,1)S(1)}, u32[]{:S(2)}, u32[]{:S(2)}) %collective-permute-start.2) | collective-permute-done | bytes 524320 | tf_op jit(solution)/shard_map/ppermute | solution.py:167
  58.0 0.9 shard_map.79
  58.9 0.0 reduce-scatter.2.cloned.1.call-update
  58.9 10.0 %collective-permute-start.3 = (bf16[2,2,64,128]{3,2,1,0:T(8,128)(2,1)S(1)}, bf16[2,2,64,128]{3,2,1,0:T(8,128)(2,1)S(1)}, u32[]{:S(2)}, u32[]{:S(2)}) collective-permute-start(bf16[2,2,64,128]{3,2,1,0:T(8,128)(2,1)S(1)} %shard_map.77.after), channel_id=1, source_target_pairs={{0,6},{2,4},{4,2},{6,0},{1,7},{3,5},{5,3},{7,1},{8,14},{10,12},{12... | collective-permute-start | bytes 196616 | tf_op jit(solution)/shard_map/ppermute | solution.py:167
  69.0 5.4 %collective-permute-done.3.second = bf16[2,2,64,128]{3,2,1,0:T(8,128)(2,1)S(1)} collective-permute-done((bf16[2,2,64,128]{3,2,1,0:T(8,128)(2,1)S(1)}, bf16[2,2,64,128]{3,2,1,0:T(8,128)(2,1)S(1)}, u32[]{:S(2)}, u32[]{:S(2)}) %collective-permute-start.3) | collective-permute-done | bytes 65568 | tf_op jit(solution)/shard_map/ppermute | solution.py:167
  74.4 0.6 shard_map.80
  75.0 1.4 broadcast_in_dim.10
  76.3 3.7 %all-to-all-start.2 = ((bf16[16,48,1024]{2,1,0:T(8,128)(2,1)}), bf16[16,48,1024]{2,1,0:T(8,128)(2,1)S(1)}, u32[]{:S(2)}, u32[]{:S(2)}) async-start(bf16[16,48,1024]{2,1,0:T(8,128)(2,1)} %broadcast_in_dim.10), calls=%async_computation.3 | async-start | bytes 3145728 | tf_op jit(solution)/shard_map/all_to_all | solution.py:159
  80.1 20.1 %reduce-scatter.2.cloned.1.call-done.sums = bf16[128,512]{1,0:T(8,128)(2,1)} async-done(((bf16[512,512]{1,0:T(8,128)(2,1)}), bf16[128,512]{1,0:T(8,128)(2,1)}) %reduce-scatter.2.cloned.1.call-update) | async-done | bytes 131088 | tf_op jit(solution)/shard_map/reduce_scatter | solution.py:211
  100.1 0.0 copy-start.6
  100.1 0.9 copy-done.6
  101.0 0.4 shard_map.81.msgs
  101.4 4.3 %all-to-all-done.2 = bf16[16,48,1024]{2,1,0:T(8,128)(2,1)S(1)} async-done(((bf16[16,48,1024]{2,1,0:T(8,128)(2,1)}), bf16[16,48,1024]{2,1,0:T(8,128)(2,1)S(1)}, u32[]{:S(2)}, u32[]{:S(2)}) %all-to-all-start.2) | async-done | bytes 1572896 | tf_op jit(solution)/shard_map/all_to_all | solution.py:159
  105.7 1.0 shard_map.82
  106.7 1.9 %collective-permute-start.4 = (bf16[4,16,1024]{2,1,0:T(8,128)(2,1)S(1)}, bf16[4,16,1024]{2,1,0:T(8,128)(2,1)S(1)}, u32[]{:S(2)}, u32[]{:S(2)}) collective-permute-start(bf16[4,16,1024]{2,1,0:T(8,128)(2,1)S(1)} %get-tuple-element.30), channel_id=1, source_target_pairs={{0,1},{1,0},{2,3},{3,2},{4,5},{5,4},{6,7},{7,6},{8,9},{9,8},{10,11... | collective-permute-start | bytes 393224 | tf_op jit(solution)/shard_map/ppermute | solution.py:167
  108.6 1.3 collective-permute-done.4.got
  109.9 23.1 %all_to_all.21.got = bf16[4,16,1024]{2,1,0:T(8,128)(2,1)S(1)} all-to-all(bf16[4,16,1024]{2,1,0:T(8,128)(2,1)S(1)} %shard_map.83), channel_id=1, replica_groups=mesh['y'=4,'x'=4,'zl'=4,'zh'=4,'core'=2] {'zh'}, dimensions={0} | all-to-all | bytes 262144 | tf_op jit(solution)/shard_map/all_to_all | solution.py:159
  133.1 0.6 shard_map.84
  (3 shorter events, 0.0 us)
Async XLA Ops:
  6.5 0.9 copy-start.1
  7.4 0.7 copy-start.2
  8.2 0.7 copy-start.3
  22.2 20.5 %copy-start.4 = (s32[1,1,56]{2,1,0:T(1,128)S(1)}, s32[1,1,56]{2,1,0:T(1,128)}, u32[]{:S(2)}) copy-start(s32[1,1,56]{2,1,0:T(1,128)} %param.11) | copy-start | bytes 676
  22.2 20.5 %copy-start.5 = (s32[1,1,56]{2,1,0:T(1,128)S(1)}, s32[1,1,56]{2,1,0:T(1,128)}, u32[]{:S(2)}) copy-start(s32[1,1,56]{2,1,0:T(1,128)} %param.12) | copy-start | bytes 676
  22.2 30.1 %all-to-all-start.1 = ((bf16[16,64,768]{2,1,0:T(8,128)(2,1)}), bf16[16,64,768]{2,1,0:T(8,128)(2,1)S(1)}, u32[]{:S(2)}, u32[]{:S(2)}) async-start(bf16[16,64,768]{2,1,0:T(8,128)(2,1)} %broadcast_in_dim.9), calls=%async_computation.1 | async-start | bytes 3145728 | tf_op jit(solution)/shard_map/all_to_all | solution.py:159
  28.6 71.5 %reduce-scatter.2.cloned.1.call-start = ((), (), s32[]{:S(2)}) async-start(), calls=%async_computation.5 | async-start | bytes 655360 | tf_op jit(solution)/shard_map/reduce_scatter | solution.py:211
  29.3 3.1 %collective-permute-start = (bf16[4,64,128]{2,1,0:T(8,128)(2,1)S(1)}, bf16[4,64,128]{2,1,0:T(8,128)(2,1)S(1)}, u32[]{:S(2)}, u32[]{:S(2)}) collective-permute-start(bf16[4,64,128]{2,1,0:T(8,128)(2,1)S(1)} %get-tuple-element.21), channel_id=1, source_target_pairs={{0,1},{1,0},{2,3},{3,2},{4,5},{5,4},{6,7},{7,6},{8,9},{9,8},{10,11... | collective-permute-start | bytes 196616 | tf_op jit(solution)/shard_map/ppermute | solution.py:167
  33.0 14.7 %collective-permute-start.1 = (bf16[2,2,64,128]{3,2,1,0:T(8,128)(2,1)S(1)}, bf16[2,2,64,128]{3,2,1,0:T(8,128)(2,1)S(1)}, u32[]{:S(2)}, u32[]{:S(2)}) collective-permute-start(bf16[2,2,64,128]{3,2,1,0:T(8,128)(2,1)S(1)} %get-tuple-element.23), channel_id=1, source_target_pairs={{0,2},{2,0},{4,6},{6,4},{1,3},{3,1},{5,7},{7,5},{8,10},{10,8},{12,... | collective-permute-start | bytes 196616 | tf_op jit(solution)/shard_map/ppermute | solution.py:167
  42.8 1.5 %copy-start = (bf16[1,1,56,128,128]{4,3,2,1,0:T(8,128)(2,1)S(1)}, bf16[1,1,56,128,128]{4,3,2,1,0:T(8,128)(2,1)}, u32[]{:S(2)}) copy-start(bf16[1,1,56,128,128]{4,3,2,1,0:T(8,128)(2,1)} %param.10) | copy-start | bytes 5505028
  54.2 3.8 %collective-permute-start.2 = (bf16[4,128,512]{2,1,0:T(8,128)(2,1)S(1)}, bf16[4,128,512]{2,1,0:T(8,128)(2,1)S(1)}, u32[]{:S(2)}, u32[]{:S(2)}) collective-permute-start(bf16[4,128,512]{2,1,0:T(8,128)(2,1)S(1)} %get-tuple-element.25), channel_id=1, source_target_pairs={{0,1},{1,0},{2,3},{3,2},{4,5},{5,4},{6,7},{7,6},{8,9},{9,8},{10,11... | collective-permute-start | bytes 1572872 | tf_op jit(solution)/shard_map/ppermute | solution.py:167
  58.9 15.5 %collective-permute-start.3 = (bf16[2,2,64,128]{3,2,1,0:T(8,128)(2,1)S(1)}, bf16[2,2,64,128]{3,2,1,0:T(8,128)(2,1)S(1)}, u32[]{:S(2)}, u32[]{:S(2)}) collective-permute-start(bf16[2,2,64,128]{3,2,1,0:T(8,128)(2,1)S(1)} %shard_map.77.after), channel_id=1, source_target_pairs={{0,6},{2,4},{4,2},{6,0},{1,7},{3,5},{5,3},{7,1},{8,14},{10,12},{12... | collective-permute-start | bytes 196616 | tf_op jit(solution)/shard_map/ppermute | solution.py:167
  76.3 29.4 %all-to-all-start.2 = ((bf16[16,48,1024]{2,1,0:T(8,128)(2,1)}), bf16[16,48,1024]{2,1,0:T(8,128)(2,1)S(1)}, u32[]{:S(2)}, u32[]{:S(2)}) async-start(bf16[16,48,1024]{2,1,0:T(8,128)(2,1)} %broadcast_in_dim.10), calls=%async_computation.3 | async-start | bytes 3145728 | tf_op jit(solution)/shard_map/all_to_all | solution.py:159
  100.1 0.9 copy-start.6
  106.7 3.2 %collective-permute-start.4 = (bf16[4,16,1024]{2,1,0:T(8,128)(2,1)S(1)}, bf16[4,16,1024]{2,1,0:T(8,128)(2,1)S(1)}, u32[]{:S(2)}, u32[]{:S(2)}) collective-permute-start(bf16[4,16,1024]{2,1,0:T(8,128)(2,1)S(1)} %get-tuple-element.30), channel_id=1, source_target_pairs={{0,1},{1,0},{2,3},{3,2},{4,5},{5,4},{6,7},{7,6},{8,9},{9,8},{10,11... | collective-permute-start | bytes 393224 | tf_op jit(solution)/shard_map/ppermute | solution.py:167
Sparse Core Ops, SparseCore 0:
  59.0 41.0 reduce-scatter.1

commit v6 on v5

--- a/solution.py
+++ b/solution.py
@@ -1,3 +1,5 @@
+import functools
+
 import jax
 import jax.numpy as jnp
 from jax import lax
@@ -13,6 +15,7 @@
 YX = ("y", "x")
 VMEM = pl.BlockSpec(memory_space=pltpu.VMEM)
 ANY = pl.BlockSpec(memory_space=pl.ANY)
+HBM = pl.BlockSpec(memory_space=pltpu.HBM)
 SMEM = pl.BlockSpec(memory_space=pltpu.SMEM)
 PARAMS = pltpu.CompilerParams(vmem_limit_bytes=16 * 1024 * 1024)
 
@@ -27,6 +30,8 @@
 SLOT = 8
 SELF = 2
 CHUNK = SLOT * NODES
+HALF = TILE // 2
+PIECE = 256
 WEIGHT = 10**11
 
 
@@ -46,10 +51,18 @@
     return jax.ShapeDtypeStruct(dims, kind)
 
 
-def start(own, coef, bases, padded, copies, rows):
+def start(own_in, coef_in, bases_in, padded, copies, own, coef, bases, rows, sems):
+    moves = [
+        pltpu.make_async_copy(src, dst, sems.at[i])
+        for i, (src, dst) in enumerate(((own_in, own), (coef_in, coef), (bases_in, bases)))
+    ]
+    for move in moves:
+        move.start()
     src = lax.broadcasted_iota(jnp.int32, (DIN, DIN), 0)
     out = lax.broadcasted_iota(jnp.int32, (DIN, DIN), 1)
     swap = jnp.where(src == PER * (out & (NODES - 1)) + (out >> 6), 1.0, 0.0).astype(BF)
+    for move in moves:
+        move.wait()
     value = jnp.dot(own[...], swap, preferred_element_type=F32).astype(BF)
     padded[:, :DIN] = value
     padded[:, DIN:] = jnp.zeros((ROWS, 8 * TILE - DIN), BF)
@@ -82,7 +95,8 @@
         fill(send, z, 2 * z + 1 - core)
 
 
-def join_cores(place, keep, got, send, mine, relay):
+def join_cores(place, keep, got, gathered, send, mine, relay, feats):
+    feats[...] = gathered[:, :, :DIN].reshape(NODES, DIN)
     zh, core = place[0], place[1]
     for e, ref in ((1, send.at[0]), (2, send.at[1]), (0, mine), (3, relay)):
         z = zh ^ e
@@ -116,29 +130,51 @@
     for r in range(RELS):
         for s in range(SRC):
             dense[r, :, s * TILE : (s + 1) * TILE] = acc[r * SRC + s].astype(BF)
-
-
-def aggregate(place, dense, feats, after, send, keep, full):
-    for r in range(RELS):
-        full[:, r * DIN : (r + 1) * DIN] = jnp.dot(dense[r], feats[...], preferred_element_type=F32)
-    full[:, RELS * DIN :] = jnp.zeros((TILE, 8 * CHUNK - RELS * DIN), F32)
+    dense[RELS] = jnp.zeros((TILE, SRC * TILE), BF)
+
+
+def aggregate(owner, place, dense, feats, after, out):
+    core = place[1] ^ owner
+    for e in range(4):
+        for i in range(2):
+            piece = 2 * (2 * (place[0] ^ e) + core) + i
+            spot = pl.ds(pl.multiple_of(lax.rem(piece, 3) * PIECE, PIECE), PIECE)
+            value = jnp.dot(dense[lax.div(piece, 3)], feats[:, spot], preferred_element_type=F32)
+            out[e, :, i * PIECE : (i + 1) * PIECE] = value.astype(out.dtype)
+
+
+def first_half(keep, got, send_a, send_b, keep_a, keep_b):
+    def total(e, rows):
+        return keep[e, rows] + got[e, rows].astype(F32)
+
+    a, b = slice(0, HALF), slice(HALF, TILE)
+    send_a[0] = total(1, a).astype(BF)
+    send_a[1] = total(2, a).astype(BF)
+    send_b[0] = total(3, b).astype(BF)
+    send_b[1] = total(2, b).astype(BF)
+    keep_a[0] = total(0, a)
+    keep_a[1] = total(3, a)
+    keep_b[0] = total(0, b)
+    keep_b[1] = total(1, b)
+
+
+def second_half(keep_a, keep_b, got_a, got_b, send_a, send_b, hold):
+    hold[:HALF] = keep_a[0] + got_a[0].astype(F32)
+    hold[HALF:] = keep_b[0] + got_b[0].astype(F32)
+    send_a[...] = (keep_a[1] + got_a[1].astype(F32)).astype(BF)
+    send_b[...] = (keep_b[1] + got_b[1].astype(F32)).astype(BF)
+
+
+def transform(place, hold, got_a, got_b, own, weights, send, keep, part):
     core = place[1]
-    for z in range(4):
-        keep[z] = full[:, pl.ds(pl.multiple_of((2 * z + core) * CHUNK, CHUNK), CHUNK)]
-        send[z] = full[:, pl.ds(pl.multiple_of((2 * z + 1 - core) * CHUNK, CHUNK), CHUNK)].astype(BF)
-
-
-def arrange(sums, own, msgs):
     src = lax.broadcasted_iota(jnp.int32, (CHUNK + TILE, DIN), 0)
     out = lax.broadcasted_iota(jnp.int32, (CHUNK + TILE, DIN), 1)
     swap = jnp.where(out == PER * (src & (NODES - 1)) + (src >> 6), 1.0, 0.0).astype(BF)
-    value = jnp.concatenate([sums[...], own[...]], axis=1)
-    msgs[...] = jnp.dot(value, swap, preferred_element_type=F32).astype(BF)
-
-
-def transform(place, msgs, weights, send, keep, part):
-    core = place[1]
-    part[...] = jnp.dot(msgs[...], weights[...], preferred_element_type=F32)
+    top = (hold[:HALF] + got_a[...].astype(F32)).astype(BF)
+    low = (hold[HALF:] + got_b[...].astype(F32)).astype(BF)
+    msgs = jnp.concatenate([jnp.concatenate([top, low], axis=0), own[...]], axis=1)
+    msgs = jnp.dot(msgs, swap, preferred_element_type=F32).astype(BF)
+    part[...] = jnp.dot(msgs, weights[...], preferred_element_type=F32)
     for z in range(4):
         keep[z] = part[pl.ds(pl.multiple_of((2 * z + core) * ROWS, ROWS), ROWS)]
         send[z] = part[pl.ds(pl.multiple_of((2 * z + 1 - core) * ROWS, ROWS), ROWS)].astype(BF)
@@ -172,26 +208,31 @@
     padded, copies = call(
         start,
         (shape(BF, ROWS, 8 * TILE), shape(BF, 4, ROWS, DIN + 8 * TILE)),
-        [VMEM] * 3,
-        [pltpu.VMEM((8, ROWS, TILE), F32)],
+        [HBM] * 3,
+        [
+            pltpu.VMEM((ROWS, DIN), BF),
+            pltpu.VMEM((RELS + 1, bases.shape[0]), F32),
+            pltpu.VMEM((PER, bases.shape[0], TILE), BF),
+            pltpu.VMEM((8, ROWS, TILE), F32),
+            pltpu.SemaphoreType.DMA((3,)),
+        ],
     )(features[0], coefficients, jnp.swapaxes(bases, 0, 1))
     gathered = exchange(copies, "zl")
     dense = call(
         densify,
-        shape(BF, RELS, TILE, SRC * TILE),
+        shape(BF, RELS + 1, TILE, SRC * TILE),
         [SMEM, SMEM, SMEM, VMEM],
         [pltpu.VMEM((RELS * SRC, TILE, TILE), F32)],
         pl.CostEstimate(flops=1 << 20, bytes_accessed=1 << 23, transcendentals=0),
     )(tile_count[0], tile_source[0, 0], tile_relation[0, 0], tile_values[0, 0])
-    feats = spread(gathered[:, :, :DIN].reshape(NODES, DIN), YX).reshape(SRC * TILE, DIN)
-
     parcel = shape(BF, 4, ROWS + 4 * PER, TILE)
     send, keep = call(sort, (parcel, parcel), [SMEM, VMEM, VMEM])(place, padded, gathered)
     block = shape(BF, 2, ROWS + 4 * PER, TILE)
     blocks = shape(BF, 2, 2, ROWS + 4 * PER, TILE)
-    send, mine, relay = call(join_cores, (blocks, block, block), [SMEM, VMEM, VMEM])(
-        place, keep, partner(send, "core", 1)
-    )
+    send, mine, relay, feats = call(
+        join_cores, (blocks, block, block, shape(BF, NODES, DIN)), [SMEM] + [VMEM] * 3
+    )(place, keep, partner(send, "core", 1), gathered)
+    feats = spread(feats, YX).reshape(SRC * TILE, DIN)
     first = partner(send, "zh", 1)
     relay = call(pass_on, blocks, [VMEM] * 2)(relay, first)
     second = partner(relay, "zh", 3)
@@ -201,27 +242,31 @@
         [SMEM] + [VMEM] * 3,
     )(place, mine, first, second)
 
-    send, keep = call(
-        aggregate,
-        (shape(BF, 4, TILE, CHUNK), shape(F32, 4, TILE, CHUNK)),
-        [SMEM, VMEM, VMEM, ANY],
-        [pltpu.VMEM((TILE, 8 * CHUNK), F32)],
-    )(place, dense, feats, relay)
-    pair = call(pair_sum, shape(BF, 4, TILE, CHUNK), [VMEM] * 2)(keep, partner(send, "core", 1))
-    sums = lax.psum_scatter(pair.reshape(4 * TILE, CHUNK), "zh", scatter_dimension=0, tiled=True)
+    send = call(functools.partial(aggregate, 1), shape(BF, 4, TILE, CHUNK), [SMEM, VMEM, VMEM, ANY])(
+        place, dense, feats, rows
+    )
+    keep = call(functools.partial(aggregate, 0), shape(F32, 4, TILE, CHUNK), [SMEM, VMEM, VMEM, ANY])(
+        place, dense, feats, send
+    )
+    two = shape(BF, 2, HALF, CHUNK)
+    wide = shape(F32, 2, HALF, CHUNK)
+    send_a, send_b, keep_a, keep_b = call(first_half, (two, two, wide, wide), [VMEM] * 2)(
+        keep, partner(send, "core", 1)
+    )
+    one = shape(BF, HALF, CHUNK)
+    send_a, send_b, hold = call(
+        second_half,
+        (one, one, shape(F32, TILE, CHUNK)),
+        [VMEM] * 4,
+        cost=pl.CostEstimate(flops=WEIGHT, bytes_accessed=1 << 20, transcendentals=0),
+    )(keep_a, keep_b, partner(send_a, "zh", 1), partner(send_b, "zh", 3))
     weights = spread(rows, YX).reshape(NODES * PER, DOUT)
-    msgs = call(
-        arrange,
-        shape(BF, TILE, DIN),
-        [VMEM] * 2,
-        cost=pl.CostEstimate(flops=WEIGHT, bytes_accessed=1 << 20, transcendentals=0),
-    )(sums, own.reshape(TILE, TILE))
     send, keep = call(
         transform,
         (shape(BF, 4, ROWS, DOUT), shape(F32, 4, ROWS, DOUT)),
-        [SMEM] + [VMEM] * 2,
+        [SMEM] + [VMEM] * 5,
         [pltpu.VMEM((TILE, DOUT), F32)],
-    )(place, msgs, weights)
+    )(place, hold, partner(send_a, "zh", 3), partner(send_b, "zh", 1), own.reshape(TILE, TILE), weights)
     pair = call(pair_sum, shape(BF, 4, ROWS, DOUT), [VMEM] * 2)(keep, partner(send, "core", 1))
     return call(finish, shape(BF, ROWS, DOUT), [VMEM])(exchange(pair, "zh"))[None]
 

time: 141 us -> 131 us (0.929)
  the two profiles are of different devices: /device:TPU:96 before, /device:TPU:1 now
where the time goes in v6:
time: 131 us; the launch traced here: 130 us
  starting transfers between devices  76.1 us (58%)
  waiting for transfers between devices  21.8 us (17%)
  blocking collectives  15.1 us (12%)
  Pallas kernels  9.4 us (7%)
  local copies, waits for them, and re-layouts  6.53 us (5%)
    ppermute x9, starting transfers between devices, partner(): lax.ppermute(x, axis, [(i, i ^ mask) for i in range(lax.axis_size(axis))])  58.3 us
    all_to_all x3, starting transfers between devices, exchange(): return lax.all_to_all(x, axis, split_axis=0, concat_axis=0, tiled=True)  17.8 us
    all_to_all x1, blocking collectives, exchange(): return lax.all_to_all(x, axis, split_axis=0, concat_axis=0, tiled=True)  15.1 us
    all_to_all x3, waiting for transfers between devices, exchange(): return lax.all_to_all(x, axis, split_axis=0, concat_axis=0, tiled=True)  13.7 us
    ppermute x9, waiting for transfers between devices, partner(): lax.ppermute(x, axis, [(i, i ^ mask) for i in range(lax.axis_size(axis))])  8.12 us
    unnamed x12, local copies, waits for them, and re-layouts  3.82 us
    broadcast_in_dim x2, local copies, waits for them, and re-layouts, spread(): return exchange(jnp.broadcast_to(x, (lax.axis_size(axis), *x.shape)), axis)  2.71 us
  transfers between devices with their start and end apart: 12, of which 6 were waited for; matrix products, arithmetic and copies ran while one was open for 1% of the time, Pallas kernels for 3%

profile of v6, /device:TPU:1, one launch (start us, length us, event | category | flops | bytes accessed | tf_op | source)
XLA Modules:
  0.0 129.9 jit_solution(8896850250905289292)
XLA Ops:
  0.0 0.0 copy-start.1
  0.0 0.9 copy-done.1
  0.9 0.0 copy-start.2
  0.9 0.7 copy-done.2
  1.6 0.0 copy-start.3
  1.6 0.7 copy-done.3
  2.3 1.7 %shard_map.74 = (bf16[16,1024]{1,0:T(8,128)(2,1)S(1)}, bf16[4,16,1792]{2,1,0:T(8,128)(2,1)}) custom-call(bf16[16,768]{1,0:T(8,128)(2,1)S(1)} %bitcast.19, f32[6,30]{1,0:T(8,128)S(1)} %copy-done.3, bf16[12,30,128]{2,1,0:T(8,128)(2,1)S(1)} %bitcast.17), custom_call_target="tpu_custom_call" | custom-call | tf_op jit(solution)/shard_map/pallas_call | solution.py:208
  4.0 6.5 %all-to-all-start = ((bf16[4,16,1792]{2,1,0:T(8,128)(2,1)}), bf16[4,16,1792]{2,1,0:T(8,128)(2,1)S(1)}, u32[]{:S(2)}, u32[]{:S(2)}) async-start(bf16[4,16,1792]{2,1,0:T(8,128)(2,1)} %get-tuple-element.25), calls=%async_computation | async-start | bytes 458752 | tf_op jit(solution)/shard_map/all_to_all | solution.py:195
  10.5 0.1 pad_add_fusion.place
  10.6 5.3 %all-to-all-done.gathered = bf16[4,16,1792]{2,1,0:T(8,128)(2,1)S(1)} async-done(((bf16[4,16,1792]{2,1,0:T(8,128)(2,1)}), bf16[4,16,1792]{2,1,0:T(8,128)(2,1)S(1)}, u32[]{:S(2)}, u32[]{:S(2)}) %all-to-all-start) | async-done | bytes 229408 | tf_op jit(solution)/shard_map/all_to_all | solution.py:195
  15.8 0.6 shard_map.75
  16.4 6.8 %collective-permute-start = (bf16[4,64,128]{2,1,0:T(8,128)(2,1)S(1)}, bf16[4,64,128]{2,1,0:T(8,128)(2,1)S(1)}, u32[]{:S(2)}, u32[]{:S(2)}) collective-permute-start(bf16[4,64,128]{2,1,0:T(8,128)(2,1)S(1)} %get-tuple-element.27), channel_id=1, source_target_pairs={{0,1},{1,0},{2,3},{3,2},{4,5},{5,4},{6,7},{7,6},{8,9},{9,8},{10,11... | collective-permute-start | bytes 196616 | tf_op jit(solution)/shard_map/ppermute | solution.py:203
  23.3 0.9 collective-permute-done.got
  24.2 0.6 shard_map.76
  24.7 1.3 %broadcast_in_dim.9 = bf16[16,64,768]{2,1,0:T(8,128)(2,1)} broadcast(bf16[64,768]{1,0:T(8,128)(2,1)S(1)} %get-tuple-element.28), dimensions={1,2} | broadcast | bytes 1671168 | tf_op jit(solution)/shard_map/broadcast_in_dim | solution.py:199
  26.1 0.0 copy-start.4
  26.1 0.0 copy-start.5
  26.1 5.8 %all-to-all-start.1 = ((bf16[16,64,768]{2,1,0:T(8,128)(2,1)}), bf16[16,64,768]{2,1,0:T(8,128)(2,1)S(1)}, u32[]{:S(2)}, u32[]{:S(2)}) async-start(bf16[16,64,768]{2,1,0:T(8,128)(2,1)} %broadcast_in_dim.9), calls=%async_computation.1 | async-start | bytes 3145728 | tf_op jit(solution)/shard_map/all_to_all | solution.py:195
  31.8 8.8 %collective-permute-start.1 = (bf16[2,2,64,128]{3,2,1,0:T(8,128)(2,1)S(1)}, bf16[2,2,64,128]{3,2,1,0:T(8,128)(2,1)S(1)}, u32[]{:S(2)}, u32[]{:S(2)}) collective-permute-start(bf16[2,2,64,128]{3,2,1,0:T(8,128)(2,1)S(1)} %get-tuple-element.30), channel_id=1, source_target_pairs={{0,2},{2,0},{4,6},{6,4},{1,3},{3,1},{5,7},{7,5},{8,10},{10,8},{12,... | collective-permute-start | bytes 196616 | tf_op jit(solution)/shard_map/ppermute | solution.py:203
  40.7 6.1 %collective-permute-done.1.got.first = bf16[2,2,64,128]{3,2,1,0:T(8,128)(2,1)S(1)} collective-permute-done((bf16[2,2,64,128]{3,2,1,0:T(8,128)(2,1)S(1)}, bf16[2,2,64,128]{3,2,1,0:T(8,128)(2,1)S(1)}, u32[]{:S(2)}, u32[]{:S(2)}) %collective-permute-start.1) | collective-permute-done | bytes 65568 | tf_op jit(solution)/shard_map/ppermute | solution.py:203
  46.8 5.6 %collective-permute-start.2 = (bf16[2,2,64,128]{3,2,1,0:T(8,128)(2,1)S(1)}, bf16[2,2,64,128]{3,2,1,0:T(8,128)(2,1)S(1)}, u32[]{:S(2)}, u32[]{:S(2)}) collective-permute-start(bf16[2,2,64,128]{3,2,1,0:T(8,128)(2,1)S(1)} %shard_map.77), channel_id=1, source_target_pairs={{0,6},{2,4},{4,2},{6,0},{1,7},{3,5},{5,3},{7,1},{8,14},{10,12},{12... | collective-permute-start | bytes 196616 | tf_op jit(solution)/shard_map/ppermute | solution.py:203
  53.1 0.0 copy-done.4
  53.1 0.0 copy-done.5
  53.1 0.0 copy-start
  53.1 1.5 %copy-done = bf16[1,1,56,128,128]{4,3,2,1,0:T(8,128)(2,1)S(1)} copy-done((bf16[1,1,56,128,128]{4,3,2,1,0:T(8,128)(2,1)S(1)}, bf16[1,1,56,128,128]{4,3,2,1,0:T(8,128)(2,1)}, u32[]{:S(2)}) %copy-start) | copy-done | bytes 1835032
  54.6 1.3 shard_map.73.dense
  55.9 0.0 collective-permute-done.2.second
  55.9 0.6 shard_map.78
  56.5 0.0 all-to-all-done.1
  56.5 1.4 %shard_map.79.after = bf16[4,128,512]{2,1,0:T(8,128)(2,1)S(1)} custom-call(s32[2]{0:T(128)S(1)} %pad_add_fusion.place, bf16[6,128,1024]{2,1,0:T(8,128)(2,1)S(1)} %shard_map.73.dense, bf16[1024,768]{1,0:T(8,128)(2,1)S(1)} %bitcast.13, bf16[48,1024]{1,0:T(8,128)(2,1)S(1)} %get-tuple-element.32.after), custom_call_target="tpu_custom_call" | custom-call | tf_op jit(solution)/shard_map/pallas_call | solution.py:245
  57.8 3.4 %collective-permute-start.3 = (bf16[4,128,512]{2,1,0:T(8,128)(2,1)S(1)}, bf16[4,128,512]{2,1,0:T(8,128)(2,1)S(1)}, u32[]{:S(2)}, u32[]{:S(2)}) collective-permute-start(bf16[4,128,512]{2,1,0:T(8,128)(2,1)S(1)} %shard_map.79.after), channel_id=1, source_target_pairs={{0,1},{1,0},{2,3},{3,2},{4,5},{5,4},{6,7},{7,6},{8,9},{9,8},{10,11... | collective-permute-start | bytes 1572872 | tf_op jit(solution)/shard_map/ppermute | solution.py:203
  61.2 1.4 %shard_map.80.keep = f32[4,128,512]{2,1,0:T(8,128)S(1)} custom-call(s32[2]{0:T(128)S(1)} %pad_add_fusion.place, bf16[6,128,1024]{2,1,0:T(8,128)(2,1)S(1)} %shard_map.73.dense, bf16[1024,768]{1,0:T(8,128)(2,1)S(1)} %bitcast.14, bf16[4,128,512]{2,1,0:T(8,128)(2,1)S(1)} %shard_map.79.after), custom_call_target="tpu_custom_call" | custom-call | tf_op jit(solution)/shard_map/pallas_call | solution.py:248
  62.6 0.1 collective-permute-done.3.got
  62.8 0.1 shard_map.81
  62.8 8.7 %collective-permute-start.4 = (bf16[2,64,512]{2,1,0:T(8,128)(2,1)S(1)}, bf16[2,64,512]{2,1,0:T(8,128)(2,1)S(1)}, u32[]{:S(2)}, u32[]{:S(2)}) collective-permute-start(bf16[2,64,512]{2,1,0:T(8,128)(2,1)S(1)} %get-tuple-element.35), channel_id=1, source_target_pairs={{0,2},{2,0},{4,6},{6,4},{1,3},{3,1},{5,7},{7,5},{8,10},{10,8},{12,... | collective-permute-start | bytes 393224 | tf_op jit(solution)/shard_map/ppermute | solution.py:203
  71.6 6.3 %collective-permute-start.5 = (bf16[2,64,512]{2,1,0:T(8,128)(2,1)S(1)}, bf16[2,64,512]{2,1,0:T(8,128)(2,1)S(1)}, u32[]{:S(2)}, u32[]{:S(2)}) collective-permute-start(bf16[2,64,512]{2,1,0:T(8,128)(2,1)S(1)} %get-tuple-element.36), channel_id=1, source_target_pairs={{0,6},{2,4},{4,2},{6,0},{1,7},{3,5},{5,3},{7,1},{8,14},{10,12},{12... | collective-permute-start | bytes 393224 | tf_op jit(solution)/shard_map/ppermute | solution.py:203
  77.9 1.4 %broadcast_in_dim.10 = bf16[16,48,1024]{2,1,0:T(8,128)(2,1)} broadcast(bf16[48,1024]{1,0:T(8,128)(2,1)S(1)} %get-tuple-element.32.after), dimensions={1,2} | broadcast | bytes 1671168 | tf_op jit(solution)/shard_map/broadcast_in_dim | solution.py:199
  79.2 5.6 %all-to-all-start.2 = ((bf16[16,48,1024]{2,1,0:T(8,128)(2,1)}), bf16[16,48,1024]{2,1,0:T(8,128)(2,1)S(1)}, u32[]{:S(2)}, u32[]{:S(2)}) async-start(bf16[16,48,1024]{2,1,0:T(8,128)(2,1)} %broadcast_in_dim.10), calls=%async_computation.2 | async-start | bytes 3145728 | tf_op jit(solution)/shard_map/all_to_all | solution.py:195
  84.8 0.0 collective-permute-done.4.got_a
  84.8 0.0 collective-permute-done.5.got_b
  84.9 5.9 %collective-permute-start.6 = (bf16[64,512]{1,0:T(8,128)(2,1)S(1)}, bf16[64,512]{1,0:T(8,128)(2,1)S(1)}, u32[]{:S(2)}, u32[]{:S(2)}) collective-permute-start(bf16[64,512]{1,0:T(8,128)(2,1)S(1)} %get-tuple-element.38), channel_id=1, source_target_pairs={{0,6},{2,4},{4,2},{6,0},{1,7},{3,5},{5,3},{7,1},{8,14},{10,12},{12... | collective-permute-start | bytes 196616 | tf_op jit(solution)/shard_map/ppermute | solution.py:203
  90.8 7.5 %collective-permute-start.7 = (bf16[64,512]{1,0:T(8,128)(2,1)S(1)}, bf16[64,512]{1,0:T(8,128)(2,1)S(1)}, u32[]{:S(2)}, u32[]{:S(2)}) collective-permute-start(bf16[64,512]{1,0:T(8,128)(2,1)S(1)} %get-tuple-element.39), channel_id=1, source_target_pairs={{0,2},{2,0},{4,6},{6,4},{1,3},{3,1},{5,7},{7,5},{8,10},{10,8},{12,... | collective-permute-start | bytes 196616 | tf_op jit(solution)/shard_map/ppermute | solution.py:203
  98.4 8.4 %all-to-all-done.2 = bf16[16,48,1024]{2,1,0:T(8,128)(2,1)S(1)} async-done(((bf16[16,48,1024]{2,1,0:T(8,128)(2,1)}), bf16[16,48,1024]{2,1,0:T(8,128)(2,1)S(1)}, u32[]{:S(2)}, u32[]{:S(2)}) %all-to-all-start.2) | async-done | bytes 1572896 | tf_op jit(solution)/shard_map/all_to_all | solution.py:195
  106.8 0.0 collective-permute-done.6.got_a
  106.8 0.0 collective-permute-done.7.got_b
  106.8 1.2 shard_map.83
  108.0 5.2 %collective-permute-start.8 = (bf16[4,16,1024]{2,1,0:T(8,128)(2,1)S(1)}, bf16[4,16,1024]{2,1,0:T(8,128)(2,1)S(1)}, u32[]{:S(2)}, u32[]{:S(2)}) collective-permute-start(bf16[4,16,1024]{2,1,0:T(8,128)(2,1)S(1)} %get-tuple-element.42), channel_id=1, source_target_pairs={{0,1},{1,0},{2,3},{3,2},{4,5},{5,4},{6,7},{7,6},{8,9},{9,8},{10,11... | collective-permute-start | bytes 393224 | tf_op jit(solution)/shard_map/ppermute | solution.py:203
  113.2 1.0 collective-permute-done.8.got
  114.2 15.1 %all_to_all.20.got = bf16[4,16,1024]{2,1,0:T(8,128)(2,1)S(1)} all-to-all(bf16[4,16,1024]{2,1,0:T(8,128)(2,1)S(1)} %shard_map.84), channel_id=1, replica_groups=mesh['y'=4,'x'=4,'zl'=4,'zh'=4,'core'=2] {'zh'}, dimensions={0} | all-to-all | bytes 262144 | tf_op jit(solution)/shard_map/all_to_all | solution.py:195
  129.3 0.6 shard_map.85
  (3 shorter events, 0.1 us)
Async XLA Ops:
  0.0 0.9 copy-start.1
  0.9 0.7 copy-start.2
  1.6 0.7 copy-start.3
  4.0 11.8 %all-to-all-start = ((bf16[4,16,1792]{2,1,0:T(8,128)(2,1)}), bf16[4,16,1792]{2,1,0:T(8,128)(2,1)S(1)}, u32[]{:S(2)}, u32[]{:S(2)}) async-start(bf16[4,16,1792]{2,1,0:T(8,128)(2,1)} %get-tuple-element.25), calls=%async_computation | async-start | bytes 458752 | tf_op jit(solution)/shard_map/all_to_all | solution.py:195
  16.4 7.7 %collective-permute-start = (bf16[4,64,128]{2,1,0:T(8,128)(2,1)S(1)}, bf16[4,64,128]{2,1,0:T(8,128)(2,1)S(1)}, u32[]{:S(2)}, u32[]{:S(2)}) collective-permute-start(bf16[4,64,128]{2,1,0:T(8,128)(2,1)S(1)} %get-tuple-element.27), channel_id=1, source_target_pairs={{0,1},{1,0},{2,3},{3,2},{4,5},{5,4},{6,7},{7,6},{8,9},{9,8},{10,11... | collective-permute-start | bytes 196616 | tf_op jit(solution)/shard_map/ppermute | solution.py:203
  26.1 27.0 %copy-start.4 = (s32[1,1,56]{2,1,0:T(1,128)S(1)}, s32[1,1,56]{2,1,0:T(1,128)}, u32[]{:S(2)}) copy-start(s32[1,1,56]{2,1,0:T(1,128)} %param.11) | copy-start | bytes 676
  26.1 27.0 %copy-start.5 = (s32[1,1,56]{2,1,0:T(1,128)S(1)}, s32[1,1,56]{2,1,0:T(1,128)}, u32[]{:S(2)}) copy-start(s32[1,1,56]{2,1,0:T(1,128)} %param.12) | copy-start | bytes 676
  26.1 30.4 %all-to-all-start.1 = ((bf16[16,64,768]{2,1,0:T(8,128)(2,1)}), bf16[16,64,768]{2,1,0:T(8,128)(2,1)S(1)}, u32[]{:S(2)}, u32[]{:S(2)}) async-start(bf16[16,64,768]{2,1,0:T(8,128)(2,1)} %broadcast_in_dim.9), calls=%async_computation.1 | async-start | bytes 3145728 | tf_op jit(solution)/shard_map/all_to_all | solution.py:195
  31.8 14.9 %collective-permute-start.1 = (bf16[2,2,64,128]{3,2,1,0:T(8,128)(2,1)S(1)}, bf16[2,2,64,128]{3,2,1,0:T(8,128)(2,1)S(1)}, u32[]{:S(2)}, u32[]{:S(2)}) collective-permute-start(bf16[2,2,64,128]{3,2,1,0:T(8,128)(2,1)S(1)} %get-tuple-element.30), channel_id=1, source_target_pairs={{0,2},{2,0},{4,6},{6,4},{1,3},{3,1},{5,7},{7,5},{8,10},{10,8},{12,... | collective-permute-start | bytes 196616 | tf_op jit(solution)/shard_map/ppermute | solution.py:203
  46.8 9.1 %collective-permute-start.2 = (bf16[2,2,64,128]{3,2,1,0:T(8,128)(2,1)S(1)}, bf16[2,2,64,128]{3,2,1,0:T(8,128)(2,1)S(1)}, u32[]{:S(2)}, u32[]{:S(2)}) collective-permute-start(bf16[2,2,64,128]{3,2,1,0:T(8,128)(2,1)S(1)} %shard_map.77), channel_id=1, source_target_pairs={{0,6},{2,4},{4,2},{6,0},{1,7},{3,5},{5,3},{7,1},{8,14},{10,12},{12... | collective-permute-start | bytes 196616 | tf_op jit(solution)/shard_map/ppermute | solution.py:203
  53.1 1.5 %copy-start = (bf16[1,1,56,128,128]{4,3,2,1,0:T(8,128)(2,1)S(1)}, bf16[1,1,56,128,128]{4,3,2,1,0:T(8,128)(2,1)}, u32[]{:S(2)}) copy-start(bf16[1,1,56,128,128]{4,3,2,1,0:T(8,128)(2,1)} %param.10) | copy-start | bytes 5505028
  57.8 4.9 %collective-permute-start.3 = (bf16[4,128,512]{2,1,0:T(8,128)(2,1)S(1)}, bf16[4,128,512]{2,1,0:T(8,128)(2,1)S(1)}, u32[]{:S(2)}, u32[]{:S(2)}) collective-permute-start(bf16[4,128,512]{2,1,0:T(8,128)(2,1)S(1)} %shard_map.79.after), channel_id=1, source_target_pairs={{0,1},{1,0},{2,3},{3,2},{4,5},{5,4},{6,7},{7,6},{8,9},{9,8},{10,11... | collective-permute-start | bytes 1572872 | tf_op jit(solution)/shard_map/ppermute | solution.py:203
  62.8 22.0 %collective-permute-start.4 = (bf16[2,64,512]{2,1,0:T(8,128)(2,1)S(1)}, bf16[2,64,512]{2,1,0:T(8,128)(2,1)S(1)}, u32[]{:S(2)}, u32[]{:S(2)}) collective-permute-start(bf16[2,64,512]{2,1,0:T(8,128)(2,1)S(1)} %get-tuple-element.35), channel_id=1, source_target_pairs={{0,2},{2,0},{4,6},{6,4},{1,3},{3,1},{5,7},{7,5},{8,10},{10,8},{12,... | collective-permute-start | bytes 393224 | tf_op jit(solution)/shard_map/ppermute | solution.py:203
  71.6 13.2 %collective-permute-start.5 = (bf16[2,64,512]{2,1,0:T(8,128)(2,1)S(1)}, bf16[2,64,512]{2,1,0:T(8,128)(2,1)S(1)}, u32[]{:S(2)}, u32[]{:S(2)}) collective-permute-start(bf16[2,64,512]{2,1,0:T(8,128)(2,1)S(1)} %get-tuple-element.36), channel_id=1, source_target_pairs={{0,6},{2,4},{4,2},{6,0},{1,7},{3,5},{5,3},{7,1},{8,14},{10,12},{12... | collective-permute-start | bytes 393224 | tf_op jit(solution)/shard_map/ppermute | solution.py:203
  79.2 27.5 %all-to-all-start.2 = ((bf16[16,48,1024]{2,1,0:T(8,128)(2,1)}), bf16[16,48,1024]{2,1,0:T(8,128)(2,1)S(1)}, u32[]{:S(2)}, u32[]{:S(2)}) async-start(bf16[16,48,1024]{2,1,0:T(8,128)(2,1)} %broadcast_in_dim.10), calls=%async_computation.2 | async-start | bytes 3145728 | tf_op jit(solution)/shard_map/all_to_all | solution.py:195
  84.9 21.9 %collective-permute-start.6 = (bf16[64,512]{1,0:T(8,128)(2,1)S(1)}, bf16[64,512]{1,0:T(8,128)(2,1)S(1)}, u32[]{:S(2)}, u32[]{:S(2)}) collective-permute-start(bf16[64,512]{1,0:T(8,128)(2,1)S(1)} %get-tuple-element.38), channel_id=1, source_target_pairs={{0,6},{2,4},{4,2},{6,0},{1,7},{3,5},{5,3},{7,1},{8,14},{10,12},{12... | collective-permute-start | bytes 196616 | tf_op jit(solution)/shard_map/ppermute | solution.py:203
  90.8 16.0 %collective-permute-start.7 = (bf16[64,512]{1,0:T(8,128)(2,1)S(1)}, bf16[64,512]{1,0:T(8,128)(2,1)S(1)}, u32[]{:S(2)}, u32[]{:S(2)}) collective-permute-start(bf16[64,512]{1,0:T(8,128)(2,1)S(1)} %get-tuple-element.39), channel_id=1, source_target_pairs={{0,2},{2,0},{4,6},{6,4},{1,3},{3,1},{5,7},{7,5},{8,10},{10,8},{12,... | collective-permute-start | bytes 196616 | tf_op jit(solution)/shard_map/ppermute | solution.py:203
  108.0 6.2 %collective-permute-start.8 = (bf16[4,16,1024]{2,1,0:T(8,128)(2,1)S(1)}, bf16[4,16,1024]{2,1,0:T(8,128)(2,1)S(1)}, u32[]{:S(2)}, u32[]{:S(2)}) collective-permute-start(bf16[4,16,1024]{2,1,0:T(8,128)(2,1)S(1)} %get-tuple-element.42), channel_id=1, source_target_pairs={{0,1},{1,0},{2,3},{3,2},{4,5},{5,4},{6,7},{7,6},{8,9},{9,8},{10,11... | collective-permute-start | bytes 393224 | tf_op jit(solution)/shard_map/ppermute | solution.py:203

commit v7 on v6

--- a/solution.py
+++ b/solution.py
@@ -17,7 +17,6 @@
 ANY = pl.BlockSpec(memory_space=pl.ANY)
 HBM = pl.BlockSpec(memory_space=pltpu.HBM)
 SMEM = pl.BlockSpec(memory_space=pltpu.SMEM)
-PARAMS = pltpu.CompilerParams(vmem_limit_bytes=16 * 1024 * 1024)
 
 RELS = 5
 DIN = 768
@@ -30,12 +29,15 @@
 SLOT = 8
 SELF = 2
 CHUNK = SLOT * NODES
+QUART = 2 * (SLOT + SELF)
+DEPTH = QUART * NODES
+WIDE = DOUT // 2
 HALF = TILE // 2
 PIECE = 256
 WEIGHT = 10**11
 
 
-def call(body, outs, ins, scratch=(), cost=None):
+def call(body, outs, ins, scratch=(), cost=None, limit=16):
     return pl.pallas_call(
         body,
         cost_estimate=cost,
@@ -43,7 +45,7 @@
         in_specs=ins,
         out_specs=jax.tree.map(lambda _: VMEM, outs),
         scratch_shapes=list(scratch),
-        compiler_params=PARAMS,
+        compiler_params=pltpu.CompilerParams(vmem_limit_bytes=limit * 1024 * 1024),
     )
 
 
@@ -81,27 +83,19 @@
             copies[i, :, DIN + k * TILE : DIN + (k + 1) * TILE] = rows[k].astype(BF)
 
 
-def sort(place, padded, gathered, send, keep):
-    core = place[1]
-
-    def fill(ref, z, k):
-        ref[z, :ROWS] = padded[:, pl.ds(pl.multiple_of(k * TILE, TILE), TILE)]
-        spot = pl.ds(pl.multiple_of(DIN + k * TILE, TILE), TILE)
-        rows = [gathered[i, :, spot].astype(F32)[:PER] for i in range(4)]
-        ref[z, ROWS:] = jnp.concatenate(rows, axis=0).astype(BF)
-
-    for z in range(4):
-        fill(keep, z, 2 * z + core)
-        fill(send, z, 2 * z + 1 - core)
-
-
-def join_cores(place, keep, got, gathered, send, mine, relay, feats):
-    feats[...] = gathered[:, :, :DIN].reshape(NODES, DIN)
-    zh, core = place[0], place[1]
+def sort(place, padded, gathered, send, mine, relay):
     for e, ref in ((1, send.at[0]), (2, send.at[1]), (0, mine), (3, relay)):
-        z = zh ^ e
-        ref[core] = keep[z]
-        ref[1 - core] = got[z]
+        first = (place[0] ^ e) * 2 * TILE
+        for i in range(2):
+            ref[i * ROWS : (i + 1) * ROWS] = padded[:, pl.ds(pl.multiple_of(first + i * TILE, TILE), TILE)]
+        rows = []
+        for z in range(4):
+            a, b = (
+                gathered[z, :, pl.ds(pl.multiple_of(DIN + first + i * TILE, TILE), TILE)].astype(F32)
+                for i in range(2)
+            )
+            rows += [a[:SLOT], b[:SLOT], a[SLOT : SLOT + SELF], b[SLOT : SLOT + SELF]]
+        ref[2 * ROWS :] = jnp.concatenate(rows, axis=0).astype(BF)
 
 
 def pass_on(relay, got, send):
@@ -112,10 +106,10 @@
 def join_groups(place, mine, first, second, own, rows):
     for e, ref in ((0, mine), (1, first.at[0]), (3, second.at[0]), (2, second.at[1])):
         z = place[0] ^ e
-        for c in range(2):
-            g = 2 * z + c
-            own[g] = ref[c, :ROWS]
-            rows[:, pl.ds(pl.multiple_of(g * TILE, TILE), TILE)] = ref[c, ROWS:]
+        spot = pl.ds(pl.multiple_of(z * ROWS, ROWS), ROWS)
+        own[spot, :TILE] = ref[:ROWS]
+        own[spot, TILE:] = ref[ROWS : 2 * ROWS]
+        rows[:, pl.ds(pl.multiple_of(z * TILE, TILE), TILE)] = ref[2 * ROWS :]
 
 
 def densify(count, source, relation, values, dense, acc):
@@ -165,30 +159,46 @@
     send_b[...] = (keep_b[1] + got_b[1].astype(F32)).astype(BF)
 
 
-def transform(place, hold, got_a, got_b, own, weights, send, keep, part):
+def settle(hold, got_a, got_b, own, msgs):
+    msgs[:HALF] = (hold[:HALF] + got_a[...].astype(F32)).astype(BF)
+    msgs[HALF:TILE] = (hold[HALF:] + got_b[...].astype(F32)).astype(BF)
+    msgs[TILE:, : 2 * TILE] = own[...]
+    msgs[TILE:, 2 * TILE :] = jnp.zeros((4 * ROWS, CHUNK - 2 * TILE), BF)
+
+
+def order(swap):
+    src = lax.broadcasted_iota(jnp.int32, (DEPTH, DEPTH), 0)
+    out = lax.broadcasted_iota(jnp.int32, (DEPTH, DEPTH), 1)
+    swap[...] = jnp.where(out == QUART * (src & (NODES - 1)) + (src >> 6), 1.0, 0.0).astype(BF)
+
+
+def transform(place, msgs, got, swap, weights, send, full):
     core = place[1]
-    src = lax.broadcasted_iota(jnp.int32, (CHUNK + TILE, DIN), 0)
-    out = lax.broadcasted_iota(jnp.int32, (CHUNK + TILE, DIN), 1)
-    swap = jnp.where(out == PER * (src & (NODES - 1)) + (src >> 6), 1.0, 0.0).astype(BF)
-    top = (hold[:HALF] + got_a[...].astype(F32)).astype(BF)
-    low = (hold[HALF:] + got_b[...].astype(F32)).astype(BF)
-    msgs = jnp.concatenate([jnp.concatenate([top, low], axis=0), own[...]], axis=1)
-    msgs = jnp.dot(msgs, swap, preferred_element_type=F32).astype(BF)
-    part[...] = jnp.dot(msgs, weights[...], preferred_element_type=F32)
-    for z in range(4):
-        keep[z] = part[pl.ds(pl.multiple_of((2 * z + core) * ROWS, ROWS), ROWS)]
-        send[z] = part[pl.ds(pl.multiple_of((2 * z + 1 - core) * ROWS, ROWS), ROWS)].astype(BF)
-
-
-def pair_sum(keep, got, out):
-    out[...] = (keep[...] + got[...].astype(F32)).astype(BF)
-
-
-def finish(got, out):
-    total = got[0].astype(F32)
+    for c, ref in ((core, msgs), (1 - core, got)):
+        full[:, pl.ds(pl.multiple_of(c * CHUNK, CHUNK), CHUNK)] = ref[:TILE]
+        for z in range(4):
+            spot = pl.ds(pl.multiple_of((2 * z + c) * ROWS, ROWS), ROWS)
+            full[spot, 2 * CHUNK :] = ref[TILE + z * ROWS : TILE + (z + 1) * ROWS, : 2 * TILE]
+    value = jnp.dot(full[...], swap[...], preferred_element_type=F32).astype(BF)
+    send[...] = jnp.dot(value, weights[...], preferred_element_type=F32).astype(BF)
+
+
+def finish(place, got, mine, other, total):
+    value = got[0].astype(F32)
     for i in range(1, 4):
-        total = total + got[i].astype(F32)
-    out[...] = jnp.maximum(total, 0.0).astype(BF)
+        value = value + got[i].astype(F32)
+    total[...] = jnp.maximum(value, 0.0)
+    core = place[1]
+    mine[...] = total[pl.ds(pl.multiple_of(core * ROWS, ROWS), ROWS)].astype(BF)
+    other[...] = total[pl.ds(pl.multiple_of((1 - core) * ROWS, ROWS), ROWS)].astype(BF)
+
+
+def place_columns(place, mine, got, out):
+    core = place[1]
+    for c, ref in ((core, mine), (1 - core, got)):
+        for z in range(4):
+            spot = pl.ds(pl.multiple_of((2 * z + c) * TILE, TILE), TILE)
+            out[:, spot] = ref[:, z * TILE : (z + 1) * TILE]
 
 
 def exchange(x, axis):
@@ -216,6 +226,7 @@
             pltpu.VMEM((8, ROWS, TILE), F32),
             pltpu.SemaphoreType.DMA((3,)),
         ],
+        limit=60,
     )(features[0], coefficients, jnp.swapaxes(bases, 0, 1))
     gathered = exchange(copies, "zl")
     dense = call(
@@ -225,20 +236,17 @@
         [pltpu.VMEM((RELS * SRC, TILE, TILE), F32)],
         pl.CostEstimate(flops=1 << 20, bytes_accessed=1 << 23, transcendentals=0),
     )(tile_count[0], tile_source[0, 0], tile_relation[0, 0], tile_values[0, 0])
-    parcel = shape(BF, 4, ROWS + 4 * PER, TILE)
-    send, keep = call(sort, (parcel, parcel), [SMEM, VMEM, VMEM])(place, padded, gathered)
-    block = shape(BF, 2, ROWS + 4 * PER, TILE)
-    blocks = shape(BF, 2, 2, ROWS + 4 * PER, TILE)
-    send, mine, relay, feats = call(
-        join_cores, (blocks, block, block, shape(BF, NODES, DIN)), [SMEM] + [VMEM] * 3
-    )(place, keep, partner(send, "core", 1), gathered)
-    feats = spread(feats, YX).reshape(SRC * TILE, DIN)
+    feats = spread(gathered[:, :, :DIN].reshape(NODES, DIN), YX).reshape(SRC * TILE, DIN)
+
+    block = shape(BF, 2 * ROWS + 4 * QUART, TILE)
+    blocks = shape(BF, 2, 2 * ROWS + 4 * QUART, TILE)
+    send, mine, relay = call(sort, (blocks, block, block), [SMEM, VMEM, VMEM])(place, padded, gathered)
     first = partner(send, "zh", 1)
     relay = call(pass_on, blocks, [VMEM] * 2)(relay, first)
     second = partner(relay, "zh", 3)
     own, rows = call(
         join_groups,
-        (shape(BF, 8, ROWS, TILE), shape(BF, 4 * PER, DOUT)),
+        (shape(BF, 4 * ROWS, 2 * TILE), shape(BF, 4 * QUART, WIDE)),
         [SMEM] + [VMEM] * 3,
     )(place, mine, first, second)
 
@@ -260,15 +268,25 @@
         [VMEM] * 4,
         cost=pl.CostEstimate(flops=WEIGHT, bytes_accessed=1 << 20, transcendentals=0),
     )(keep_a, keep_b, partner(send_a, "zh", 1), partner(send_b, "zh", 3))
-    weights = spread(rows, YX).reshape(NODES * PER, DOUT)
-    send, keep = call(
+    weights = spread(rows, YX).reshape(DEPTH, WIDE)
+    msgs = call(settle, shape(BF, TILE + 4 * ROWS, CHUNK), [VMEM] * 4)(
+        hold, partner(send_a, "zh", 3), partner(send_b, "zh", 1), own
+    )
+    swap = call(order, shape(BF, DEPTH, DEPTH), [])()
+    send = call(
         transform,
-        (shape(BF, 4, ROWS, DOUT), shape(F32, 4, ROWS, DOUT)),
-        [SMEM] + [VMEM] * 5,
-        [pltpu.VMEM((TILE, DOUT), F32)],
-    )(place, hold, partner(send_a, "zh", 3), partner(send_b, "zh", 1), own.reshape(TILE, TILE), weights)
-    pair = call(pair_sum, shape(BF, 4, ROWS, DOUT), [VMEM] * 2)(keep, partner(send, "core", 1))
-    return call(finish, shape(BF, ROWS, DOUT), [VMEM])(exchange(pair, "zh"))[None]
+        shape(BF, TILE, WIDE),
+        [SMEM] + [VMEM] * 4,
+        [pltpu.VMEM((TILE, DEPTH), BF)],
+    )(place, msgs, partner(msgs, "core", 1), swap, weights)
+    half = shape(BF, ROWS, WIDE)
+    mine, other = call(finish, (half, half), [SMEM, VMEM], [pltpu.VMEM((2 * ROWS, WIDE), F32)])(
+        place, exchange(send.reshape(4, 2 * ROWS, WIDE), "zh")
+    )
+    out = call(place_columns, shape(BF, ROWS, DOUT), [SMEM, VMEM, VMEM])(
+        place, mine, partner(other, "core", 1)
+    )
+    return out[None]
 
 
 def solution(mesh):

time: 131 us -> 129 us (0.985)
  blocking collectives: 15.1 us -> 33.5 us
  waiting for transfers between devices: 21.8 us -> 5.38 us
  starting transfers between devices: 76.1 us -> 71.1 us
  Pallas kernels: 9.4 us -> 12 us
  local copies, waits for them, and re-layouts: 6.53 us -> 4.02 us
    all_to_all x1 -> x2, blocking collectives: 15.1 us -> 33.5 us  [exchange(): return lax.all_to_all(x, axis, split_axis=0, concat_axis=0, tiled=True)]
    all_to_all x3 -> x2, waiting for transfers between devices: 13.7 us -> 0.01 us  [exchange(): return lax.all_to_all(x, axis, split_axis=0, concat_axis=0, tiled=True)]
    all_to_all x3 -> x2, starting transfers between devices: 17.8 us -> 14 us  [exchange(): return lax.all_to_all(x, axis, split_axis=0, concat_axis=0, tiled=True)]
    ppermute x9, waiting for transfers between devices: 8.12 us -> 5.38 us  [partner(): lax.ppermute(x, axis, [(i, i ^ mask) for i in range(lax.axis_size(axis))])]
    unnamed x12 -> x8, local copies, waits for them, and re-layouts: 3.82 us -> 1.51 us
    pallas_call x6 -> x7, Pallas kernels: 3.57 us -> 5.76 us  [the longest x1 2.22 us: on_device(): call(transform, shape(BF, TILE, WIDE), [SMEM] + [VMEM] * 4, [pltpu.VMEM((...]
  transfers between devices with their start and end apart: 12 -> 11, of which waited for: 6 -> 5; matrix products, arithmetic and copies ran while one was open for 1% -> 1% of each run, Pallas kernels for 3% -> 4%
where the time goes in v7:
time: 129 us; the launch traced here: 127 us
  starting transfers between devices  71.1 us (55%)
  blocking collectives  33.5 us (26%)
  Pallas kernels  12 us (9%)
  waiting for transfers between devices  5.38 us (4%)
  local copies, waits for them, and re-layouts  4.02 us (3%)
    ppermute x9, starting transfers between devices, partner(): lax.ppermute(x, axis, [(i, i ^ mask) for i in range(lax.axis_size(axis))])  57.1 us
    all_to_all x2, blocking collectives, exchange(): return lax.all_to_all(x, axis, split_axis=0, concat_axis=0, tiled=True)  33.5 us
    all_to_all x2, starting transfers between devices, exchange(): return lax.all_to_all(x, axis, split_axis=0, concat_axis=0, tiled=True)  14 us
    ppermute x9, waiting for transfers between devices, partner(): lax.ppermute(x, axis, [(i, i ^ mask) for i in range(lax.axis_size(axis))])  5.38 us
  transfers between devices with their start and end apart: 11, of which 5 were waited for; matrix products, arithmetic and copies ran while one was open for 1% of the time, Pallas kernels for 4%

profile of v7, /device:TPU:1, one launch (start us, length us, event | category | flops | bytes accessed | tf_op | source)
XLA Modules:
  0.0 127.0 jit_solution(11851640917267177667)
XLA Ops:
  0.0 2.1 %shard_map.74 = (bf16[16,1024]{1,0:T(8,128)(2,1)}, bf16[4,16,1792]{2,1,0:T(8,128)(2,1)}) custom-call(bf16[16,768]{1,0:T(8,128)(2,1)} %bitcast.22, f32[6,30]{1,0:T(8,128)} %coef_in.1, bf16[12,30,128]{2,1,0:T(8,128)(2,1)} %bitcast.21), custom_call_target="tpu_custom_call" | custom-call | tf_op jit(solution)/shard_map/pallas_call | solution.py:218
  2.1 12.2 %all_to_all.20.gathered = bf16[4,16,1792]{2,1,0:T(8,128)(2,1)S(1)} all-to-all(bf16[4,16,1792]{2,1,0:T(8,128)(2,1)} %get-tuple-element.21), channel_id=1, replica_groups=mesh['y'=4,'x'=4,'zl'=4,'zh'=4,'core'=2] {'zl'}, dimensions={0} | all-to-all | bytes 458752 | tf_op jit(solution)/shard_map/all_to_all | solution.py:205
  14.3 1.3 %broadcast_in_dim.9 = bf16[16,64,768]{2,1,0:T(8,128)(2,1)} broadcast(bf16[64,768]{1,0:T(8,128)(2,1)S(1)} %bitcast.20), dimensions={1,2} | broadcast | bytes 1671168 | tf_op jit(solution)/shard_map/broadcast_in_dim | solution.py:209
  15.7 0.0 copy-start.1
  15.7 0.0 copy-start.2
  15.7 0.0 copy-start.3
  15.7 7.0 %all-to-all-start.1 = ((bf16[16,64,768]{2,1,0:T(8,128)(2,1)}), bf16[16,64,768]{2,1,0:T(8,128)(2,1)S(1)}, u32[]{:S(2)}, u32[]{:S(2)}) async-start(bf16[16,64,768]{2,1,0:T(8,128)(2,1)} %broadcast_in_dim.9), calls=%async_computation.1 | async-start | bytes 3145728 | tf_op jit(solution)/shard_map/all_to_all | solution.py:205
  22.7 0.1 pad_add_fusion.place
  22.7 0.0 copy-done.1
  22.7 0.6 shard_map.75
  23.3 8.8 %collective-permute-start = (bf16[2,112,128]{2,1,0:T(8,128)(2,1)S(1)}, bf16[2,112,128]{2,1,0:T(8,128)(2,1)S(1)}, u32[]{:S(2)}, u32[]{:S(2)}) collective-permute-start(bf16[2,112,128]{2,1,0:T(8,128)(2,1)S(1)} %get-tuple-element.24), channel_id=1, source_target_pairs={{0,2},{2,0},{4,6},{6,4},{1,3},{3,1},{5,7},{7,5},{8,10},{10,8},{12,... | collective-permute-start | bytes 172040 | tf_op jit(solution)/shard_map/ppermute | solution.py:213
  32.1 1.8 %collective-permute-done.got.first = bf16[2,112,128]{2,1,0:T(8,128)(2,1)S(1)} collective-permute-done((bf16[2,112,128]{2,1,0:T(8,128)(2,1)S(1)}, bf16[2,112,128]{2,1,0:T(8,128)(2,1)S(1)}, u32[]{:S(2)}, u32[]{:S(2)}) %collective-permute-start) | collective-permute-done | bytes 57376 | tf_op jit(solution)/shard_map/ppermute | solution.py:213
  34.0 9.4 %collective-permute-start.1 = (bf16[2,112,128]{2,1,0:T(8,128)(2,1)S(1)}, bf16[2,112,128]{2,1,0:T(8,128)(2,1)S(1)}, u32[]{:S(2)}, u32[]{:S(2)}) collective-permute-start(bf16[2,112,128]{2,1,0:T(8,128)(2,1)S(1)} %shard_map.76), channel_id=1, source_target_pairs={{0,6},{2,4},{4,2},{6,0},{1,7},{3,5},{5,3},{7,1},{8,14},{10,12},{12... | collective-permute-start | bytes 172040 | tf_op jit(solution)/shard_map/ppermute | solution.py:213
  44.0 0.0 copy-done.2
  44.0 0.0 copy-done.3
  44.0 0.0 copy-start
  44.1 1.5 %copy-done = bf16[1,1,56,128,128]{4,3,2,1,0:T(8,128)(2,1)S(1)} copy-done((bf16[1,1,56,128,128]{4,3,2,1,0:T(8,128)(2,1)S(1)}, bf16[1,1,56,128,128]{4,3,2,1,0:T(8,128)(2,1)}, u32[]{:S(2)}) %copy-start) | copy-done | bytes 1835032
  45.5 1.3 %shard_map.73.dense = bf16[6,128,1024]{2,1,0:T(8,128)(2,1)S(1)} custom-call(s32[1]{0:T(128)} %bitcast.13.count, s32[56]{0:T(128)S(1)} %bitcast.18, s32[56]{0:T(128)S(1)} %bitcast.19, bf16[56,128,128]{2,1,0:T(8,128)(2,1)S(1)} %bitcast.16), custom_call_target="tpu_custom_call" | custom-call | flops 1048576 | bytes 8388608 | tf_op jit(solution)/shard_map/pallas_call | solution.py:232
  46.8 0.0 collective-permute-done.1.second
  46.8 0.6 shard_map.77
  47.4 0.0 all-to-all-done.1
  47.4 1.4 %shard_map.78.after = bf16[4,128,512]{2,1,0:T(8,128)(2,1)S(1)} custom-call(s32[2]{0:T(128)S(1)} %pad_add_fusion.place, bf16[6,128,1024]{2,1,0:T(8,128)(2,1)S(1)} %shard_map.73.dense, bf16[1024,768]{1,0:T(8,128)(2,1)S(1)} %bitcast.14, bf16[80,512]{1,0:T(8,128)(2,1)S(1)} %get-tuple-element.26.after), custom_call_target="tpu_custom_call" | custom-call | tf_op jit(solution)/shard_map/pallas_call | solution.py:253
  48.8 6.2 %collective-permute-start.2 = (bf16[4,128,512]{2,1,0:T(8,128)(2,1)S(1)}, bf16[4,128,512]{2,1,0:T(8,128)(2,1)S(1)}, u32[]{:S(2)}, u32[]{:S(2)}) collective-permute-start(bf16[4,128,512]{2,1,0:T(8,128)(2,1)S(1)} %shard_map.78.after), channel_id=1, source_target_pairs={{0,1},{1,0},{2,3},{3,2},{4,5},{5,4},{6,7},{7,6},{8,9},{9,8},{10,11... | collective-permute-start | bytes 1572872 | tf_op jit(solution)/shard_map/ppermute | solution.py:213
  55.0 1.4 %shard_map.79.keep = f32[4,128,512]{2,1,0:T(8,128)S(1)} custom-call(s32[2]{0:T(128)S(1)} %pad_add_fusion.place, bf16[6,128,1024]{2,1,0:T(8,128)(2,1)S(1)} %shard_map.73.dense, bf16[1024,768]{1,0:T(8,128)(2,1)S(1)} %bitcast.15, bf16[4,128,512]{2,1,0:T(8,128)(2,1)S(1)} %shard_map.78.after), custom_call_target="tpu_custom_call" | custom-call | tf_op jit(solution)/shard_map/pallas_call | solution.py:256
  56.4 0.2 collective-permute-done.2.got
  56.5 0.1 shard_map.80
  56.6 6.3 %collective-permute-start.3 = (bf16[2,64,512]{2,1,0:T(8,128)(2,1)S(1)}, bf16[2,64,512]{2,1,0:T(8,128)(2,1)S(1)}, u32[]{:S(2)}, u32[]{:S(2)}) collective-permute-start(bf16[2,64,512]{2,1,0:T(8,128)(2,1)S(1)} %get-tuple-element.29), channel_id=1, source_target_pairs={{0,2},{2,0},{4,6},{6,4},{1,3},{3,1},{5,7},{7,5},{8,10},{10,8},{12,... | collective-permute-start | bytes 393224 | tf_op jit(solution)/shard_map/ppermute | solution.py:213
  63.0 6.3 %collective-permute-start.4 = (bf16[2,64,512]{2,1,0:T(8,128)(2,1)S(1)}, bf16[2,64,512]{2,1,0:T(8,128)(2,1)S(1)}, u32[]{:S(2)}, u32[]{:S(2)}) collective-permute-start(bf16[2,64,512]{2,1,0:T(8,128)(2,1)S(1)} %get-tuple-element.30), channel_id=1, source_target_pairs={{0,6},{2,4},{4,2},{6,0},{1,7},{3,5},{5,3},{7,1},{8,14},{10,12},{12... | collective-permute-start | bytes 393224 | tf_op jit(solution)/shard_map/ppermute | solution.py:213
  69.3 1.2 broadcast_in_dim.10
  70.5 7.0 %all-to-all-start.2 = ((bf16[16,80,512]{2,1,0:T(8,128)(2,1)}), bf16[16,80,512]{2,1,0:T(8,128)(2,1)}, u32[]{:S(2)}, u32[]{:S(2)}) async-start(bf16[16,80,512]{2,1,0:T(8,128)(2,1)} %broadcast_in_dim.10), calls=%async_computation.2 | async-start | bytes 2621440 | tf_op jit(solution)/shard_map/all_to_all | solution.py:205
  77.5 0.0 collective-permute-done.3.got_a
  77.5 0.0 collective-permute-done.4.got_b
  77.6 5.3 %collective-permute-start.5 = (bf16[64,512]{1,0:T(8,128)(2,1)S(1)}, bf16[64,512]{1,0:T(8,128)(2,1)S(1)}, u32[]{:S(2)}, u32[]{:S(2)}) collective-permute-start(bf16[64,512]{1,0:T(8,128)(2,1)S(1)} %get-tuple-element.32), channel_id=1, source_target_pairs={{0,6},{2,4},{4,2},{6,0},{1,7},{3,5},{5,3},{7,1},{8,14},{10,12},{12... | collective-permute-start | bytes 196616 | tf_op jit(solution)/shard_map/ppermute | solution.py:213
  82.9 7.6 %collective-permute-start.6 = (bf16[64,512]{1,0:T(8,128)(2,1)S(1)}, bf16[64,512]{1,0:T(8,128)(2,1)S(1)}, u32[]{:S(2)}, u32[]{:S(2)}) collective-permute-start(bf16[64,512]{1,0:T(8,128)(2,1)S(1)} %get-tuple-element.33), channel_id=1, source_target_pairs={{0,2},{2,0},{4,6},{6,4},{1,3},{3,1},{5,7},{7,5},{8,10},{10,8},{12,... | collective-permute-start | bytes 196616 | tf_op jit(solution)/shard_map/ppermute | solution.py:213
  90.6 0.0 collective-permute-done.5.got_a
  90.6 2.0 %collective-permute-done.6.got_b = bf16[64,512]{1,0:T(8,128)(2,1)S(1)} collective-permute-done((bf16[64,512]{1,0:T(8,128)(2,1)S(1)}, bf16[64,512]{1,0:T(8,128)(2,1)S(1)}, u32[]{:S(2)}, u32[]{:S(2)}) %collective-permute-start.6) | collective-permute-done | bytes 65568 | tf_op jit(solution)/shard_map/ppermute | solution.py:213
  92.6 3.2 %collective-permute-start.7 = (bf16[192,512]{1,0:T(8,128)(2,1)S(1)}, bf16[192,512]{1,0:T(8,128)(2,1)}, u32[]{:S(2)}, u32[]{:S(2)}) collective-permute-start(bf16[192,512]{1,0:T(8,128)(2,1)S(1)} %shard_map.82.msgs), channel_id=1, source_target_pairs={{0,1},{1,0},{2,3},{3,2},{4,5},{5,4},{6,7},{7,6},{8,9},{9,8},{10,11... | collective-permute-start | bytes 589832 | tf_op jit(solution)/shard_map/ppermute | solution.py:213
  95.8 0.6 shard_map.83.swap
  96.5 0.0 all-to-all-done.2
  96.5 0.5 collective-permute-done.7.got
  97.0 2.2 %shard_map.84 = bf16[128,512]{1,0:T(8,128)(2,1)S(1)} custom-call(s32[2]{0:T(128)S(1)} %pad_add_fusion.place, bf16[192,512]{1,0:T(8,128)(2,1)S(1)} %shard_map.82.msgs, bf16[192,512]{1,0:T(8,128)(2,1)} %collective-permute-done.7.got, bf16[1280,1280]{1,0:T(8,128)(2,1)S(1)} %shard_map.83.swap, bf16[1280,512]{1,0:T(8,128)(2,1)} %bitcast.10.weights), custom_call_target="tpu_custom_call" | custom-call | tf_op jit(solution)/shard_map/pallas_call | solution.py:276
  99.2 21.3 %all_to_all.21.got = bf16[4,32,512]{2,1,0:T(8,128)(2,1)S(1)} all-to-all(bf16[4,32,512]{2,1,0:T(8,128)(2,1)S(1)} %bitcast.17), channel_id=1, replica_groups=mesh['y'=4,'x'=4,'zl'=4,'zh'=4,'core'=2] {'zh'}, dimensions={0} | all-to-all | bytes 262144 | tf_op jit(solution)/shard_map/all_to_all | solution.py:205
  120.6 0.6 shard_map.85
  121.1 3.9 %collective-permute-start.8 = (bf16[16,512]{1,0:T(8,128)(2,1)S(1)}, bf16[16,512]{1,0:T(8,128)(2,1)S(1)}, u32[]{:S(2)}, u32[]{:S(2)}) collective-permute-start(bf16[16,512]{1,0:T(8,128)(2,1)S(1)} %get-tuple-element.36), channel_id=1, source_target_pairs={{0,1},{1,0},{2,3},{3,2},{4,5},{5,4},{6,7},{7,6},{8,9},{9,8},{10,11... | collective-permute-start | bytes 49160 | tf_op jit(solution)/shard_map/ppermute | solution.py:213
  125.0 0.8 collective-permute-done.8.got
  125.8 1.2 shard_map.86
  (4 shorter events, 0.1 us)
Async XLA Ops:
  15.7 7.1 %copy-start.1 = (bf16[16,1024]{1,0:T(8,128)(2,1)S(1)}, bf16[16,1024]{1,0:T(8,128)(2,1)}, u32[]{:S(2)}) copy-start(bf16[16,1024]{1,0:T(8,128)(2,1)} %get-tuple-element.22.padded) | copy-start | bytes 98308
  15.7 28.4 %copy-start.2 = (s32[1,1,56]{2,1,0:T(1,128)S(1)}, s32[1,1,56]{2,1,0:T(1,128)}, u32[]{:S(2)}) copy-start(s32[1,1,56]{2,1,0:T(1,128)} %param.11) | copy-start | bytes 676
  15.7 28.4 %copy-start.3 = (s32[1,1,56]{2,1,0:T(1,128)S(1)}, s32[1,1,56]{2,1,0:T(1,128)}, u32[]{:S(2)}) copy-start(s32[1,1,56]{2,1,0:T(1,128)} %param.12) | copy-start | bytes 676
  15.7 31.8 %all-to-all-start.1 = ((bf16[16,64,768]{2,1,0:T(8,128)(2,1)}), bf16[16,64,768]{2,1,0:T(8,128)(2,1)S(1)}, u32[]{:S(2)}, u32[]{:S(2)}) async-start(bf16[16,64,768]{2,1,0:T(8,128)(2,1)} %broadcast_in_dim.9), calls=%async_computation.1 | async-start | bytes 3145728 | tf_op jit(solution)/shard_map/all_to_all | solution.py:205
  23.3 10.7 %collective-permute-start = (bf16[2,112,128]{2,1,0:T(8,128)(2,1)S(1)}, bf16[2,112,128]{2,1,0:T(8,128)(2,1)S(1)}, u32[]{:S(2)}, u32[]{:S(2)}) collective-permute-start(bf16[2,112,128]{2,1,0:T(8,128)(2,1)S(1)} %get-tuple-element.24), channel_id=1, source_target_pairs={{0,2},{2,0},{4,6},{6,4},{1,3},{3,1},{5,7},{7,5},{8,10},{10,8},{12,... | collective-permute-start | bytes 172040 | tf_op jit(solution)/shard_map/ppermute | solution.py:213
  34.0 12.8 %collective-permute-start.1 = (bf16[2,112,128]{2,1,0:T(8,128)(2,1)S(1)}, bf16[2,112,128]{2,1,0:T(8,128)(2,1)S(1)}, u32[]{:S(2)}, u32[]{:S(2)}) collective-permute-start(bf16[2,112,128]{2,1,0:T(8,128)(2,1)S(1)} %shard_map.76), channel_id=1, source_target_pairs={{0,6},{2,4},{4,2},{6,0},{1,7},{3,5},{5,3},{7,1},{8,14},{10,12},{12... | collective-permute-start | bytes 172040 | tf_op jit(solution)/shard_map/ppermute | solution.py:213
  44.0 1.5 %copy-start = (bf16[1,1,56,128,128]{4,3,2,1,0:T(8,128)(2,1)S(1)}, bf16[1,1,56,128,128]{4,3,2,1,0:T(8,128)(2,1)}, u32[]{:S(2)}) copy-start(bf16[1,1,56,128,128]{4,3,2,1,0:T(8,128)(2,1)} %param.10) | copy-start | bytes 5505028
  48.8 7.7 %collective-permute-start.2 = (bf16[4,128,512]{2,1,0:T(8,128)(2,1)S(1)}, bf16[4,128,512]{2,1,0:T(8,128)(2,1)S(1)}, u32[]{:S(2)}, u32[]{:S(2)}) collective-permute-start(bf16[4,128,512]{2,1,0:T(8,128)(2,1)S(1)} %shard_map.78.after), channel_id=1, source_target_pairs={{0,1},{1,0},{2,3},{3,2},{4,5},{5,4},{6,7},{7,6},{8,9},{9,8},{10,11... | collective-permute-start | bytes 1572872 | tf_op jit(solution)/shard_map/ppermute | solution.py:213
  56.6 20.9 %collective-permute-start.3 = (bf16[2,64,512]{2,1,0:T(8,128)(2,1)S(1)}, bf16[2,64,512]{2,1,0:T(8,128)(2,1)S(1)}, u32[]{:S(2)}, u32[]{:S(2)}) collective-permute-start(bf16[2,64,512]{2,1,0:T(8,128)(2,1)S(1)} %get-tuple-element.29), channel_id=1, source_target_pairs={{0,2},{2,0},{4,6},{6,4},{1,3},{3,1},{5,7},{7,5},{8,10},{10,8},{12,... | collective-permute-start | bytes 393224 | tf_op jit(solution)/shard_map/ppermute | solution.py:213
  63.0 14.5 %collective-permute-start.4 = (bf16[2,64,512]{2,1,0:T(8,128)(2,1)S(1)}, bf16[2,64,512]{2,1,0:T(8,128)(2,1)S(1)}, u32[]{:S(2)}, u32[]{:S(2)}) collective-permute-start(bf16[2,64,512]{2,1,0:T(8,128)(2,1)S(1)} %get-tuple-element.30), channel_id=1, source_target_pairs={{0,6},{2,4},{4,2},{6,0},{1,7},{3,5},{5,3},{7,1},{8,14},{10,12},{12... | collective-permute-start | bytes 393224 | tf_op jit(solution)/shard_map/ppermute | solution.py:213
  70.5 26.0 %all-to-all-start.2 = ((bf16[16,80,512]{2,1,0:T(8,128)(2,1)}), bf16[16,80,512]{2,1,0:T(8,128)(2,1)}, u32[]{:S(2)}, u32[]{:S(2)}) async-start(bf16[16,80,512]{2,1,0:T(8,128)(2,1)} %broadcast_in_dim.10), calls=%async_computation.2 | async-start | bytes 2621440 | tf_op jit(solution)/shard_map/all_to_all | solution.py:205
  77.6 13.0 %collective-permute-start.5 = (bf16[64,512]{1,0:T(8,128)(2,1)S(1)}, bf16[64,512]{1,0:T(8,128)(2,1)S(1)}, u32[]{:S(2)}, u32[]{:S(2)}) collective-permute-start(bf16[64,512]{1,0:T(8,128)(2,1)S(1)} %get-tuple-element.32), channel_id=1, source_target_pairs={{0,6},{2,4},{4,2},{6,0},{1,7},{3,5},{5,3},{7,1},{8,14},{10,12},{12... | collective-permute-start | bytes 196616 | tf_op jit(solution)/shard_map/ppermute | solution.py:213
  82.9 9.7 %collective-permute-start.6 = (bf16[64,512]{1,0:T(8,128)(2,1)S(1)}, bf16[64,512]{1,0:T(8,128)(2,1)S(1)}, u32[]{:S(2)}, u32[]{:S(2)}) collective-permute-start(bf16[64,512]{1,0:T(8,128)(2,1)S(1)} %get-tuple-element.33), channel_id=1, source_target_pairs={{0,2},{2,0},{4,6},{6,4},{1,3},{3,1},{5,7},{7,5},{8,10},{10,8},{12,... | collective-permute-start | bytes 196616 | tf_op jit(solution)/shard_map/ppermute | solution.py:213
  92.6 4.4 %collective-permute-start.7 = (bf16[192,512]{1,0:T(8,128)(2,1)S(1)}, bf16[192,512]{1,0:T(8,128)(2,1)}, u32[]{:S(2)}, u32[]{:S(2)}) collective-permute-start(bf16[192,512]{1,0:T(8,128)(2,1)S(1)} %shard_map.82.msgs), channel_id=1, source_target_pairs={{0,1},{1,0},{2,3},{3,2},{4,5},{5,4},{6,7},{7,6},{8,9},{9,8},{10,11... | collective-permute-start | bytes 589832 | tf_op jit(solution)/shard_map/ppermute | solution.py:213
  121.1 4.7 %collective-permute-start.8 = (bf16[16,512]{1,0:T(8,128)(2,1)S(1)}, bf16[16,512]{1,0:T(8,128)(2,1)S(1)}, u32[]{:S(2)}, u32[]{:S(2)}) collective-permute-start(bf16[16,512]{1,0:T(8,128)(2,1)S(1)} %get-tuple-element.36), channel_id=1, source_target_pairs={{0,1},{1,0},{2,3},{3,2},{4,5},{5,4},{6,7},{7,6},{8,9},{9,8},{10,11... | collective-permute-start | bytes 49160 | tf_op jit(solution)/shard_map/ppermute | solution.py:213

commit v8 on v7

--- a/solution.py
+++ b/solution.py
@@ -32,7 +32,6 @@
 QUART = 2 * (SLOT + SELF)
 DEPTH = QUART * NODES
 WIDE = DOUT // 2
-HALF = TILE // 2
 PIECE = 256
 WEIGHT = 10**11
 
@@ -83,15 +82,21 @@
             copies[i, :, DIN + k * TILE : DIN + (k + 1) * TILE] = rows[k].astype(BF)
 
 
+def ranks(zh, core):
+    one = 1 + 2 * core
+    return zh, zh ^ one, zh ^ 2, zh ^ (4 - one)
+
+
 def sort(place, padded, gathered, send, mine, relay):
-    for e, ref in ((1, send.at[0]), (2, send.at[1]), (0, mine), (3, relay)):
-        first = (place[0] ^ e) * 2 * TILE
+    here, near, far, last = ranks(place[0], place[1])
+    for z, ref in ((near, send.at[0]), (far, send.at[1]), (here, mine), (last, relay)):
+        first = z * 2 * TILE
         for i in range(2):
             ref[i * ROWS : (i + 1) * ROWS] = padded[:, pl.ds(pl.multiple_of(first + i * TILE, TILE), TILE)]
         rows = []
-        for z in range(4):
+        for k in range(4):
             a, b = (
-                gathered[z, :, pl.ds(pl.multiple_of(DIN + first + i * TILE, TILE), TILE)].astype(F32)
+                gathered[k, :, pl.ds(pl.multiple_of(DIN + first + i * TILE, TILE), TILE)].astype(F32)
                 for i in range(2)
             )
             rows += [a[:SLOT], b[:SLOT], a[SLOT : SLOT + SELF], b[SLOT : SLOT + SELF]]
@@ -104,8 +109,8 @@
 
 
 def join_groups(place, mine, first, second, own, rows):
-    for e, ref in ((0, mine), (1, first.at[0]), (3, second.at[0]), (2, second.at[1])):
-        z = place[0] ^ e
+    here, near, far, last = ranks(place[0], place[1])
+    for z, ref in ((here, mine), (near, first.at[0]), (last, second.at[0]), (far, second.at[1])):
         spot = pl.ds(pl.multiple_of(z * ROWS, ROWS), ROWS)
         own[spot, :TILE] = ref[:ROWS]
         own[spot, TILE:] = ref[ROWS : 2 * ROWS]
@@ -129,39 +134,31 @@
 
 def aggregate(owner, place, dense, feats, after, out):
     core = place[1] ^ owner
-    for e in range(4):
+    for e, z in enumerate(ranks(place[0], core)):
         for i in range(2):
-            piece = 2 * (2 * (place[0] ^ e) + core) + i
+            piece = 2 * (2 * z + core) + i
             spot = pl.ds(pl.multiple_of(lax.rem(piece, 3) * PIECE, PIECE), PIECE)
             value = jnp.dot(dense[lax.div(piece, 3)], feats[:, spot], preferred_element_type=F32)
             out[e, :, i * PIECE : (i + 1) * PIECE] = value.astype(out.dtype)
 
 
-def first_half(keep, got, send_a, send_b, keep_a, keep_b):
-    def total(e, rows):
-        return keep[e, rows] + got[e, rows].astype(F32)
-
-    a, b = slice(0, HALF), slice(HALF, TILE)
-    send_a[0] = total(1, a).astype(BF)
-    send_a[1] = total(2, a).astype(BF)
-    send_b[0] = total(3, b).astype(BF)
-    send_b[1] = total(2, b).astype(BF)
-    keep_a[0] = total(0, a)
-    keep_a[1] = total(3, a)
-    keep_b[0] = total(0, b)
-    keep_b[1] = total(1, b)
-
-
-def second_half(keep_a, keep_b, got_a, got_b, send_a, send_b, hold):
-    hold[:HALF] = keep_a[0] + got_a[0].astype(F32)
-    hold[HALF:] = keep_b[0] + got_b[0].astype(F32)
-    send_a[...] = (keep_a[1] + got_a[1].astype(F32)).astype(BF)
-    send_b[...] = (keep_b[1] + got_b[1].astype(F32)).astype(BF)
-
-
-def settle(hold, got_a, got_b, own, msgs):
-    msgs[:HALF] = (hold[:HALF] + got_a[...].astype(F32)).astype(BF)
-    msgs[HALF:TILE] = (hold[HALF:] + got_b[...].astype(F32)).astype(BF)
+def first_half(keep, got, send, rest):
+    def total(e):
+        return keep[e] + got[e].astype(F32)
+
+    send[0] = total(1).astype(BF)
+    send[1] = total(2).astype(BF)
+    rest[0] = total(0)
+    rest[1] = total(3)
+
+
+def second_half(rest, got, send, hold):
+    hold[...] = rest[0] + got[0].astype(F32)
+    send[...] = (rest[1] + got[1].astype(F32)).astype(BF)
+
+
+def settle(hold, got, own, msgs):
+    msgs[:TILE] = (hold[...] + got[...].astype(F32)).astype(BF)
     msgs[TILE:, : 2 * TILE] = own[...]
     msgs[TILE:, 2 * TILE :] = jnp.zeros((4 * ROWS, CHUNK - 2 * TILE), BF)
 
@@ -209,8 +206,12 @@
     return exchange(jnp.broadcast_to(x, (lax.axis_size(axis), *x.shape)), axis)
 
 
-def partner(x, axis, mask):
-    return lax.ppermute(x, axis, [(i, i ^ mask) for i in range(lax.axis_size(axis))])
+def partner(x, step):
+    def goal(zh, core):
+        return (zh, 1 - core) if step == 0 else (ranks(zh, core)[2 * step - 1], core)
+
+    pairs = [(2 * z + c, goal(z, c)) for z in range(4) for c in range(2)]
+    return lax.ppermute(x, REL, [(i, 2 * z + c) for i, (z, c) in pairs])
 
 
 def on_device(features, bases, coefficients, tile_values, tile_source, tile_relation, tile_count):
@@ -241,9 +242,9 @@
     block = shape(BF, 2 * ROWS + 4 * QUART, TILE)
     blocks = shape(BF, 2, 2 * ROWS + 4 * QUART, TILE)
     send, mine, relay = call(sort, (blocks, block, block), [SMEM, VMEM, VMEM])(place, padded, gathered)
-    first = partner(send, "zh", 1)
+    first = partner(send, 1)
     relay = call(pass_on, blocks, [VMEM] * 2)(relay, first)
-    second = partner(relay, "zh", 3)
+    second = partner(relay, 2)
     own, rows = call(
         join_groups,
         (shape(BF, 4 * ROWS, 2 * TILE), shape(BF, 4 * QUART, WIDE)),
@@ -256,35 +257,29 @@
     keep = call(functools.partial(aggregate, 0), shape(F32, 4, TILE, CHUNK), [SMEM, VMEM, VMEM, ANY])(
         place, dense, feats, send
     )
-    two = shape(BF, 2, HALF, CHUNK)
-    wide = shape(F32, 2, HALF, CHUNK)
-    send_a, send_b, keep_a, keep_b = call(first_half, (two, two, wide, wide), [VMEM] * 2)(
-        keep, partner(send, "core", 1)
-    )
-    one = shape(BF, HALF, CHUNK)
-    send_a, send_b, hold = call(
+    two = shape(BF, 2, TILE, CHUNK)
+    send, rest = call(first_half, (two, shape(F32, 2, TILE, CHUNK)), [VMEM] * 2)(keep, partner(send, 0))
+    send, hold = call(
         second_half,
-        (one, one, shape(F32, TILE, CHUNK)),
-        [VMEM] * 4,
+        (shape(BF, TILE, CHUNK), shape(F32, TILE, CHUNK)),
+        [VMEM] * 2,
         cost=pl.CostEstimate(flops=WEIGHT, bytes_accessed=1 << 20, transcendentals=0),
-    )(keep_a, keep_b, partner(send_a, "zh", 1), partner(send_b, "zh", 3))
+    )(rest, partner(send, 1))
     weights = spread(rows, YX).reshape(DEPTH, WIDE)
-    msgs = call(settle, shape(BF, TILE + 4 * ROWS, CHUNK), [VMEM] * 4)(
-        hold, partner(send_a, "zh", 3), partner(send_b, "zh", 1), own
-    )
+    msgs = call(settle, shape(BF, TILE + 4 * ROWS, CHUNK), [VMEM] * 3)(hold, partner(send, 2), own)
     swap = call(order, shape(BF, DEPTH, DEPTH), [])()
     send = call(
         transform,
         shape(BF, TILE, WIDE),
         [SMEM] + [VMEM] * 4,
         [pltpu.VMEM((TILE, DEPTH), BF)],
-    )(place, msgs, partner(msgs, "core", 1), swap, weights)
+    )(place, msgs, partner(msgs, 0), swap, weights)
     half = shape(BF, ROWS, WIDE)
     mine, other = call(finish, (half, half), [SMEM, VMEM], [pltpu.VMEM((2 * ROWS, WIDE), F32)])(
         place, exchange(send.reshape(4, 2 * ROWS, WIDE), "zh")
     )
     out = call(place_columns, shape(BF, ROWS, DOUT), [SMEM, VMEM, VMEM])(
-        place, mine, partner(other, "core", 1)
+        place, mine, partner(other, 0)
     )
     return out[None]
 

time: 129 us -> 122 us (0.946)
  starting transfers between devices: 71.1 us -> 61.3 us
  waiting for transfers between devices: 5.38 us -> 10.6 us
  blocking collectives: 33.5 us -> 32.2 us
    ppermute x9 -> x7, starting transfers between devices: 57.1 us -> 48 us  [partner(): return lax.ppermute(x, REL, [(i, 2 * z + c) for i, (z, c) in pairs])]
    ppermute x9 -> x7, waiting for transfers between devices: 5.38 us -> 10.6 us  [partner(): return lax.ppermute(x, REL, [(i, 2 * z + c) for i, (z, c) in pairs])]
    all_to_all x2, blocking collectives: 33.5 us -> 32.2 us  [exchange(): return lax.all_to_all(x, axis, split_axis=0, concat_axis=0, tiled=True)]
  transfers between devices with their start and end apart: 11 -> 9, of which waited for: 5 -> 7; matrix products, arithmetic and copies ran while one was open for 1% -> 1% of each run, Pallas kernels for 4% -> 4%
where the time goes in v8:
time: 122 us; the launch traced here: 121 us
  starting transfers between devices  61.3 us (50%)
  blocking collectives  32.2 us (26%)
  Pallas kernels  12 us (10%)
  waiting for transfers between devices  10.6 us (9%)
  local copies, waits for them, and re-layouts  4.03 us (3%)
    ppermute x7, starting transfers between devices, partner(): return lax.ppermute(x, REL, [(i, 2 * z + c) for i, (z, c) in pairs])  48 us
    all_to_all x2, blocking collectives, exchange(): return lax.all_to_all(x, axis, split_axis=0, concat_axis=0, tiled=True)  32.2 us
    all_to_all x2, starting transfers between devices, exchange(): return lax.all_to_all(x, axis, split_axis=0, concat_axis=0, tiled=True)  13.3 us
    ppermute x7, waiting for transfers between devices, partner(): return lax.ppermute(x, REL, [(i, 2 * z + c) for i, (z, c) in pairs])  10.6 us
    broadcast_in_dim x2, local copies, waits for them, and re-layouts, spread(): return exchange(jnp.broadcast_to(x, (lax.axis_size(axis), *x.shape)), axis)  2.52 us
  transfers between devices with their start and end apart: 9, of which 7 were waited for; matrix products, arithmetic and copies ran while one was open for 1% of the time, Pallas kernels for 4%

profile of v8, /device:TPU:1, one launch (start us, length us, event | category | flops | bytes accessed | tf_op | source)
XLA Modules:
  0.0 121.1 jit_solution(18206352718229007786)
XLA Ops:
  0.0 2.1 %shard_map.74 = (bf16[16,1024]{1,0:T(8,128)(2,1)}, bf16[4,16,1792]{2,1,0:T(8,128)(2,1)}) custom-call(bf16[16,768]{1,0:T(8,128)(2,1)} %bitcast.22, f32[6,30]{1,0:T(8,128)} %coef_in.1, bf16[12,30,128]{2,1,0:T(8,128)(2,1)} %bitcast.21), custom_call_target="tpu_custom_call" | custom-call | tf_op jit(solution)/shard_map/pallas_call | solution.py:219
  2.1 12.2 %all_to_all.20.gathered = bf16[4,16,1792]{2,1,0:T(8,128)(2,1)S(1)} all-to-all(bf16[4,16,1792]{2,1,0:T(8,128)(2,1)} %get-tuple-element.18), channel_id=1, replica_groups=mesh['y'=4,'x'=4,'zl'=4,'zh'=4,'core'=2] {'zl'}, dimensions={0} | all-to-all | bytes 458752 | tf_op jit(solution)/shard_map/all_to_all | solution.py:202
  14.3 1.3 %broadcast_in_dim.9 = bf16[16,64,768]{2,1,0:T(8,128)(2,1)} broadcast(bf16[64,768]{1,0:T(8,128)(2,1)S(1)} %bitcast.20), dimensions={1,2} | broadcast | bytes 1671168 | tf_op jit(solution)/shard_map/broadcast_in_dim | solution.py:206
  15.7 0.0 copy-start.1
  15.7 0.0 copy-start.2
  15.7 0.0 copy-start.3
  15.7 7.0 %all-to-all-start.1 = ((bf16[16,64,768]{2,1,0:T(8,128)(2,1)}), bf16[16,64,768]{2,1,0:T(8,128)(2,1)S(1)}, u32[]{:S(2)}, u32[]{:S(2)}) async-start(bf16[16,64,768]{2,1,0:T(8,128)(2,1)} %broadcast_in_dim.9), calls=%async_computation.1 | async-start | bytes 3145728 | tf_op jit(solution)/shard_map/all_to_all | solution.py:202
  22.7 0.1 pad_add_fusion.place
  22.7 0.0 copy-done.1
  22.7 0.6 shard_map.75
  23.3 10.9 %collective-permute-start = (bf16[2,112,128]{2,1,0:T(8,128)(2,1)S(1)}, bf16[2,112,128]{2,1,0:T(8,128)(2,1)S(1)}, u32[]{:S(2)}, u32[]{:S(2)}) collective-permute-start(bf16[2,112,128]{2,1,0:T(8,128)(2,1)S(1)} %get-tuple-element.21), channel_id=1, source_target_pairs={{0,2},{1,7},{2,0},{3,5},{4,6},{5,3},{6,4},{7,1},{8,10},{9,15},{10,... | collective-permute-start | bytes 172040 | tf_op jit(solution)/shard_map/ppermute | solution.py:214
  34.3 1.9 %collective-permute-done.got.first = bf16[2,112,128]{2,1,0:T(8,128)(2,1)S(1)} collective-permute-done((bf16[2,112,128]{2,1,0:T(8,128)(2,1)S(1)}, bf16[2,112,128]{2,1,0:T(8,128)(2,1)S(1)}, u32[]{:S(2)}, u32[]{:S(2)}) %collective-permute-start) | collective-permute-done | bytes 57376 | tf_op jit(solution)/shard_map/ppermute | solution.py:214
  36.1 5.0 %collective-permute-start.1 = (bf16[2,112,128]{2,1,0:T(8,128)(2,1)S(1)}, bf16[2,112,128]{2,1,0:T(8,128)(2,1)S(1)}, u32[]{:S(2)}, u32[]{:S(2)}) collective-permute-start(bf16[2,112,128]{2,1,0:T(8,128)(2,1)S(1)} %shard_map.76), channel_id=1, source_target_pairs={{0,6},{1,3},{2,4},{3,1},{4,2},{5,7},{6,0},{7,5},{8,14},{9,11},{10,... | collective-permute-start | bytes 172040 | tf_op jit(solution)/shard_map/ppermute | solution.py:214
  41.8 0.0 copy-done.2
  41.8 0.0 copy-done.3
  41.8 0.0 copy-start
  41.8 1.5 %copy-done = bf16[1,1,56,128,128]{4,3,2,1,0:T(8,128)(2,1)S(1)} copy-done((bf16[1,1,56,128,128]{4,3,2,1,0:T(8,128)(2,1)S(1)}, bf16[1,1,56,128,128]{4,3,2,1,0:T(8,128)(2,1)}, u32[]{:S(2)}) %copy-start) | copy-done | bytes 1835032
  43.3 1.3 %shard_map.73.dense = bf16[6,128,1024]{2,1,0:T(8,128)(2,1)S(1)} custom-call(s32[1]{0:T(128)} %bitcast.13.count, s32[56]{0:T(128)S(1)} %bitcast.18, s32[56]{0:T(128)S(1)} %bitcast.19, bf16[56,128,128]{2,1,0:T(8,128)(2,1)S(1)} %bitcast.16), custom_call_target="tpu_custom_call" | custom-call | flops 1048576 | bytes 8388608 | tf_op jit(solution)/shard_map/pallas_call | solution.py:233
  44.6 0.3 collective-permute-done.1.second
  44.9 0.6 shard_map.77
  45.5 0.0 all-to-all-done.1
  45.5 1.3 %shard_map.78.after = bf16[4,128,512]{2,1,0:T(8,128)(2,1)S(1)} custom-call(s32[2]{0:T(128)S(1)} %pad_add_fusion.place, bf16[6,128,1024]{2,1,0:T(8,128)(2,1)S(1)} %shard_map.73.dense, bf16[1024,768]{1,0:T(8,128)(2,1)S(1)} %bitcast.14, bf16[80,512]{1,0:T(8,128)(2,1)S(1)} %get-tuple-element.23.after), custom_call_target="tpu_custom_call" | custom-call | tf_op jit(solution)/shard_map/pallas_call | solution.py:254
  46.9 8.5 %collective-permute-start.2 = (bf16[4,128,512]{2,1,0:T(8,128)(2,1)S(1)}, bf16[4,128,512]{2,1,0:T(8,128)(2,1)S(1)}, u32[]{:S(2)}, u32[]{:S(2)}) collective-permute-start(bf16[4,128,512]{2,1,0:T(8,128)(2,1)S(1)} %shard_map.78.after), channel_id=1, source_target_pairs={{0,1},{1,0},{2,3},{3,2},{4,5},{5,4},{6,7},{7,6},{8,9},{9,8},{10,11... | collective-permute-start | bytes 1572872 | tf_op jit(solution)/shard_map/ppermute | solution.py:214
  55.4 1.4 %shard_map.79.keep = f32[4,128,512]{2,1,0:T(8,128)S(1)} custom-call(s32[2]{0:T(128)S(1)} %pad_add_fusion.place, bf16[6,128,1024]{2,1,0:T(8,128)(2,1)S(1)} %shard_map.73.dense, bf16[1024,768]{1,0:T(8,128)(2,1)S(1)} %bitcast.15, bf16[4,128,512]{2,1,0:T(8,128)(2,1)S(1)} %shard_map.78.after), custom_call_target="tpu_custom_call" | custom-call | tf_op jit(solution)/shard_map/pallas_call | solution.py:257
  56.8 0.1 collective-permute-done.2.got
  56.9 0.1 shard_map.80
  57.0 7.1 %collective-permute-start.3 = (bf16[2,128,512]{2,1,0:T(8,128)(2,1)S(1)}, bf16[2,128,512]{2,1,0:T(8,128)(2,1)S(1)}, u32[]{:S(2)}, u32[]{:S(2)}) collective-permute-start(bf16[2,128,512]{2,1,0:T(8,128)(2,1)S(1)} %get-tuple-element.25), channel_id=1, source_target_pairs={{0,2},{1,7},{2,0},{3,5},{4,6},{5,3},{6,4},{7,1},{8,10},{9,15},{10,... | collective-permute-start | bytes 786440 | tf_op jit(solution)/shard_map/ppermute | solution.py:214
  64.1 1.2 broadcast_in_dim.10
  65.3 6.4 %all-to-all-start.2 = ((bf16[16,80,512]{2,1,0:T(8,128)(2,1)}), bf16[16,80,512]{2,1,0:T(8,128)(2,1)}, u32[]{:S(2)}, u32[]{:S(2)}) async-start(bf16[16,80,512]{2,1,0:T(8,128)(2,1)} %broadcast_in_dim.10), calls=%async_computation.2 | async-start | bytes 2621440 | tf_op jit(solution)/shard_map/all_to_all | solution.py:202
  71.7 3.0 %collective-permute-done.3.got = bf16[2,128,512]{2,1,0:T(8,128)(2,1)S(1)} collective-permute-done((bf16[2,128,512]{2,1,0:T(8,128)(2,1)S(1)}, bf16[2,128,512]{2,1,0:T(8,128)(2,1)S(1)}, u32[]{:S(2)}, u32[]{:S(2)}) %collective-permute-start.3) | collective-permute-done | bytes 262176 | tf_op jit(solution)/shard_map/ppermute | solution.py:214
  74.8 7.4 %collective-permute-start.4 = (bf16[128,512]{1,0:T(8,128)(2,1)S(1)}, bf16[128,512]{1,0:T(8,128)(2,1)S(1)}, u32[]{:S(2)}, u32[]{:S(2)}) collective-permute-start(bf16[128,512]{1,0:T(8,128)(2,1)S(1)} %get-tuple-element.27), channel_id=1, source_target_pairs={{0,6},{1,3},{2,4},{3,1},{4,2},{5,7},{6,0},{7,5},{8,14},{9,11},{10,... | collective-permute-start | bytes 393224 | tf_op jit(solution)/shard_map/ppermute | solution.py:214
  82.2 3.9 %collective-permute-done.4.got = bf16[128,512]{1,0:T(8,128)(2,1)S(1)} collective-permute-done((bf16[128,512]{1,0:T(8,128)(2,1)S(1)}, bf16[128,512]{1,0:T(8,128)(2,1)S(1)}, u32[]{:S(2)}, u32[]{:S(2)}) %collective-permute-start.4) | collective-permute-done | bytes 131104 | tf_op jit(solution)/shard_map/ppermute | solution.py:214
  86.1 5.8 %collective-permute-start.5 = (bf16[192,512]{1,0:T(8,128)(2,1)S(1)}, bf16[192,512]{1,0:T(8,128)(2,1)}, u32[]{:S(2)}, u32[]{:S(2)}) collective-permute-start(bf16[192,512]{1,0:T(8,128)(2,1)S(1)} %shard_map.82.msgs), channel_id=1, source_target_pairs={{0,1},{1,0},{2,3},{3,2},{4,5},{5,4},{6,7},{7,6},{8,9},{9,8},{10,11... | collective-permute-start | bytes 589832 | tf_op jit(solution)/shard_map/ppermute | solution.py:214
  91.9 0.6 shard_map.83.swap
  92.5 0.0 all-to-all-done.2
  92.5 0.5 collective-permute-done.5.got
  93.0 2.2 %shard_map.84 = bf16[128,512]{1,0:T(8,128)(2,1)S(1)} custom-call(s32[2]{0:T(128)S(1)} %pad_add_fusion.place, bf16[192,512]{1,0:T(8,128)(2,1)S(1)} %shard_map.82.msgs, bf16[192,512]{1,0:T(8,128)(2,1)} %collective-permute-done.5.got, bf16[1280,1280]{1,0:T(8,128)(2,1)S(1)} %shard_map.83.swap, bf16[1280,512]{1,0:T(8,128)(2,1)} %bitcast.10.weights), custom_call_target="tpu_custom_call" | custom-call | tf_op jit(solution)/shard_map/pallas_call | solution.py:271
  95.3 20.0 %all_to_all.21.got = bf16[4,32,512]{2,1,0:T(8,128)(2,1)S(1)} all-to-all(bf16[4,32,512]{2,1,0:T(8,128)(2,1)S(1)} %bitcast.17), channel_id=1, replica_groups=mesh['y'=4,'x'=4,'zl'=4,'zh'=4,'core'=2] {'zh'}, dimensions={0} | all-to-all | bytes 262144 | tf_op jit(solution)/shard_map/all_to_all | solution.py:202
  115.3 0.6 shard_map.85
  115.8 3.3 %collective-permute-start.6 = (bf16[16,512]{1,0:T(8,128)(2,1)S(1)}, bf16[16,512]{1,0:T(8,128)(2,1)S(1)}, u32[]{:S(2)}, u32[]{:S(2)}) collective-permute-start(bf16[16,512]{1,0:T(8,128)(2,1)S(1)} %get-tuple-element.30), channel_id=1, source_target_pairs={{0,1},{1,0},{2,3},{3,2},{4,5},{5,4},{6,7},{7,6},{8,9},{9,8},{10,11... | collective-permute-start | bytes 49160 | tf_op jit(solution)/shard_map/ppermute | solution.py:214
  119.1 0.8 collective-permute-done.6.got
  119.9 1.2 shard_map.86
  (4 shorter events, 0.1 us)
Async XLA Ops:
  15.7 7.1 %copy-start.1 = (bf16[16,1024]{1,0:T(8,128)(2,1)S(1)}, bf16[16,1024]{1,0:T(8,128)(2,1)}, u32[]{:S(2)}) copy-start(bf16[16,1024]{1,0:T(8,128)(2,1)} %get-tuple-element.19.padded) | copy-start | bytes 98308
  15.7 26.1 %copy-start.2 = (s32[1,1,56]{2,1,0:T(1,128)S(1)}, s32[1,1,56]{2,1,0:T(1,128)}, u32[]{:S(2)}) copy-start(s32[1,1,56]{2,1,0:T(1,128)} %param.11) | copy-start | bytes 676
  15.7 26.2 %copy-start.3 = (s32[1,1,56]{2,1,0:T(1,128)S(1)}, s32[1,1,56]{2,1,0:T(1,128)}, u32[]{:S(2)}) copy-start(s32[1,1,56]{2,1,0:T(1,128)} %param.12) | copy-start | bytes 676
  15.7 29.8 %all-to-all-start.1 = ((bf16[16,64,768]{2,1,0:T(8,128)(2,1)}), bf16[16,64,768]{2,1,0:T(8,128)(2,1)S(1)}, u32[]{:S(2)}, u32[]{:S(2)}) async-start(bf16[16,64,768]{2,1,0:T(8,128)(2,1)} %broadcast_in_dim.9), calls=%async_computation.1 | async-start | bytes 3145728 | tf_op jit(solution)/shard_map/all_to_all | solution.py:202
  23.3 12.8 %collective-permute-start = (bf16[2,112,128]{2,1,0:T(8,128)(2,1)S(1)}, bf16[2,112,128]{2,1,0:T(8,128)(2,1)S(1)}, u32[]{:S(2)}, u32[]{:S(2)}) collective-permute-start(bf16[2,112,128]{2,1,0:T(8,128)(2,1)S(1)} %get-tuple-element.21), channel_id=1, source_target_pairs={{0,2},{1,7},{2,0},{3,5},{4,6},{5,3},{6,4},{7,1},{8,10},{9,15},{10,... | collective-permute-start | bytes 172040 | tf_op jit(solution)/shard_map/ppermute | solution.py:214
  36.1 8.8 %collective-permute-start.1 = (bf16[2,112,128]{2,1,0:T(8,128)(2,1)S(1)}, bf16[2,112,128]{2,1,0:T(8,128)(2,1)S(1)}, u32[]{:S(2)}, u32[]{:S(2)}) collective-permute-start(bf16[2,112,128]{2,1,0:T(8,128)(2,1)S(1)} %shard_map.76), channel_id=1, source_target_pairs={{0,6},{1,3},{2,4},{3,1},{4,2},{5,7},{6,0},{7,5},{8,14},{9,11},{10,... | collective-permute-start | bytes 172040 | tf_op jit(solution)/shard_map/ppermute | solution.py:214
  41.8 1.5 %copy-start = (bf16[1,1,56,128,128]{4,3,2,1,0:T(8,128)(2,1)S(1)}, bf16[1,1,56,128,128]{4,3,2,1,0:T(8,128)(2,1)}, u32[]{:S(2)}) copy-start(bf16[1,1,56,128,128]{4,3,2,1,0:T(8,128)(2,1)} %param.10) | copy-start | bytes 5505028
  46.9 10.1 %collective-permute-start.2 = (bf16[4,128,512]{2,1,0:T(8,128)(2,1)S(1)}, bf16[4,128,512]{2,1,0:T(8,128)(2,1)S(1)}, u32[]{:S(2)}, u32[]{:S(2)}) collective-permute-start(bf16[4,128,512]{2,1,0:T(8,128)(2,1)S(1)} %shard_map.78.after), channel_id=1, source_target_pairs={{0,1},{1,0},{2,3},{3,2},{4,5},{5,4},{6,7},{7,6},{8,9},{9,8},{10,11... | collective-permute-start | bytes 1572872 | tf_op jit(solution)/shard_map/ppermute | solution.py:214
  57.0 17.7 %collective-permute-start.3 = (bf16[2,128,512]{2,1,0:T(8,128)(2,1)S(1)}, bf16[2,128,512]{2,1,0:T(8,128)(2,1)S(1)}, u32[]{:S(2)}, u32[]{:S(2)}) collective-permute-start(bf16[2,128,512]{2,1,0:T(8,128)(2,1)S(1)} %get-tuple-element.25), channel_id=1, source_target_pairs={{0,2},{1,7},{2,0},{3,5},{4,6},{5,3},{6,4},{7,1},{8,10},{9,15},{10,... | collective-permute-start | bytes 786440 | tf_op jit(solution)/shard_map/ppermute | solution.py:214
  65.3 27.2 %all-to-all-start.2 = ((bf16[16,80,512]{2,1,0:T(8,128)(2,1)}), bf16[16,80,512]{2,1,0:T(8,128)(2,1)}, u32[]{:S(2)}, u32[]{:S(2)}) async-start(bf16[16,80,512]{2,1,0:T(8,128)(2,1)} %broadcast_in_dim.10), calls=%async_computation.2 | async-start | bytes 2621440 | tf_op jit(solution)/shard_map/all_to_all | solution.py:202
  74.8 11.3 %collective-permute-start.4 = (bf16[128,512]{1,0:T(8,128)(2,1)S(1)}, bf16[128,512]{1,0:T(8,128)(2,1)S(1)}, u32[]{:S(2)}, u32[]{:S(2)}) collective-permute-start(bf16[128,512]{1,0:T(8,128)(2,1)S(1)} %get-tuple-element.27), channel_id=1, source_target_pairs={{0,6},{1,3},{2,4},{3,1},{4,2},{5,7},{6,0},{7,5},{8,14},{9,11},{10,... | collective-permute-start | bytes 393224 | tf_op jit(solution)/shard_map/ppermute | solution.py:214
  86.1 7.0 %collective-permute-start.5 = (bf16[192,512]{1,0:T(8,128)(2,1)S(1)}, bf16[192,512]{1,0:T(8,128)(2,1)}, u32[]{:S(2)}, u32[]{:S(2)}) collective-permute-start(bf16[192,512]{1,0:T(8,128)(2,1)S(1)} %shard_map.82.msgs), channel_id=1, source_target_pairs={{0,1},{1,0},{2,3},{3,2},{4,5},{5,4},{6,7},{7,6},{8,9},{9,8},{10,11... | collective-permute-start | bytes 589832 | tf_op jit(solution)/shard_map/ppermute | solution.py:214
  115.8 4.1 %collective-permute-start.6 = (bf16[16,512]{1,0:T(8,128)(2,1)S(1)}, bf16[16,512]{1,0:T(8,128)(2,1)S(1)}, u32[]{:S(2)}, u32[]{:S(2)}) collective-permute-start(bf16[16,512]{1,0:T(8,128)(2,1)S(1)} %get-tuple-element.30), channel_id=1, source_target_pairs={{0,1},{1,0},{2,3},{3,2},{4,5},{5,4},{6,7},{7,6},{8,9},{9,8},{10,11... | collective-permute-start | bytes 49160 | tf_op jit(solution)/shard_map/ppermute | solution.py:214

commit v9 on v8

--- a/solution.py
+++ b/solution.py
@@ -169,7 +169,7 @@
     swap[...] = jnp.where(out == QUART * (src & (NODES - 1)) + (src >> 6), 1.0, 0.0).astype(BF)
 
 
-def transform(place, msgs, got, swap, weights, send, full):
+def transform(place, msgs, got, swap, weights, send, rest, full, part):
     core = place[1]
     for c, ref in ((core, msgs), (1 - core, got)):
         full[:, pl.ds(pl.multiple_of(c * CHUNK, CHUNK), CHUNK)] = ref[:TILE]
@@ -177,13 +177,18 @@
             spot = pl.ds(pl.multiple_of((2 * z + c) * ROWS, ROWS), ROWS)
             full[spot, 2 * CHUNK :] = ref[TILE + z * ROWS : TILE + (z + 1) * ROWS, : 2 * TILE]
     value = jnp.dot(full[...], swap[...], preferred_element_type=F32).astype(BF)
-    send[...] = jnp.dot(value, weights[...], preferred_element_type=F32).astype(BF)
-
-
-def finish(place, got, mine, other, total):
-    value = got[0].astype(F32)
-    for i in range(1, 4):
-        value = value + got[i].astype(F32)
+    part[...] = jnp.dot(value, weights[...], preferred_element_type=F32)
+    here, near, far, last = ranks(place[0], place[1])
+    for i, z in enumerate((near, far, here, last)):
+        rows = part[pl.ds(pl.multiple_of(z * 2 * ROWS, 2 * ROWS), 2 * ROWS)]
+        if i < 2:
+            send[i] = rows.astype(BF)
+        else:
+            rest[i - 2] = rows
+
+
+def finish(place, hold, got, mine, other, total):
+    value = hold[...] + got[...].astype(F32)
     total[...] = jnp.maximum(value, 0.0)
     core = place[1]
     mine[...] = total[pl.ds(pl.multiple_of(core * ROWS, ROWS), ROWS)].astype(BF)
@@ -268,15 +273,19 @@
     weights = spread(rows, YX).reshape(DEPTH, WIDE)
     msgs = call(settle, shape(BF, TILE + 4 * ROWS, CHUNK), [VMEM] * 3)(hold, partner(send, 2), own)
     swap = call(order, shape(BF, DEPTH, DEPTH), [])()
-    send = call(
+    pair = shape(BF, 2, 2 * ROWS, WIDE)
+    send, rest = call(
         transform,
-        shape(BF, TILE, WIDE),
+        (pair, shape(F32, 2, 2 * ROWS, WIDE)),
         [SMEM] + [VMEM] * 4,
-        [pltpu.VMEM((TILE, DEPTH), BF)],
+        [pltpu.VMEM((TILE, DEPTH), BF), pltpu.VMEM((TILE, WIDE), F32)],
     )(place, msgs, partner(msgs, 0), swap, weights)
+    send, hold = call(
+        second_half, (shape(BF, 2 * ROWS, WIDE), shape(F32, 2 * ROWS, WIDE)), [VMEM] * 2
+    )(rest, partner(send, 1))
     half = shape(BF, ROWS, WIDE)
-    mine, other = call(finish, (half, half), [SMEM, VMEM], [pltpu.VMEM((2 * ROWS, WIDE), F32)])(
-        place, exchange(send.reshape(4, 2 * ROWS, WIDE), "zh")
+    mine, other = call(finish, (half, half), [SMEM, VMEM, VMEM], [pltpu.VMEM((2 * ROWS, WIDE), F32)])(
+        place, hold, partner(send, 2)
     )
     out = call(place_columns, shape(BF, ROWS, DOUT), [SMEM, VMEM, VMEM])(
         place, mine, partner(other, 0)

time: 122 us -> 122 us (level)
  blocking collectives: 32.2 us -> 12.2 us
  starting transfers between devices: 61.3 us -> 71.8 us
  waiting for transfers between devices: 10.6 us -> 20 us
    all_to_all x2 -> x1, blocking collectives: 32.2 us -> 12.2 us  [exchange(): return lax.all_to_all(x, axis, split_axis=0, concat_axis=0, tiled=True)]
    ppermute x7 -> x9, starting transfers between devices: 48 us -> 58.4 us  [partner(): return lax.ppermute(x, REL, [(i, 2 * z + c) for i, (z, c) in pairs])]
    ppermute x7 -> x9, waiting for transfers between devices: 10.6 us -> 19.3 us  [partner(): return lax.ppermute(x, REL, [(i, 2 * z + c) for i, (z, c) in pairs])]
    pallas_call x2 -> x3, Pallas kernels: 2.79 us -> 2.81 us  [the longest x1 2.23 us: on_device(): call(transform, (pair, shape(F32, 2, 2 * ROWS, WIDE)), [SMEM] + [VMEM] *...]
  transfers between devices with their start and end apart: 9 -> 11, of which waited for: 7 -> 9; matrix products, arithmetic and copies ran while one was open for 1% -> 1% of each run, Pallas kernels for 4% -> 4%
where the time goes in v9:
time: 122 us; the launch traced here: 121 us
  starting transfers between devices  71.8 us (59%)
  waiting for transfers between devices  20 us (16%)
  blocking collectives  12.2 us (10%)
  Pallas kernels  11.9 us (10%)
  local copies, waits for them, and re-layouts  4.02 us (3%)
    ppermute x9, starting transfers between devices, partner(): return lax.ppermute(x, REL, [(i, 2 * z + c) for i, (z, c) in pairs])  58.4 us
    ppermute x9, waiting for transfers between devices, partner(): return lax.ppermute(x, REL, [(i, 2 * z + c) for i, (z, c) in pairs])  19.3 us
    all_to_all x2, starting transfers between devices, exchange(): return lax.all_to_all(x, axis, split_axis=0, concat_axis=0, tiled=True)  13.3 us
    all_to_all x1, blocking collectives, exchange(): return lax.all_to_all(x, axis, split_axis=0, concat_axis=0, tiled=True)  12.2 us
    broadcast_in_dim x2, local copies, waits for them, and re-layouts, spread(): return exchange(jnp.broadcast_to(x, (lax.axis_size(axis), *x.shape)), axis)  2.51 us
  transfers between devices with their start and end apart: 11, of which 9 were waited for; matrix products, arithmetic and copies ran while one was open for 1% of the time, Pallas kernels for 4%

profile of v9, /device:TPU:1, one launch (start us, length us, event | category | flops | bytes accessed | tf_op | source)
XLA Modules:
  0.0 120.9 jit_solution(10954668495519213853)
XLA Ops:
  0.0 2.1 %shard_map.74 = (bf16[16,1024]{1,0:T(8,128)(2,1)}, bf16[4,16,1792]{2,1,0:T(8,128)(2,1)}) custom-call(bf16[16,768]{1,0:T(8,128)(2,1)} %bitcast.20, f32[6,30]{1,0:T(8,128)} %coef_in.1, bf16[12,30,128]{2,1,0:T(8,128)(2,1)} %bitcast.19), custom_call_target="tpu_custom_call" | custom-call | tf_op jit(solution)/shard_map/pallas_call | solution.py:224
  2.1 12.2 %all_to_all.15.gathered = bf16[4,16,1792]{2,1,0:T(8,128)(2,1)S(1)} all-to-all(bf16[4,16,1792]{2,1,0:T(8,128)(2,1)} %get-tuple-element.22), channel_id=1, replica_groups=mesh['y'=4,'x'=4,'zl'=4,'zh'=4,'core'=2] {'zl'}, dimensions={0} | all-to-all | bytes 458752 | tf_op jit(solution)/shard_map/all_to_all | solution.py:207
  14.3 1.3 %broadcast_in_dim.9 = bf16[16,64,768]{2,1,0:T(8,128)(2,1)} broadcast(bf16[64,768]{1,0:T(8,128)(2,1)S(1)} %bitcast.18), dimensions={1,2} | broadcast | bytes 1671168 | tf_op jit(solution)/shard_map/broadcast_in_dim | solution.py:211
  15.6 0.0 copy-start.1
  15.6 0.0 copy-start.2
  15.7 0.0 copy-start.3
  15.7 7.0 %all-to-all-start.1 = ((bf16[16,64,768]{2,1,0:T(8,128)(2,1)}), bf16[16,64,768]{2,1,0:T(8,128)(2,1)S(1)}, u32[]{:S(2)}, u32[]{:S(2)}) async-start(bf16[16,64,768]{2,1,0:T(8,128)(2,1)} %broadcast_in_dim.9), calls=%async_computation.1 | async-start | bytes 3145728 | tf_op jit(solution)/shard_map/all_to_all | solution.py:207
  22.6 0.1 pad_add_fusion.place
  22.7 0.0 copy-done.1
  22.7 0.6 shard_map.75
  23.3 10.9 %collective-permute-start = (bf16[2,112,128]{2,1,0:T(8,128)(2,1)S(1)}, bf16[2,112,128]{2,1,0:T(8,128)(2,1)S(1)}, u32[]{:S(2)}, u32[]{:S(2)}) collective-permute-start(bf16[2,112,128]{2,1,0:T(8,128)(2,1)S(1)} %get-tuple-element.25), channel_id=1, source_target_pairs={{0,2},{1,7},{2,0},{3,5},{4,6},{5,3},{6,4},{7,1},{8,10},{9,15},{10,... | collective-permute-start | bytes 172040 | tf_op jit(solution)/shard_map/ppermute | solution.py:219
  34.2 1.9 %collective-permute-done.got.first = bf16[2,112,128]{2,1,0:T(8,128)(2,1)S(1)} collective-permute-done((bf16[2,112,128]{2,1,0:T(8,128)(2,1)S(1)}, bf16[2,112,128]{2,1,0:T(8,128)(2,1)S(1)}, u32[]{:S(2)}, u32[]{:S(2)}) %collective-permute-start) | collective-permute-done | bytes 57376 | tf_op jit(solution)/shard_map/ppermute | solution.py:219
  36.1 5.0 %collective-permute-start.1 = (bf16[2,112,128]{2,1,0:T(8,128)(2,1)S(1)}, bf16[2,112,128]{2,1,0:T(8,128)(2,1)S(1)}, u32[]{:S(2)}, u32[]{:S(2)}) collective-permute-start(bf16[2,112,128]{2,1,0:T(8,128)(2,1)S(1)} %shard_map.76), channel_id=1, source_target_pairs={{0,6},{1,3},{2,4},{3,1},{4,2},{5,7},{6,0},{7,5},{8,14},{9,11},{10,... | collective-permute-start | bytes 172040 | tf_op jit(solution)/shard_map/ppermute | solution.py:219
  41.8 0.0 copy-done.2
  41.8 0.0 copy-done.3
  41.8 0.0 copy-start
  41.8 1.5 %copy-done = bf16[1,1,56,128,128]{4,3,2,1,0:T(8,128)(2,1)S(1)} copy-done((bf16[1,1,56,128,128]{4,3,2,1,0:T(8,128)(2,1)S(1)}, bf16[1,1,56,128,128]{4,3,2,1,0:T(8,128)(2,1)}, u32[]{:S(2)}) %copy-start) | copy-done | bytes 1835032
  43.3 1.2 shard_map.73.dense
  44.5 0.4 collective-permute-done.1.second
  44.9 0.6 shard_map.77
  45.5 0.0 all-to-all-done.1
  45.5 1.4 %shard_map.78.after = bf16[4,128,512]{2,1,0:T(8,128)(2,1)S(1)} custom-call(s32[2]{0:T(128)S(1)} %pad_add_fusion.place, bf16[6,128,1024]{2,1,0:T(8,128)(2,1)S(1)} %shard_map.73.dense, bf16[1024,768]{1,0:T(8,128)(2,1)S(1)} %bitcast.13, bf16[80,512]{1,0:T(8,128)(2,1)S(1)} %get-tuple-element.27.after), custom_call_target="tpu_custom_call" | custom-call | tf_op jit(solution)/shard_map/pallas_call | solution.py:259
  46.9 8.5 %collective-permute-start.2 = (bf16[4,128,512]{2,1,0:T(8,128)(2,1)S(1)}, bf16[4,128,512]{2,1,0:T(8,128)(2,1)S(1)}, u32[]{:S(2)}, u32[]{:S(2)}) collective-permute-start(bf16[4,128,512]{2,1,0:T(8,128)(2,1)S(1)} %shard_map.78.after), channel_id=1, source_target_pairs={{0,1},{1,0},{2,3},{3,2},{4,5},{5,4},{6,7},{7,6},{8,9},{9,8},{10,11... | collective-permute-start | bytes 1572872 | tf_op jit(solution)/shard_map/ppermute | solution.py:219
  55.4 1.4 %shard_map.79.keep = f32[4,128,512]{2,1,0:T(8,128)S(1)} custom-call(s32[2]{0:T(128)S(1)} %pad_add_fusion.place, bf16[6,128,1024]{2,1,0:T(8,128)(2,1)S(1)} %shard_map.73.dense, bf16[1024,768]{1,0:T(8,128)(2,1)S(1)} %bitcast.14, bf16[4,128,512]{2,1,0:T(8,128)(2,1)S(1)} %shard_map.78.after), custom_call_target="tpu_custom_call" | custom-call | tf_op jit(solution)/shard_map/pallas_call | solution.py:262
  56.8 0.1 collective-permute-done.2.got
  56.9 0.1 shard_map.80
  57.0 7.1 %collective-permute-start.3 = (bf16[2,128,512]{2,1,0:T(8,128)(2,1)S(1)}, bf16[2,128,512]{2,1,0:T(8,128)(2,1)S(1)}, u32[]{:S(2)}, u32[]{:S(2)}) collective-permute-start(bf16[2,128,512]{2,1,0:T(8,128)(2,1)S(1)} %get-tuple-element.29), channel_id=1, source_target_pairs={{0,2},{1,7},{2,0},{3,5},{4,6},{5,3},{6,4},{7,1},{8,10},{9,15},{10,... | collective-permute-start | bytes 786440 | tf_op jit(solution)/shard_map/ppermute | solution.py:219
  64.1 1.2 broadcast_in_dim.10
  65.3 6.4 %all-to-all-start.2 = ((bf16[16,80,512]{2,1,0:T(8,128)(2,1)}), bf16[16,80,512]{2,1,0:T(8,128)(2,1)}, u32[]{:S(2)}, u32[]{:S(2)}) async-start(bf16[16,80,512]{2,1,0:T(8,128)(2,1)} %broadcast_in_dim.10), calls=%async_computation.2 | async-start | bytes 2621440 | tf_op jit(solution)/shard_map/all_to_all | solution.py:207
  71.7 2.8 %collective-permute-done.3.got = bf16[2,128,512]{2,1,0:T(8,128)(2,1)S(1)} collective-permute-done((bf16[2,128,512]{2,1,0:T(8,128)(2,1)S(1)}, bf16[2,128,512]{2,1,0:T(8,128)(2,1)S(1)}, u32[]{:S(2)}, u32[]{:S(2)}) %collective-permute-start.3) | collective-permute-done | bytes 262176 | tf_op jit(solution)/shard_map/ppermute | solution.py:219
  74.6 8.2 %collective-permute-start.4 = (bf16[128,512]{1,0:T(8,128)(2,1)S(1)}, bf16[128,512]{1,0:T(8,128)(2,1)S(1)}, u32[]{:S(2)}, u32[]{:S(2)}) collective-permute-start(bf16[128,512]{1,0:T(8,128)(2,1)S(1)} %get-tuple-element.31), channel_id=1, source_target_pairs={{0,6},{1,3},{2,4},{3,1},{4,2},{5,7},{6,0},{7,5},{8,14},{9,11},{10,... | collective-permute-start | bytes 393224 | tf_op jit(solution)/shard_map/ppermute | solution.py:219
  82.7 3.6 %collective-permute-done.4.got = bf16[128,512]{1,0:T(8,128)(2,1)S(1)} collective-permute-done((bf16[128,512]{1,0:T(8,128)(2,1)S(1)}, bf16[128,512]{1,0:T(8,128)(2,1)S(1)}, u32[]{:S(2)}, u32[]{:S(2)}) %collective-permute-start.4) | collective-permute-done | bytes 131104 | tf_op jit(solution)/shard_map/ppermute | solution.py:219
  86.4 5.2 %collective-permute-start.5 = (bf16[192,512]{1,0:T(8,128)(2,1)S(1)}, bf16[192,512]{1,0:T(8,128)(2,1)}, u32[]{:S(2)}, u32[]{:S(2)}) collective-permute-start(bf16[192,512]{1,0:T(8,128)(2,1)S(1)} %shard_map.82.msgs), channel_id=1, source_target_pairs={{0,1},{1,0},{2,3},{3,2},{4,5},{5,4},{6,7},{7,6},{8,9},{9,8},{10,11... | collective-permute-start | bytes 589832 | tf_op jit(solution)/shard_map/ppermute | solution.py:219
  91.6 0.6 shard_map.83.swap
  92.3 0.7 all-to-all-done.2
  92.9 0.0 collective-permute-done.5.got
  92.9 2.2 %shard_map.84 = (bf16[2,32,512]{2,1,0:T(8,128)(2,1)S(1)}, f32[2,32,512]{2,1,0:T(8,128)S(1)}) custom-call(s32[2]{0:T(128)S(1)} %pad_add_fusion.place, bf16[192,512]{1,0:T(8,128)(2,1)S(1)} %shard_map.82.msgs, bf16[192,512]{1,0:T(8,128)(2,1)} %collective-permute-done.5.got, bf16[1280,1280]{1,0:T(8,128)(2,1)S(1)} %shard_map.83.swap, ...), custom_call_target="tpu_custom_call" | custom-call | tf_op jit(solution)/shard_map/pallas_call | solution.py:277
  95.2 3.1 %collective-permute-start.6 = (bf16[2,32,512]{2,1,0:T(8,128)(2,1)S(1)}, bf16[2,32,512]{2,1,0:T(8,128)(2,1)S(1)}, u32[]{:S(2)}, u32[]{:S(2)}) collective-permute-start(bf16[2,32,512]{2,1,0:T(8,128)(2,1)S(1)} %get-tuple-element.34), channel_id=1, source_target_pairs={{0,2},{1,7},{2,0},{3,5},{4,6},{5,3},{6,4},{7,1},{8,10},{9,15},{10,... | collective-permute-start | bytes 196616 | tf_op jit(solution)/shard_map/ppermute | solution.py:219
  98.3 6.5 %collective-permute-done.6.got = bf16[2,32,512]{2,1,0:T(8,128)(2,1)S(1)} collective-permute-done((bf16[2,32,512]{2,1,0:T(8,128)(2,1)S(1)}, bf16[2,32,512]{2,1,0:T(8,128)(2,1)S(1)}, u32[]{:S(2)}, u32[]{:S(2)}) %collective-permute-start.6) | collective-permute-done | bytes 65568 | tf_op jit(solution)/shard_map/ppermute | solution.py:219
  104.8 5.4 %collective-permute-start.7 = (bf16[32,512]{1,0:T(8,128)(2,1)S(1)}, bf16[32,512]{1,0:T(8,128)(2,1)S(1)}, u32[]{:S(2)}, u32[]{:S(2)}) collective-permute-start(bf16[32,512]{1,0:T(8,128)(2,1)S(1)} %get-tuple-element.36), channel_id=1, source_target_pairs={{0,6},{1,3},{2,4},{3,1},{4,2},{5,7},{6,0},{7,5},{8,14},{9,11},{10,... | collective-permute-start | bytes 98312 | tf_op jit(solution)/shard_map/ppermute | solution.py:219
  110.2 3.2 %collective-permute-done.7.got = bf16[32,512]{1,0:T(8,128)(2,1)S(1)} collective-permute-done((bf16[32,512]{1,0:T(8,128)(2,1)S(1)}, bf16[32,512]{1,0:T(8,128)(2,1)S(1)}, u32[]{:S(2)}, u32[]{:S(2)}) %collective-permute-start.7) | collective-permute-done | bytes 32800 | tf_op jit(solution)/shard_map/ppermute | solution.py:219
  113.3 0.6 shard_map.86
  113.9 5.0 %collective-permute-start.8 = (bf16[16,512]{1,0:T(8,128)(2,1)S(1)}, bf16[16,512]{1,0:T(8,128)(2,1)S(1)}, u32[]{:S(2)}, u32[]{:S(2)}) collective-permute-start(bf16[16,512]{1,0:T(8,128)(2,1)S(1)} %get-tuple-element.38), channel_id=1, source_target_pairs={{0,1},{1,0},{2,3},{3,2},{4,5},{5,4},{6,7},{7,6},{8,9},{9,8},{10,11... | collective-permute-start | bytes 49160 | tf_op jit(solution)/shard_map/ppermute | solution.py:219
  118.9 0.8 collective-permute-done.8.got
  119.7 1.2 shard_map.87
  (5 shorter events, 0.1 us)
Async XLA Ops:
  15.6 7.1 %copy-start.1 = (bf16[16,1024]{1,0:T(8,128)(2,1)S(1)}, bf16[16,1024]{1,0:T(8,128)(2,1)}, u32[]{:S(2)}) copy-start(bf16[16,1024]{1,0:T(8,128)(2,1)} %get-tuple-element.23.padded) | copy-start | bytes 98308
  15.6 26.1 %copy-start.2 = (s32[1,1,56]{2,1,0:T(1,128)S(1)}, s32[1,1,56]{2,1,0:T(1,128)}, u32[]{:S(2)}) copy-start(s32[1,1,56]{2,1,0:T(1,128)} %param.11) | copy-start | bytes 676
  15.7 26.2 %copy-start.3 = (s32[1,1,56]{2,1,0:T(1,128)S(1)}, s32[1,1,56]{2,1,0:T(1,128)}, u32[]{:S(2)}) copy-start(s32[1,1,56]{2,1,0:T(1,128)} %param.12) | copy-start | bytes 676
  15.7 29.8 %all-to-all-start.1 = ((bf16[16,64,768]{2,1,0:T(8,128)(2,1)}), bf16[16,64,768]{2,1,0:T(8,128)(2,1)S(1)}, u32[]{:S(2)}, u32[]{:S(2)}) async-start(bf16[16,64,768]{2,1,0:T(8,128)(2,1)} %broadcast_in_dim.9), calls=%async_computation.1 | async-start | bytes 3145728 | tf_op jit(solution)/shard_map/all_to_all | solution.py:207
  23.3 12.8 %collective-permute-start = (bf16[2,112,128]{2,1,0:T(8,128)(2,1)S(1)}, bf16[2,112,128]{2,1,0:T(8,128)(2,1)S(1)}, u32[]{:S(2)}, u32[]{:S(2)}) collective-permute-start(bf16[2,112,128]{2,1,0:T(8,128)(2,1)S(1)} %get-tuple-element.25), channel_id=1, source_target_pairs={{0,2},{1,7},{2,0},{3,5},{4,6},{5,3},{6,4},{7,1},{8,10},{9,15},{10,... | collective-permute-start | bytes 172040 | tf_op jit(solution)/shard_map/ppermute | solution.py:219
  36.1 8.8 %collective-permute-start.1 = (bf16[2,112,128]{2,1,0:T(8,128)(2,1)S(1)}, bf16[2,112,128]{2,1,0:T(8,128)(2,1)S(1)}, u32[]{:S(2)}, u32[]{:S(2)}) collective-permute-start(bf16[2,112,128]{2,1,0:T(8,128)(2,1)S(1)} %shard_map.76), channel_id=1, source_target_pairs={{0,6},{1,3},{2,4},{3,1},{4,2},{5,7},{6,0},{7,5},{8,14},{9,11},{10,... | collective-permute-start | bytes 172040 | tf_op jit(solution)/shard_map/ppermute | solution.py:219
  41.8 1.5 %copy-start = (bf16[1,1,56,128,128]{4,3,2,1,0:T(8,128)(2,1)S(1)}, bf16[1,1,56,128,128]{4,3,2,1,0:T(8,128)(2,1)}, u32[]{:S(2)}) copy-start(bf16[1,1,56,128,128]{4,3,2,1,0:T(8,128)(2,1)} %param.10) | copy-start | bytes 5505028
  46.9 10.1 %collective-permute-start.2 = (bf16[4,128,512]{2,1,0:T(8,128)(2,1)S(1)}, bf16[4,128,512]{2,1,0:T(8,128)(2,1)S(1)}, u32[]{:S(2)}, u32[]{:S(2)}) collective-permute-start(bf16[4,128,512]{2,1,0:T(8,128)(2,1)S(1)} %shard_map.78.after), channel_id=1, source_target_pairs={{0,1},{1,0},{2,3},{3,2},{4,5},{5,4},{6,7},{7,6},{8,9},{9,8},{10,11... | collective-permute-start | bytes 1572872 | tf_op jit(solution)/shard_map/ppermute | solution.py:219
  57.0 17.5 %collective-permute-start.3 = (bf16[2,128,512]{2,1,0:T(8,128)(2,1)S(1)}, bf16[2,128,512]{2,1,0:T(8,128)(2,1)S(1)}, u32[]{:S(2)}, u32[]{:S(2)}) collective-permute-start(bf16[2,128,512]{2,1,0:T(8,128)(2,1)S(1)} %get-tuple-element.29), channel_id=1, source_target_pairs={{0,2},{1,7},{2,0},{3,5},{4,6},{5,3},{6,4},{7,1},{8,10},{9,15},{10,... | collective-permute-start | bytes 786440 | tf_op jit(solution)/shard_map/ppermute | solution.py:219
  65.3 27.6 %all-to-all-start.2 = ((bf16[16,80,512]{2,1,0:T(8,128)(2,1)}), bf16[16,80,512]{2,1,0:T(8,128)(2,1)}, u32[]{:S(2)}, u32[]{:S(2)}) async-start(bf16[16,80,512]{2,1,0:T(8,128)(2,1)} %broadcast_in_dim.10), calls=%async_computation.2 | async-start | bytes 2621440 | tf_op jit(solution)/shard_map/all_to_all | solution.py:207
  74.6 11.8 %collective-permute-start.4 = (bf16[128,512]{1,0:T(8,128)(2,1)S(1)}, bf16[128,512]{1,0:T(8,128)(2,1)S(1)}, u32[]{:S(2)}, u32[]{:S(2)}) collective-permute-start(bf16[128,512]{1,0:T(8,128)(2,1)S(1)} %get-tuple-element.31), channel_id=1, source_target_pairs={{0,6},{1,3},{2,4},{3,1},{4,2},{5,7},{6,0},{7,5},{8,14},{9,11},{10,... | collective-permute-start | bytes 393224 | tf_op jit(solution)/shard_map/ppermute | solution.py:219
  86.4 6.5 %collective-permute-start.5 = (bf16[192,512]{1,0:T(8,128)(2,1)S(1)}, bf16[192,512]{1,0:T(8,128)(2,1)}, u32[]{:S(2)}, u32[]{:S(2)}) collective-permute-start(bf16[192,512]{1,0:T(8,128)(2,1)S(1)} %shard_map.82.msgs), channel_id=1, source_target_pairs={{0,1},{1,0},{2,3},{3,2},{4,5},{5,4},{6,7},{7,6},{8,9},{9,8},{10,11... | collective-permute-start | bytes 589832 | tf_op jit(solution)/shard_map/ppermute | solution.py:219
  95.2 9.6 %collective-permute-start.6 = (bf16[2,32,512]{2,1,0:T(8,128)(2,1)S(1)}, bf16[2,32,512]{2,1,0:T(8,128)(2,1)S(1)}, u32[]{:S(2)}, u32[]{:S(2)}) collective-permute-start(bf16[2,32,512]{2,1,0:T(8,128)(2,1)S(1)} %get-tuple-element.34), channel_id=1, source_target_pairs={{0,2},{1,7},{2,0},{3,5},{4,6},{5,3},{6,4},{7,1},{8,10},{9,15},{10,... | collective-permute-start | bytes 196616 | tf_op jit(solution)/shard_map/ppermute | solution.py:219
  104.8 8.6 %collective-permute-start.7 = (bf16[32,512]{1,0:T(8,128)(2,1)S(1)}, bf16[32,512]{1,0:T(8,128)(2,1)S(1)}, u32[]{:S(2)}, u32[]{:S(2)}) collective-permute-start(bf16[32,512]{1,0:T(8,128)(2,1)S(1)} %get-tuple-element.36), channel_id=1, source_target_pairs={{0,6},{1,3},{2,4},{3,1},{4,2},{5,7},{6,0},{7,5},{8,14},{9,11},{10,... | collective-permute-start | bytes 98312 | tf_op jit(solution)/shard_map/ppermute | solution.py:219
  113.9 5.8 %collective-permute-start.8 = (bf16[16,512]{1,0:T(8,128)(2,1)S(1)}, bf16[16,512]{1,0:T(8,128)(2,1)S(1)}, u32[]{:S(2)}, u32[]{:S(2)}) collective-permute-start(bf16[16,512]{1,0:T(8,128)(2,1)S(1)} %get-tuple-element.38), channel_id=1, source_target_pairs={{0,1},{1,0},{2,3},{3,2},{4,5},{5,4},{6,7},{7,6},{8,9},{9,8},{10,11... | collective-permute-start | bytes 49160 | tf_op jit(solution)/shard_map/ppermute | solution.py:219

commit v10 on v9

--- a/solution.py
+++ b/solution.py
@@ -30,7 +30,7 @@
 SELF = 2
 CHUNK = SLOT * NODES
 QUART = 2 * (SLOT + SELF)
-DEPTH = QUART * NODES
+PARTS = 5
 WIDE = DOUT // 2
 PIECE = 256
 WEIGHT = 10**11
@@ -61,24 +61,26 @@
         move.start()
     src = lax.broadcasted_iota(jnp.int32, (DIN, DIN), 0)
     out = lax.broadcasted_iota(jnp.int32, (DIN, DIN), 1)
-    swap = jnp.where(src == PER * (out & (NODES - 1)) + (out >> 6), 1.0, 0.0).astype(BF)
+    goal = PER * ((out & (PIECE - 1)) >> 2) + 4 * (out >> 8) + (out & 3)
+    swap = jnp.where(src == goal, 1.0, 0.0).astype(BF)
+    rows[...] = jnp.zeros_like(rows)
     for move in moves:
         move.wait()
     value = jnp.dot(own[...], swap, preferred_element_type=F32).astype(BF)
     padded[:, :DIN] = value
     padded[:, DIN:] = jnp.zeros((ROWS, 8 * TILE - DIN), BF)
-    rows[...] = jnp.zeros_like(rows)
     for d in range(PER):
         part = jnp.dot(
             coef[...], bases[d].astype(F32), precision=lax.Precision.HIGHEST, preferred_element_type=F32
         )
         for r in range(RELS):
-            j = r * PER + d
-            rows[j // SLOT, j % SLOT : j % SLOT + 1] = part[r : r + 1]
-        rows[d // SELF, SLOT + d % SELF : SLOT + d % SELF + 1] = part[RELS :]
+            piece = 3 * r + d // 4
+            spot = piece // 4 * 4 + d % 4
+            rows[piece % 4, spot : spot + 1] = part[r : r + 1]
+        rows[PARTS - 1, d : d + 1] = part[RELS:]
     for i in range(4):
         copies[i, :, :DIN] = value
-        for k in range(8):
+        for k in range(PARTS):
             copies[i, :, DIN + k * TILE : DIN + (k + 1) * TILE] = rows[k].astype(BF)
 
 
@@ -87,23 +89,21 @@
     return zh, zh ^ one, zh ^ 2, zh ^ (4 - one)
 
 
-def sort(place, padded, gathered, send, mine, relay):
+def sort(place, padded, gathered, send, mine, relay, table):
+    wide = gathered[:, :, DIN:].astype(F32)
+    for z in range(4):
+        for i in range(PARTS):
+            rows = [wide[k, 4 * z : 4 * z + 4, i * TILE : (i + 1) * TILE] for k in range(4)]
+            table[z, i * ROWS : (i + 1) * ROWS] = jnp.concatenate(rows, axis=0).astype(BF)
     here, near, far, last = ranks(place[0], place[1])
     for z, ref in ((near, send.at[0]), (far, send.at[1]), (here, mine), (last, relay)):
-        first = z * 2 * TILE
         for i in range(2):
-            ref[i * ROWS : (i + 1) * ROWS] = padded[:, pl.ds(pl.multiple_of(first + i * TILE, TILE), TILE)]
-        rows = []
-        for k in range(4):
-            a, b = (
-                gathered[k, :, pl.ds(pl.multiple_of(DIN + first + i * TILE, TILE), TILE)].astype(F32)
-                for i in range(2)
-            )
-            rows += [a[:SLOT], b[:SLOT], a[SLOT : SLOT + SELF], b[SLOT : SLOT + SELF]]
-        ref[2 * ROWS :] = jnp.concatenate(rows, axis=0).astype(BF)
-
-
-def pass_on(relay, got, send):
+            spot = pl.ds(pl.multiple_of(z * PIECE + i * TILE, TILE), TILE)
+            ref[i * ROWS : (i + 1) * ROWS] = padded[:, spot]
+        ref[2 * ROWS :] = table[z]
+
+
+def pass_on(after, relay, got, send):
     send[0] = relay[...]
     send[1] = got[1]
 
@@ -163,21 +163,22 @@
     msgs[TILE:, 2 * TILE :] = jnp.zeros((4 * ROWS, CHUNK - 2 * TILE), BF)
 
 
-def order(swap):
-    src = lax.broadcasted_iota(jnp.int32, (DEPTH, DEPTH), 0)
-    out = lax.broadcasted_iota(jnp.int32, (DEPTH, DEPTH), 1)
-    swap[...] = jnp.where(out == QUART * (src & (NODES - 1)) + (src >> 6), 1.0, 0.0).astype(BF)
-
-
-def transform(place, msgs, got, swap, weights, send, rest, full, part):
+def transform(place, msgs, got, weights, send, rest, own, part):
     core = place[1]
+
+    def times(value, i):
+        block = weights[:, pl.ds(pl.multiple_of(i * ROWS, ROWS), ROWS)].reshape(PIECE, WIDE)
+        return jnp.dot(value, block, preferred_element_type=F32)
+
+    total = None
     for c, ref in ((core, msgs), (1 - core, got)):
-        full[:, pl.ds(pl.multiple_of(c * CHUNK, CHUNK), CHUNK)] = ref[:TILE]
         for z in range(4):
             spot = pl.ds(pl.multiple_of((2 * z + c) * ROWS, ROWS), ROWS)
-            full[spot, 2 * CHUNK :] = ref[TILE + z * ROWS : TILE + (z + 1) * ROWS, : 2 * TILE]
-    value = jnp.dot(full[...], swap[...], preferred_element_type=F32).astype(BF)
-    part[...] = jnp.dot(value, weights[...], preferred_element_type=F32)
+            own[spot] = ref[TILE + z * ROWS : TILE + (z + 1) * ROWS, :PIECE]
+        for i in range(2):
+            value = times(ref[:TILE, i * PIECE : (i + 1) * PIECE], 2 * c + i)
+            total = value if total is None else total + value
+    part[...] = total + times(own[...], PARTS - 1)
     here, near, far, last = ranks(place[0], place[1])
     for i, z in enumerate((near, far, here, last)):
         rows = part[pl.ds(pl.multiple_of(z * 2 * ROWS, 2 * ROWS), 2 * ROWS)]
@@ -223,13 +224,13 @@
     place = jnp.stack([lax.axis_index(a) for a in REL]).astype(jnp.int32)
     padded, copies = call(
         start,
-        (shape(BF, ROWS, 8 * TILE), shape(BF, 4, ROWS, DIN + 8 * TILE)),
+        (shape(BF, ROWS, 8 * TILE), shape(BF, 4, ROWS, DIN + PARTS * TILE)),
         [HBM] * 3,
         [
             pltpu.VMEM((ROWS, DIN), BF),
             pltpu.VMEM((RELS + 1, bases.shape[0]), F32),
             pltpu.VMEM((PER, bases.shape[0], TILE), BF),
-            pltpu.VMEM((8, ROWS, TILE), F32),
+            pltpu.VMEM((PARTS, ROWS, TILE), F32),
             pltpu.SemaphoreType.DMA((3,)),
         ],
         limit=60,
@@ -246,9 +247,11 @@
 
     block = shape(BF, 2 * ROWS + 4 * QUART, TILE)
     blocks = shape(BF, 2, 2 * ROWS + 4 * QUART, TILE)
-    send, mine, relay = call(sort, (blocks, block, block), [SMEM, VMEM, VMEM])(place, padded, gathered)
+    send, mine, relay = call(sort, (blocks, block, block), [SMEM, VMEM, VMEM], [pltpu.VMEM((4, PARTS * ROWS, TILE), BF)])(
+        place, padded, gathered
+    )
     first = partner(send, 1)
-    relay = call(pass_on, blocks, [VMEM] * 2)(relay, first)
+    relay = call(pass_on, blocks, [ANY, VMEM, VMEM])(dense, relay, first)
     second = partner(relay, 2)
     own, rows = call(
         join_groups,
@@ -270,16 +273,15 @@
         [VMEM] * 2,
         cost=pl.CostEstimate(flops=WEIGHT, bytes_accessed=1 << 20, transcendentals=0),
     )(rest, partner(send, 1))
-    weights = spread(rows, YX).reshape(DEPTH, WIDE)
+    weights = spread(rows, YX)
     msgs = call(settle, shape(BF, TILE + 4 * ROWS, CHUNK), [VMEM] * 3)(hold, partner(send, 2), own)
-    swap = call(order, shape(BF, DEPTH, DEPTH), [])()
     pair = shape(BF, 2, 2 * ROWS, WIDE)
     send, rest = call(
         transform,
         (pair, shape(F32, 2, 2 * ROWS, WIDE)),
-        [SMEM] + [VMEM] * 4,
-        [pltpu.VMEM((TILE, DEPTH), BF), pltpu.VMEM((TILE, WIDE), F32)],
-    )(place, msgs, partner(msgs, 0), swap, weights)
+        [SMEM] + [VMEM] * 3,
+        [pltpu.VMEM((TILE, PIECE), BF), pltpu.VMEM((TILE, WIDE), F32)],
+    )(place, msgs, partner(msgs, 0), weights)
     send, hold = call(
         second_half, (shape(BF, 2 * ROWS, WIDE), shape(F32, 2 * ROWS, WIDE)), [VMEM] * 2
     )(rest, partner(send, 1))

time: 122 us -> 122 us (level)
  waiting for transfers between devices: 20 us -> 31.1 us
  starting transfers between devices: 71.8 us -> 62.8 us
  Pallas kernels: 11.9 us -> 9.96 us
    ppermute x9, starting transfers between devices: 58.4 us -> 48.9 us  [partner(): return lax.ppermute(x, REL, [(i, 2 * z + c) for i, (z, c) in pairs])]
    ppermute x9, waiting for transfers between devices: 19.3 us -> 27.3 us  [partner(): return lax.ppermute(x, REL, [(i, 2 * z + c) for i, (z, c) in pairs])]
    all_to_all x2, waiting for transfers between devices: 0.68 us -> 3.77 us  [exchange(): return lax.all_to_all(x, axis, split_axis=0, concat_axis=0, tiled=True)]
    pallas_call x1, Pallas kernels: 2.23 us -> 0.91 us  [on_device(): call(transform, (pair, shape(F32, 2, 2 * ROWS, WIDE)), [SMEM] + [VMEM] *...]
    pallas_call x4 -> x3, Pallas kernels: 3.34 us -> 2.68 us  [the longest x1 2.1 us: on_device(): call(start, (shape(BF, ROWS, 8 * TILE), shape(BF, 4, ROWS, DIN + PARTS *...]
  transfers between devices with their start and end apart: 11 -> 11, of which waited for: 9 -> 8; matrix products, arithmetic and copies ran while one was open for 1% -> 1% of each run, Pallas kernels for 4% -> 3%
where the time goes in v10:
time: 122 us; the launch traced here: 121 us
  starting transfers between devices  62.8 us (51%)
  waiting for transfers between devices  31.1 us (25%)
  blocking collectives  12.1 us (10%)
  Pallas kernels  9.96 us (8%)
  local copies, waits for them, and re-layouts  4.02 us (3%)
    ppermute x9, starting transfers between devices, partner(): return lax.ppermute(x, REL, [(i, 2 * z + c) for i, (z, c) in pairs])  48.9 us
    ppermute x9, waiting for transfers between devices, partner(): return lax.ppermute(x, REL, [(i, 2 * z + c) for i, (z, c) in pairs])  27.3 us
    all_to_all x2, starting transfers between devices, exchange(): return lax.all_to_all(x, axis, split_axis=0, concat_axis=0, tiled=True)  13.9 us
    all_to_all x1, blocking collectives, exchange(): return lax.all_to_all(x, axis, split_axis=0, concat_axis=0, tiled=True)  12.1 us
    all_to_all x2, waiting for transfers between devices, exchange(): return lax.all_to_all(x, axis, split_axis=0, concat_axis=0, tiled=True)  3.77 us
    broadcast_in_dim x2, local copies, waits for them, and re-layouts, spread(): return exchange(jnp.broadcast_to(x, (lax.axis_size(axis), *x.shape)), axis)  2.5 us
  transfers between devices with their start and end apart: 11, of which 8 were waited for; matrix products, arithmetic and copies ran while one was open for 1% of the time, Pallas kernels for 3%

profile of v10, /device:TPU:1, one launch (start us, length us, event | category | flops | bytes accessed | tf_op | source)
XLA Modules:
  0.0 120.8 jit_solution(13895511257628102634)
XLA Ops:
  0.0 2.1 %shard_map.74 = (bf16[16,1024]{1,0:T(8,128)(2,1)}, bf16[4,16,1408]{2,1,0:T(8,128)(2,1)}) custom-call(bf16[16,768]{1,0:T(8,128)(2,1)} %bitcast.19, f32[6,30]{1,0:T(8,128)} %coef_in.1, bf16[12,30,128]{2,1,0:T(8,128)(2,1)} %bitcast.18), custom_call_target="tpu_custom_call" | custom-call | tf_op jit(solution)/shard_map/pallas_call | solution.py:225
  2.1 12.1 %all_to_all.15.gathered = bf16[4,16,1408]{2,1,0:T(8,128)(2,1)S(1)} all-to-all(bf16[4,16,1408]{2,1,0:T(8,128)(2,1)} %get-tuple-element.22), channel_id=1, replica_groups=mesh['y'=4,'x'=4,'zl'=4,'zh'=4,'core'=2] {'zl'}, dimensions={0} | all-to-all | bytes 360448 | tf_op jit(solution)/shard_map/all_to_all | solution.py:208
  14.2 1.3 %broadcast_in_dim.9 = bf16[16,64,768]{2,1,0:T(8,128)(2,1)} broadcast(bf16[64,768]{1,0:T(8,128)(2,1)S(1)} %bitcast.17), dimensions={1,2} | broadcast | bytes 1671168 | tf_op jit(solution)/shard_map/broadcast_in_dim | solution.py:212
  15.5 0.0 copy-start.1
  15.5 0.0 copy-start.2
  15.5 0.0 copy-start.3
  15.5 6.9 %all-to-all-start.1 = ((bf16[16,64,768]{2,1,0:T(8,128)(2,1)}), bf16[16,64,768]{2,1,0:T(8,128)(2,1)S(1)}, u32[]{:S(2)}, u32[]{:S(2)}) async-start(bf16[16,64,768]{2,1,0:T(8,128)(2,1)} %broadcast_in_dim.9), calls=%async_computation.1 | async-start | bytes 3145728 | tf_op jit(solution)/shard_map/all_to_all | solution.py:208
  22.4 0.1 pad_add_fusion.place
  22.5 0.0 copy-done.1
  22.5 0.6 shard_map.75
  23.1 10.4 %collective-permute-start = (bf16[2,112,128]{2,1,0:T(8,128)(2,1)S(1)}, bf16[2,112,128]{2,1,0:T(8,128)(2,1)S(1)}, u32[]{:S(2)}, u32[]{:S(2)}) collective-permute-start(bf16[2,112,128]{2,1,0:T(8,128)(2,1)S(1)} %get-tuple-element.25), channel_id=1, source_target_pairs={{0,2},{1,7},{2,0},{3,5},{4,6},{5,3},{6,4},{7,1},{8,10},{9,15},{10,... | collective-permute-start | bytes 172040 | tf_op jit(solution)/shard_map/ppermute | solution.py:220
  34.2 0.0 copy-done.2
  34.2 0.0 copy-done.3
  34.2 0.0 copy-start
  34.2 1.5 %copy-done = bf16[1,1,56,128,128]{4,3,2,1,0:T(8,128)(2,1)S(1)} copy-done((bf16[1,1,56,128,128]{4,3,2,1,0:T(8,128)(2,1)S(1)}, bf16[1,1,56,128,128]{4,3,2,1,0:T(8,128)(2,1)}, u32[]{:S(2)}) %copy-start) | copy-done | bytes 1835032
  35.7 1.2 shard_map.73.after.dense
  36.9 0.0 collective-permute-done.got.first
  37.0 5.3 %collective-permute-start.1 = (bf16[2,112,128]{2,1,0:T(8,128)(2,1)S(1)}, bf16[2,112,128]{2,1,0:T(8,128)(2,1)S(1)}, u32[]{:S(2)}, u32[]{:S(2)}) collective-permute-start(bf16[2,112,128]{2,1,0:T(8,128)(2,1)S(1)} %shard_map.76), channel_id=1, source_target_pairs={{0,6},{1,3},{2,4},{3,1},{4,2},{5,7},{6,0},{7,5},{8,14},{9,11},{10,... | collective-permute-start | bytes 172040 | tf_op jit(solution)/shard_map/ppermute | solution.py:220
  42.2 4.8 %collective-permute-done.1.second = bf16[2,112,128]{2,1,0:T(8,128)(2,1)S(1)} collective-permute-done((bf16[2,112,128]{2,1,0:T(8,128)(2,1)S(1)}, bf16[2,112,128]{2,1,0:T(8,128)(2,1)S(1)}, u32[]{:S(2)}, u32[]{:S(2)}) %collective-permute-start.1) | collective-permute-done | bytes 57376 | tf_op jit(solution)/shard_map/ppermute | solution.py:220
  47.0 0.6 shard_map.77
  47.6 0.0 all-to-all-done.1
  47.6 1.4 %shard_map.78.after = bf16[4,128,512]{2,1,0:T(8,128)(2,1)S(1)} custom-call(s32[2]{0:T(128)S(1)} %pad_add_fusion.place, bf16[6,128,1024]{2,1,0:T(8,128)(2,1)S(1)} %shard_map.73.after.dense, bf16[1024,768]{1,0:T(8,128)(2,1)S(1)} %bitcast.12, bf16[80,512]{1,0:T(8,128)(2,1)S(1)} %get-tuple-element.27.after), custom_call_target="tpu_custom_call" | custom-call | tf_op jit(solution)/shard_map/pallas_call | solution.py:262
  49.0 5.5 %collective-permute-start.2 = (bf16[4,128,512]{2,1,0:T(8,128)(2,1)S(1)}, bf16[4,128,512]{2,1,0:T(8,128)(2,1)S(1)}, u32[]{:S(2)}, u32[]{:S(2)}) collective-permute-start(bf16[4,128,512]{2,1,0:T(8,128)(2,1)S(1)} %shard_map.78.after), channel_id=1, source_target_pairs={{0,1},{1,0},{2,3},{3,2},{4,5},{5,4},{6,7},{7,6},{8,9},{9,8},{10,11... | collective-permute-start | bytes 1572872 | tf_op jit(solution)/shard_map/ppermute | solution.py:220
  54.5 1.4 %shard_map.79.keep = f32[4,128,512]{2,1,0:T(8,128)S(1)} custom-call(s32[2]{0:T(128)S(1)} %pad_add_fusion.place, bf16[6,128,1024]{2,1,0:T(8,128)(2,1)S(1)} %shard_map.73.after.dense, bf16[1024,768]{1,0:T(8,128)(2,1)S(1)} %bitcast.13, bf16[4,128,512]{2,1,0:T(8,128)(2,1)S(1)} %shard_map.78.after), custom_call_target="tpu_custom_call" | custom-call | tf_op jit(solution)/shard_map/pallas_call | solution.py:265
  55.9 0.1 collective-permute-done.2.got
  56.0 0.1 shard_map.80
  56.1 7.1 %collective-permute-start.3 = (bf16[2,128,512]{2,1,0:T(8,128)(2,1)S(1)}, bf16[2,128,512]{2,1,0:T(8,128)(2,1)S(1)}, u32[]{:S(2)}, u32[]{:S(2)}) collective-permute-start(bf16[2,128,512]{2,1,0:T(8,128)(2,1)S(1)} %get-tuple-element.29), channel_id=1, source_target_pairs={{0,2},{1,7},{2,0},{3,5},{4,6},{5,3},{6,4},{7,1},{8,10},{9,15},{10,... | collective-permute-start | bytes 786440 | tf_op jit(solution)/shard_map/ppermute | solution.py:220
  63.1 1.2 broadcast_in_dim.10
  64.3 6.9 %all-to-all-start.2 = ((bf16[16,80,512]{2,1,0:T(8,128)(2,1)}), bf16[16,80,512]{2,1,0:T(8,128)(2,1)S(1)}, u32[]{:S(2)}, u32[]{:S(2)}) async-start(bf16[16,80,512]{2,1,0:T(8,128)(2,1)} %broadcast_in_dim.10), calls=%async_computation.2 | async-start | bytes 2621440 | tf_op jit(solution)/shard_map/all_to_all | solution.py:208
  71.3 2.1 %collective-permute-done.3.got = bf16[2,128,512]{2,1,0:T(8,128)(2,1)S(1)} collective-permute-done((bf16[2,128,512]{2,1,0:T(8,128)(2,1)S(1)}, bf16[2,128,512]{2,1,0:T(8,128)(2,1)S(1)}, u32[]{:S(2)}, u32[]{:S(2)}) %collective-permute-start.3) | collective-permute-done | bytes 262176 | tf_op jit(solution)/shard_map/ppermute | solution.py:220
  73.5 7.1 %collective-permute-start.4 = (bf16[128,512]{1,0:T(8,128)(2,1)S(1)}, bf16[128,512]{1,0:T(8,128)(2,1)S(1)}, u32[]{:S(2)}, u32[]{:S(2)}) collective-permute-start(bf16[128,512]{1,0:T(8,128)(2,1)S(1)} %get-tuple-element.31), channel_id=1, source_target_pairs={{0,6},{1,3},{2,4},{3,1},{4,2},{5,7},{6,0},{7,5},{8,14},{9,11},{10,... | collective-permute-start | bytes 393224 | tf_op jit(solution)/shard_map/ppermute | solution.py:220
  80.5 4.1 %collective-permute-done.4.got = bf16[128,512]{1,0:T(8,128)(2,1)S(1)} collective-permute-done((bf16[128,512]{1,0:T(8,128)(2,1)S(1)}, bf16[128,512]{1,0:T(8,128)(2,1)S(1)}, u32[]{:S(2)}, u32[]{:S(2)}) %collective-permute-start.4) | collective-permute-done | bytes 131104 | tf_op jit(solution)/shard_map/ppermute | solution.py:220
  84.7 6.2 %collective-permute-start.5 = (bf16[192,512]{1,0:T(8,128)(2,1)S(1)}, bf16[192,512]{1,0:T(8,128)(2,1)S(1)}, u32[]{:S(2)}, u32[]{:S(2)}) collective-permute-start(bf16[192,512]{1,0:T(8,128)(2,1)S(1)} %shard_map.82.msgs), channel_id=1, source_target_pairs={{0,1},{1,0},{2,3},{3,2},{4,5},{5,4},{6,7},{7,6},{8,9},{9,8},{10,11... | collective-permute-start | bytes 589832 | tf_op jit(solution)/shard_map/ppermute | solution.py:220
  90.8 3.8 %all-to-all-done.2.weights = bf16[16,80,512]{2,1,0:T(8,128)(2,1)S(1)} async-done(((bf16[16,80,512]{2,1,0:T(8,128)(2,1)}), bf16[16,80,512]{2,1,0:T(8,128)(2,1)S(1)}, u32[]{:S(2)}, u32[]{:S(2)}) %all-to-all-start.2) | async-done | bytes 1310752 | tf_op jit(solution)/shard_map/all_to_all | solution.py:208
  94.6 0.0 collective-permute-done.5.got
  94.6 0.9 shard_map.83
  95.5 1.9 %collective-permute-start.6 = (bf16[2,32,512]{2,1,0:T(8,128)(2,1)S(1)}, bf16[2,32,512]{2,1,0:T(8,128)(2,1)S(1)}, u32[]{:S(2)}, u32[]{:S(2)}) collective-permute-start(bf16[2,32,512]{2,1,0:T(8,128)(2,1)S(1)} %get-tuple-element.34), channel_id=1, source_target_pairs={{0,2},{1,7},{2,0},{3,5},{4,6},{5,3},{6,4},{7,1},{8,10},{9,15},{10,... | collective-permute-start | bytes 196616 | tf_op jit(solution)/shard_map/ppermute | solution.py:220
  97.4 8.7 %collective-permute-done.6.got = bf16[2,32,512]{2,1,0:T(8,128)(2,1)S(1)} collective-permute-done((bf16[2,32,512]{2,1,0:T(8,128)(2,1)S(1)}, bf16[2,32,512]{2,1,0:T(8,128)(2,1)S(1)}, u32[]{:S(2)}, u32[]{:S(2)}) %collective-permute-start.6) | collective-permute-done | bytes 65568 | tf_op jit(solution)/shard_map/ppermute | solution.py:220
  106.2 1.9 %collective-permute-start.7 = (bf16[32,512]{1,0:T(8,128)(2,1)S(1)}, bf16[32,512]{1,0:T(8,128)(2,1)S(1)}, u32[]{:S(2)}, u32[]{:S(2)}) collective-permute-start(bf16[32,512]{1,0:T(8,128)(2,1)S(1)} %get-tuple-element.36), channel_id=1, source_target_pairs={{0,6},{1,3},{2,4},{3,1},{4,2},{5,7},{6,0},{7,5},{8,14},{9,11},{10,... | collective-permute-start | bytes 98312 | tf_op jit(solution)/shard_map/ppermute | solution.py:220
  108.1 6.6 %collective-permute-done.7.got = bf16[32,512]{1,0:T(8,128)(2,1)S(1)} collective-permute-done((bf16[32,512]{1,0:T(8,128)(2,1)S(1)}, bf16[32,512]{1,0:T(8,128)(2,1)S(1)}, u32[]{:S(2)}, u32[]{:S(2)}) %collective-permute-start.7) | collective-permute-done | bytes 32800 | tf_op jit(solution)/shard_map/ppermute | solution.py:220
  114.7 0.6 shard_map.85
  115.3 3.5 %collective-permute-start.8 = (bf16[16,512]{1,0:T(8,128)(2,1)S(1)}, bf16[16,512]{1,0:T(8,128)(2,1)S(1)}, u32[]{:S(2)}, u32[]{:S(2)}) collective-permute-start(bf16[16,512]{1,0:T(8,128)(2,1)S(1)} %get-tuple-element.38), channel_id=1, source_target_pairs={{0,1},{1,0},{2,3},{3,2},{4,5},{5,4},{6,7},{7,6},{8,9},{9,8},{10,11... | collective-permute-start | bytes 49160 | tf_op jit(solution)/shard_map/ppermute | solution.py:220
  118.9 0.8 collective-permute-done.8.got
  119.7 1.2 shard_map.86
  (5 shorter events, 0.1 us)
Async XLA Ops:
  15.5 7.0 %copy-start.1 = (bf16[16,1024]{1,0:T(8,128)(2,1)S(1)}, bf16[16,1024]{1,0:T(8,128)(2,1)}, u32[]{:S(2)}) copy-start(bf16[16,1024]{1,0:T(8,128)(2,1)} %get-tuple-element.23.padded) | copy-start | bytes 98308
  15.5 18.7 %copy-start.2 = (s32[1,1,56]{2,1,0:T(1,128)S(1)}, s32[1,1,56]{2,1,0:T(1,128)}, u32[]{:S(2)}) copy-start(s32[1,1,56]{2,1,0:T(1,128)} %param.11) | copy-start | bytes 676
  15.5 18.7 %copy-start.3 = (s32[1,1,56]{2,1,0:T(1,128)S(1)}, s32[1,1,56]{2,1,0:T(1,128)}, u32[]{:S(2)}) copy-start(s32[1,1,56]{2,1,0:T(1,128)} %param.12) | copy-start | bytes 676
  15.5 32.1 %all-to-all-start.1 = ((bf16[16,64,768]{2,1,0:T(8,128)(2,1)}), bf16[16,64,768]{2,1,0:T(8,128)(2,1)S(1)}, u32[]{:S(2)}, u32[]{:S(2)}) async-start(bf16[16,64,768]{2,1,0:T(8,128)(2,1)} %broadcast_in_dim.9), calls=%async_computation.1 | async-start | bytes 3145728 | tf_op jit(solution)/shard_map/all_to_all | solution.py:208
  23.1 13.8 %collective-permute-start = (bf16[2,112,128]{2,1,0:T(8,128)(2,1)S(1)}, bf16[2,112,128]{2,1,0:T(8,128)(2,1)S(1)}, u32[]{:S(2)}, u32[]{:S(2)}) collective-permute-start(bf16[2,112,128]{2,1,0:T(8,128)(2,1)S(1)} %get-tuple-element.25), channel_id=1, source_target_pairs={{0,2},{1,7},{2,0},{3,5},{4,6},{5,3},{6,4},{7,1},{8,10},{9,15},{10,... | collective-permute-start | bytes 172040 | tf_op jit(solution)/shard_map/ppermute | solution.py:220
  34.2 1.5 %copy-start = (bf16[1,1,56,128,128]{4,3,2,1,0:T(8,128)(2,1)S(1)}, bf16[1,1,56,128,128]{4,3,2,1,0:T(8,128)(2,1)}, u32[]{:S(2)}) copy-start(bf16[1,1,56,128,128]{4,3,2,1,0:T(8,128)(2,1)} %param.10) | copy-start | bytes 5505028
  37.0 10.1 %collective-permute-start.1 = (bf16[2,112,128]{2,1,0:T(8,128)(2,1)S(1)}, bf16[2,112,128]{2,1,0:T(8,128)(2,1)S(1)}, u32[]{:S(2)}, u32[]{:S(2)}) collective-permute-start(bf16[2,112,128]{2,1,0:T(8,128)(2,1)S(1)} %shard_map.76), channel_id=1, source_target_pairs={{0,6},{1,3},{2,4},{3,1},{4,2},{5,7},{6,0},{7,5},{8,14},{9,11},{10,... | collective-permute-start | bytes 172040 | tf_op jit(solution)/shard_map/ppermute | solution.py:220
  49.0 7.0 %collective-permute-start.2 = (bf16[4,128,512]{2,1,0:T(8,128)(2,1)S(1)}, bf16[4,128,512]{2,1,0:T(8,128)(2,1)S(1)}, u32[]{:S(2)}, u32[]{:S(2)}) collective-permute-start(bf16[4,128,512]{2,1,0:T(8,128)(2,1)S(1)} %shard_map.78.after), channel_id=1, source_target_pairs={{0,1},{1,0},{2,3},{3,2},{4,5},{5,4},{6,7},{7,6},{8,9},{9,8},{10,11... | collective-permute-start | bytes 1572872 | tf_op jit(solution)/shard_map/ppermute | solution.py:220
  56.1 17.3 %collective-permute-start.3 = (bf16[2,128,512]{2,1,0:T(8,128)(2,1)S(1)}, bf16[2,128,512]{2,1,0:T(8,128)(2,1)S(1)}, u32[]{:S(2)}, u32[]{:S(2)}) collective-permute-start(bf16[2,128,512]{2,1,0:T(8,128)(2,1)S(1)} %get-tuple-element.29), channel_id=1, source_target_pairs={{0,2},{1,7},{2,0},{3,5},{4,6},{5,3},{6,4},{7,1},{8,10},{9,15},{10,... | collective-permute-start | bytes 786440 | tf_op jit(solution)/shard_map/ppermute | solution.py:220
  64.3 30.3 %all-to-all-start.2 = ((bf16[16,80,512]{2,1,0:T(8,128)(2,1)}), bf16[16,80,512]{2,1,0:T(8,128)(2,1)S(1)}, u32[]{:S(2)}, u32[]{:S(2)}) async-start(bf16[16,80,512]{2,1,0:T(8,128)(2,1)} %broadcast_in_dim.10), calls=%async_computation.2 | async-start | bytes 2621440 | tf_op jit(solution)/shard_map/all_to_all | solution.py:208
  73.5 11.2 %collective-permute-start.4 = (bf16[128,512]{1,0:T(8,128)(2,1)S(1)}, bf16[128,512]{1,0:T(8,128)(2,1)S(1)}, u32[]{:S(2)}, u32[]{:S(2)}) collective-permute-start(bf16[128,512]{1,0:T(8,128)(2,1)S(1)} %get-tuple-element.31), channel_id=1, source_target_pairs={{0,6},{1,3},{2,4},{3,1},{4,2},{5,7},{6,0},{7,5},{8,14},{9,11},{10,... | collective-permute-start | bytes 393224 | tf_op jit(solution)/shard_map/ppermute | solution.py:220
  84.7 9.9 %collective-permute-start.5 = (bf16[192,512]{1,0:T(8,128)(2,1)S(1)}, bf16[192,512]{1,0:T(8,128)(2,1)S(1)}, u32[]{:S(2)}, u32[]{:S(2)}) collective-permute-start(bf16[192,512]{1,0:T(8,128)(2,1)S(1)} %shard_map.82.msgs), channel_id=1, source_target_pairs={{0,1},{1,0},{2,3},{3,2},{4,5},{5,4},{6,7},{7,6},{8,9},{9,8},{10,11... | collective-permute-start | bytes 589832 | tf_op jit(solution)/shard_map/ppermute | solution.py:220
  95.5 10.6 %collective-permute-start.6 = (bf16[2,32,512]{2,1,0:T(8,128)(2,1)S(1)}, bf16[2,32,512]{2,1,0:T(8,128)(2,1)S(1)}, u32[]{:S(2)}, u32[]{:S(2)}) collective-permute-start(bf16[2,32,512]{2,1,0:T(8,128)(2,1)S(1)} %get-tuple-element.34), channel_id=1, source_target_pairs={{0,2},{1,7},{2,0},{3,5},{4,6},{5,3},{6,4},{7,1},{8,10},{9,15},{10,... | collective-permute-start | bytes 196616 | tf_op jit(solution)/shard_map/ppermute | solution.py:220
  106.2 8.6 %collective-permute-start.7 = (bf16[32,512]{1,0:T(8,128)(2,1)S(1)}, bf16[32,512]{1,0:T(8,128)(2,1)S(1)}, u32[]{:S(2)}, u32[]{:S(2)}) collective-permute-start(bf16[32,512]{1,0:T(8,128)(2,1)S(1)} %get-tuple-element.36), channel_id=1, source_target_pairs={{0,6},{1,3},{2,4},{3,1},{4,2},{5,7},{6,0},{7,5},{8,14},{9,11},{10,... | collective-permute-start | bytes 98312 | tf_op jit(solution)/shard_map/ppermute | solution.py:220
  115.3 4.4 %collective-permute-start.8 = (bf16[16,512]{1,0:T(8,128)(2,1)S(1)}, bf16[16,512]{1,0:T(8,128)(2,1)S(1)}, u32[]{:S(2)}, u32[]{:S(2)}) collective-permute-start(bf16[16,512]{1,0:T(8,128)(2,1)S(1)} %get-tuple-element.38), channel_id=1, source_target_pairs={{0,1},{1,0},{2,3},{3,2},{4,5},{5,4},{6,7},{7,6},{8,9},{9,8},{10,11... | collective-permute-start | bytes 49160 | tf_op jit(solution)/shard_map/ppermute | solution.py:220

commit v11 on v10

--- a/solution.py
+++ b/solution.py
@@ -129,20 +129,27 @@
     for r in range(RELS):
         for s in range(SRC):
             dense[r, :, s * TILE : (s + 1) * TILE] = acc[r * SRC + s].astype(BF)
-    dense[RELS] = jnp.zeros((TILE, SRC * TILE), BF)
-
-
-def aggregate(owner, place, dense, feats, after, out):
+
+
+def aggregate(owner, place, dense, feats, after, out, rows, full):
     core = place[1] ^ owner
+    for r in range(RELS):
+        for z in range(4):
+            spot = pl.ds(pl.multiple_of((2 * z + core) * ROWS, ROWS), ROWS)
+            rows[(4 * r + z) * ROWS : (4 * r + z + 1) * ROWS] = dense[r, spot]
+    value = jnp.dot(rows[...], feats[...], preferred_element_type=F32)
+    for r in range(RELS):
+        for i in range(3):
+            full[3 * r + i] = value[4 * ROWS * r : 4 * ROWS * (r + 1), i * PIECE : (i + 1) * PIECE]
+    full[3 * RELS] = jnp.zeros((4 * ROWS, PIECE), F32)
     for e, z in enumerate(ranks(place[0], core)):
-        for i in range(2):
-            piece = 2 * (2 * z + core) + i
-            spot = pl.ds(pl.multiple_of(lax.rem(piece, 3) * PIECE, PIECE), PIECE)
-            value = jnp.dot(dense[lax.div(piece, 3)], feats[:, spot], preferred_element_type=F32)
-            out[e, :, i * PIECE : (i + 1) * PIECE] = value.astype(out.dtype)
-
-
-def first_half(keep, got, send, rest):
+        for i in range(4):
+            out[e, :, i * PIECE : (i + 1) * PIECE] = full[4 * z + i].astype(out.dtype)
+
+
+def first_half(keep, got, rows, send, rest, same):
+    same[...] = rows[...]
+
     def total(e):
         return keep[e] + got[e].astype(F32)
 
@@ -157,51 +164,34 @@
     send[...] = (rest[1] + got[1].astype(F32)).astype(BF)
 
 
-def settle(hold, got, own, msgs):
-    msgs[:TILE] = (hold[...] + got[...].astype(F32)).astype(BF)
-    msgs[TILE:, : 2 * TILE] = own[...]
-    msgs[TILE:, 2 * TILE :] = jnp.zeros((4 * ROWS, CHUNK - 2 * TILE), BF)
-
-
-def transform(place, msgs, got, weights, send, rest, own, part):
+def hand(after, value, same):
+    same[...] = value[...]
+
+
+def transform(place, hold, got, own, weights, others, send, rest, part):
     core = place[1]
-
-    def times(value, i):
-        block = weights[:, pl.ds(pl.multiple_of(i * ROWS, ROWS), ROWS)].reshape(PIECE, WIDE)
-        return jnp.dot(value, block, preferred_element_type=F32)
-
-    total = None
-    for c, ref in ((core, msgs), (1 - core, got)):
+    value = (hold[...] + got[...].astype(F32)).astype(BF)
+    for c, ref in ((core, weights), (1 - core, others)):
+        total = None
+        for i in range(PARTS):
+            block = ref[:, i * ROWS : (i + 1) * ROWS].reshape(PIECE, WIDE)
+            left = value[:, i * PIECE : (i + 1) * PIECE] if i < 4 else own[...]
+            term = jnp.dot(left, block, preferred_element_type=F32)
+            total = term if total is None else total + term
         for z in range(4):
-            spot = pl.ds(pl.multiple_of((2 * z + c) * ROWS, ROWS), ROWS)
-            own[spot] = ref[TILE + z * ROWS : TILE + (z + 1) * ROWS, :PIECE]
-        for i in range(2):
-            value = times(ref[:TILE, i * PIECE : (i + 1) * PIECE], 2 * c + i)
-            total = value if total is None else total + value
-    part[...] = total + times(own[...], PARTS - 1)
-    here, near, far, last = ranks(place[0], place[1])
+            spot = pl.ds(pl.multiple_of((2 * z + c) * TILE, TILE), TILE)
+            part[:, spot] = total[:, z * TILE : (z + 1) * TILE]
+    here, near, far, last = ranks(place[0], core)
     for i, z in enumerate((near, far, here, last)):
-        rows = part[pl.ds(pl.multiple_of(z * 2 * ROWS, 2 * ROWS), 2 * ROWS)]
+        rows = part[pl.ds(pl.multiple_of(z * ROWS, ROWS), ROWS)]
         if i < 2:
             send[i] = rows.astype(BF)
         else:
             rest[i - 2] = rows
 
 
-def finish(place, hold, got, mine, other, total):
-    value = hold[...] + got[...].astype(F32)
-    total[...] = jnp.maximum(value, 0.0)
-    core = place[1]
-    mine[...] = total[pl.ds(pl.multiple_of(core * ROWS, ROWS), ROWS)].astype(BF)
-    other[...] = total[pl.ds(pl.multiple_of((1 - core) * ROWS, ROWS), ROWS)].astype(BF)
-
-
-def place_columns(place, mine, got, out):
-    core = place[1]
-    for c, ref in ((core, mine), (1 - core, got)):
-        for z in range(4):
-            spot = pl.ds(pl.multiple_of((2 * z + c) * TILE, TILE), TILE)
-            out[:, spot] = ref[:, z * TILE : (z + 1) * TILE]
+def finish(hold, got, out):
+    out[...] = jnp.maximum(hold[...] + got[...].astype(F32), 0.0).astype(BF)
 
 
 def exchange(x, axis):
@@ -238,7 +228,7 @@
     gathered = exchange(copies, "zl")
     dense = call(
         densify,
-        shape(BF, RELS + 1, TILE, SRC * TILE),
+        shape(BF, RELS, TILE, SRC * TILE),
         [SMEM, SMEM, SMEM, VMEM],
         [pltpu.VMEM((RELS * SRC, TILE, TILE), F32)],
         pl.CostEstimate(flops=1 << 20, bytes_accessed=1 << 23, transcendentals=0),
@@ -259,40 +249,32 @@
         [SMEM] + [VMEM] * 3,
     )(place, mine, first, second)
 
-    send = call(functools.partial(aggregate, 1), shape(BF, 4, TILE, CHUNK), [SMEM, VMEM, VMEM, ANY])(
-        place, dense, feats, rows
-    )
-    keep = call(functools.partial(aggregate, 0), shape(F32, 4, TILE, CHUNK), [SMEM, VMEM, VMEM, ANY])(
-        place, dense, feats, send
-    )
-    two = shape(BF, 2, TILE, CHUNK)
-    send, rest = call(first_half, (two, shape(F32, 2, TILE, CHUNK)), [VMEM] * 2)(keep, partner(send, 0))
+    mid = (4 * ROWS, 4 * PIECE)
+    scratch = [pltpu.VMEM((4 * RELS * ROWS, SRC * TILE), BF), pltpu.VMEM((16, 4 * ROWS, PIECE), F32)]
+    ins = [SMEM, VMEM, VMEM, ANY]
+    send = call(functools.partial(aggregate, 1), shape(BF, 4, *mid), ins, scratch)(place, dense, feats, rows)
+    keep = call(functools.partial(aggregate, 0), shape(F32, 4, *mid), ins, scratch)(place, dense, feats, send)
+    send, rest, rows = call(
+        first_half, (shape(BF, 2, *mid), shape(F32, 2, *mid), shape(BF, 4 * QUART, WIDE)), [VMEM] * 3
+    )(keep, partner(send, 0), rows)
     send, hold = call(
         second_half,
-        (shape(BF, TILE, CHUNK), shape(F32, TILE, CHUNK)),
+        (shape(BF, *mid), shape(F32, *mid)),
         [VMEM] * 2,
         cost=pl.CostEstimate(flops=WEIGHT, bytes_accessed=1 << 20, transcendentals=0),
     )(rest, partner(send, 1))
-    weights = spread(rows, YX)
-    msgs = call(settle, shape(BF, TILE + 4 * ROWS, CHUNK), [VMEM] * 3)(hold, partner(send, 2), own)
-    pair = shape(BF, 2, 2 * ROWS, WIDE)
+    got = partner(send, 2)
+    weights = call(hand, shape(BF, 16, 4 * QUART, WIDE), [ANY, VMEM])(got, spread(rows, YX))
     send, rest = call(
         transform,
-        (pair, shape(F32, 2, 2 * ROWS, WIDE)),
-        [SMEM] + [VMEM] * 3,
-        [pltpu.VMEM((TILE, PIECE), BF), pltpu.VMEM((TILE, WIDE), F32)],
-    )(place, msgs, partner(msgs, 0), weights)
-    send, hold = call(
-        second_half, (shape(BF, 2 * ROWS, WIDE), shape(F32, 2 * ROWS, WIDE)), [VMEM] * 2
-    )(rest, partner(send, 1))
-    half = shape(BF, ROWS, WIDE)
-    mine, other = call(finish, (half, half), [SMEM, VMEM, VMEM], [pltpu.VMEM((2 * ROWS, WIDE), F32)])(
-        place, hold, partner(send, 2)
-    )
-    out = call(place_columns, shape(BF, ROWS, DOUT), [SMEM, VMEM, VMEM])(
-        place, mine, partner(other, 0)
-    )
-    return out[None]
+        (shape(BF, 2, ROWS, DOUT), shape(F32, 2, ROWS, DOUT)),
+        [SMEM] + [VMEM] * 5,
+        [pltpu.VMEM((4 * ROWS, DOUT), F32)],
+    )(place, hold, got, own, weights, partner(weights, 0))
+    send, hold = call(second_half, (shape(BF, ROWS, DOUT), shape(F32, ROWS, DOUT)), [VMEM] * 2)(
+        rest, partner(send, 1)
+    )
+    return call(finish, shape(BF, ROWS, DOUT), [VMEM] * 2)(hold, partner(send, 2))[None]
 
 
 def solution(mesh):

time: 122 us -> 120 us (0.984)
  starting transfers between devices: 62.8 us -> 56.2 us
  waiting for transfers between devices: 31.1 us -> 37.2 us
    ppermute x9 -> x8, starting transfers between devices: 48.9 us -> 42.3 us  [partner(): return lax.ppermute(x, REL, [(i, 2 * z + c) for i, (z, c) in pairs])]
    all_to_all x2, waiting for transfers between devices: 3.77 us -> 9.97 us  [exchange(): return lax.all_to_all(x, axis, split_axis=0, concat_axis=0, tiled=True)]
    pallas_call x10 -> x9, Pallas kernels: 6.72 us -> 5.73 us  [the longest x1 1.29 us: on_device(): call(functools.partial(aggregate, 0), shape(F32, 4, *mid), ins, scratch)]
    ppermute x9 -> x8, waiting for transfers between devices: 27.3 us -> 27.2 us  [partner(): return lax.ppermute(x, REL, [(i, 2 * z + c) for i, (z, c) in pairs])]
  transfers between devices with their start and end apart: 11 -> 10, of which waited for: 8 -> 8; matrix products, arithmetic and copies ran while one was open for 1% -> 1% of each run, Pallas kernels for 3% -> 3%
where the time goes in v11:
time: 120 us; the launch traced here: 119 us
  starting transfers between devices  56.2 us (47%)
  waiting for transfers between devices  37.2 us (31%)
  blocking collectives  12.1 us (10%)
  Pallas kernels  8.96 us (7%)
  local copies, waits for them, and re-layouts  4.03 us (3%)
    ppermute x8, starting transfers between devices, partner(): return lax.ppermute(x, REL, [(i, 2 * z + c) for i, (z, c) in pairs])  42.3 us
    ppermute x8, waiting for transfers between devices, partner(): return lax.ppermute(x, REL, [(i, 2 * z + c) for i, (z, c) in pairs])  27.2 us
    all_to_all x2, starting transfers between devices, exchange(): return lax.all_to_all(x, axis, split_axis=0, concat_axis=0, tiled=True)  13.9 us
    all_to_all x1, blocking collectives, exchange(): return lax.all_to_all(x, axis, split_axis=0, concat_axis=0, tiled=True)  12.1 us
    all_to_all x2, waiting for transfers between devices, exchange(): return lax.all_to_all(x, axis, split_axis=0, concat_axis=0, tiled=True)  9.97 us
    broadcast_in_dim x2, local copies, waits for them, and re-layouts, spread(): return exchange(jnp.broadcast_to(x, (lax.axis_size(axis), *x.shape)), axis)  2.52 us
  transfers between devices with their start and end apart: 10, of which 8 were waited for; matrix products, arithmetic and copies ran while one was open for 1% of the time, Pallas kernels for 3%

profile of v11, /device:TPU:1, one launch (start us, length us, event | category | flops | bytes accessed | tf_op | source)
XLA Modules:
  0.0 119.3 jit_solution(16669515551273369648)
XLA Ops:
  0.0 2.1 %shard_map.74 = (bf16[16,1024]{1,0:T(8,128)(2,1)}, bf16[4,16,1408]{2,1,0:T(8,128)(2,1)}) custom-call(bf16[16,768]{1,0:T(8,128)(2,1)} %bitcast.19, f32[6,30]{1,0:T(8,128)} %coef_in.1, bf16[12,30,128]{2,1,0:T(8,128)(2,1)} %bitcast.18), custom_call_target="tpu_custom_call" | custom-call | tf_op jit(solution)/shard_map/pallas_call | solution.py:215
  2.1 12.1 %all_to_all.15.gathered = bf16[4,16,1408]{2,1,0:T(8,128)(2,1)S(1)} all-to-all(bf16[4,16,1408]{2,1,0:T(8,128)(2,1)} %get-tuple-element.21), channel_id=1, replica_groups=mesh['y'=4,'x'=4,'zl'=4,'zh'=4,'core'=2] {'zl'}, dimensions={0} | all-to-all | bytes 360448 | tf_op jit(solution)/shard_map/all_to_all | solution.py:198
  14.2 1.3 %broadcast_in_dim.9 = bf16[16,64,768]{2,1,0:T(8,128)(2,1)} broadcast(bf16[64,768]{1,0:T(8,128)(2,1)S(1)} %bitcast.17), dimensions={1,2} | broadcast | bytes 1671168 | tf_op jit(solution)/shard_map/broadcast_in_dim | solution.py:202
  15.5 0.0 copy-start.1
  15.5 0.0 copy-start.2
  15.5 0.0 copy-start.3
  15.5 6.9 %all-to-all-start.1 = ((bf16[16,64,768]{2,1,0:T(8,128)(2,1)}), bf16[16,64,768]{2,1,0:T(8,128)(2,1)S(1)}, u32[]{:S(2)}, u32[]{:S(2)}) async-start(bf16[16,64,768]{2,1,0:T(8,128)(2,1)} %broadcast_in_dim.9), calls=%async_computation.1 | async-start | bytes 3145728 | tf_op jit(solution)/shard_map/all_to_all | solution.py:198
  22.4 0.1 pad_add_fusion.place
  22.5 0.0 copy-done.1
  22.5 0.6 shard_map.75
  23.1 10.4 %collective-permute-start = (bf16[2,112,128]{2,1,0:T(8,128)(2,1)S(1)}, bf16[2,112,128]{2,1,0:T(8,128)(2,1)S(1)}, u32[]{:S(2)}, u32[]{:S(2)}) collective-permute-start(bf16[2,112,128]{2,1,0:T(8,128)(2,1)S(1)} %get-tuple-element.24), channel_id=1, source_target_pairs={{0,2},{1,7},{2,0},{3,5},{4,6},{5,3},{6,4},{7,1},{8,10},{9,15},{10,... | collective-permute-start | bytes 172040 | tf_op jit(solution)/shard_map/ppermute | solution.py:210
  34.2 0.0 copy-done.2
  34.2 0.0 copy-done.3
  34.2 0.0 copy-start
  34.2 1.5 %copy-done = bf16[1,1,56,128,128]{4,3,2,1,0:T(8,128)(2,1)S(1)} copy-done((bf16[1,1,56,128,128]{4,3,2,1,0:T(8,128)(2,1)S(1)}, bf16[1,1,56,128,128]{4,3,2,1,0:T(8,128)(2,1)}, u32[]{:S(2)}) %copy-start) | copy-done | bytes 1835032
  35.7 1.2 shard_map.73.after.dense
  36.9 0.0 collective-permute-done.got.first
  36.9 5.2 %collective-permute-start.1 = (bf16[2,112,128]{2,1,0:T(8,128)(2,1)S(1)}, bf16[2,112,128]{2,1,0:T(8,128)(2,1)S(1)}, u32[]{:S(2)}, u32[]{:S(2)}) collective-permute-start(bf16[2,112,128]{2,1,0:T(8,128)(2,1)S(1)} %shard_map.76), channel_id=1, source_target_pairs={{0,6},{1,3},{2,4},{3,1},{4,2},{5,7},{6,0},{7,5},{8,14},{9,11},{10,... | collective-permute-start | bytes 172040 | tf_op jit(solution)/shard_map/ppermute | solution.py:210
  42.1 4.9 %collective-permute-done.1.second = bf16[2,112,128]{2,1,0:T(8,128)(2,1)S(1)} collective-permute-done((bf16[2,112,128]{2,1,0:T(8,128)(2,1)S(1)}, bf16[2,112,128]{2,1,0:T(8,128)(2,1)S(1)}, u32[]{:S(2)}, u32[]{:S(2)}) %collective-permute-start.1) | collective-permute-done | bytes 57376 | tf_op jit(solution)/shard_map/ppermute | solution.py:210
  47.0 0.6 shard_map.77
  47.6 0.0 all-to-all-done.1
  47.6 1.3 %shard_map.78.after = bf16[4,64,1024]{2,1,0:T(8,128)(2,1)S(1)} custom-call(s32[2]{0:T(128)S(1)} %pad_add_fusion.place, bf16[5,128,1024]{2,1,0:T(8,128)(2,1)S(1)} %shard_map.73.after.dense, bf16[1024,768]{1,0:T(8,128)(2,1)S(1)} %bitcast.12, bf16[80,512]{1,0:T(8,128)(2,1)S(1)} %get-tuple-element.26.after.rows), custom_call_target="tpu_custom_call" | custom-call | tf_op jit(solution)/shard_map/pallas_call | solution.py:255
  48.9 5.5 %collective-permute-start.2 = (bf16[4,64,1024]{2,1,0:T(8,128)(2,1)S(1)}, bf16[4,64,1024]{2,1,0:T(8,128)(2,1)S(1)}, u32[]{:S(2)}, u32[]{:S(2)}) collective-permute-start(bf16[4,64,1024]{2,1,0:T(8,128)(2,1)S(1)} %shard_map.78.after), channel_id=1, source_target_pairs={{0,1},{1,0},{2,3},{3,2},{4,5},{5,4},{6,7},{7,6},{8,9},{9,8},{10,11... | collective-permute-start | bytes 1572872 | tf_op jit(solution)/shard_map/ppermute | solution.py:210
  54.4 1.3 %shard_map.79.keep = f32[4,64,1024]{2,1,0:T(8,128)S(1)} custom-call(s32[2]{0:T(128)S(1)} %pad_add_fusion.place, bf16[5,128,1024]{2,1,0:T(8,128)(2,1)S(1)} %shard_map.73.after.dense, bf16[1024,768]{1,0:T(8,128)(2,1)S(1)} %bitcast.13, bf16[4,64,1024]{2,1,0:T(8,128)(2,1)S(1)} %shard_map.78.after), custom_call_target="tpu_custom_call" | custom-call | tf_op jit(solution)/shard_map/pallas_call | solution.py:256
  55.7 0.2 collective-permute-done.2.got
  55.9 0.1 shard_map.80
  56.0 7.1 %collective-permute-start.3 = (bf16[2,64,1024]{2,1,0:T(8,128)(2,1)S(1)}, bf16[2,64,1024]{2,1,0:T(8,128)(2,1)S(1)}, u32[]{:S(2)}, u32[]{:S(2)}) collective-permute-start(bf16[2,64,1024]{2,1,0:T(8,128)(2,1)S(1)} %get-tuple-element.28), channel_id=1, source_target_pairs={{0,2},{1,7},{2,0},{3,5},{4,6},{5,3},{6,4},{7,1},{8,10},{9,15},{10,... | collective-permute-start | bytes 786440 | tf_op jit(solution)/shard_map/ppermute | solution.py:210
  63.1 1.2 %broadcast_in_dim.10 = bf16[16,80,512]{2,1,0:T(8,128)(2,1)} broadcast(bf16[80,512]{1,0:T(8,128)(2,1)S(1)} %get-tuple-element.32), dimensions={1,2} | broadcast | bytes 1392640 | tf_op jit(solution)/shard_map/broadcast_in_dim | solution.py:202
  64.3 6.9 %all-to-all-start.2 = ((bf16[16,80,512]{2,1,0:T(8,128)(2,1)}), bf16[16,80,512]{2,1,0:T(8,128)(2,1)S(1)}, u32[]{:S(2)}, u32[]{:S(2)}) async-start(bf16[16,80,512]{2,1,0:T(8,128)(2,1)} %broadcast_in_dim.10), calls=%async_computation.2 | async-start | bytes 2621440 | tf_op jit(solution)/shard_map/all_to_all | solution.py:198
  71.2 2.1 %collective-permute-done.3.got = bf16[2,64,1024]{2,1,0:T(8,128)(2,1)S(1)} collective-permute-done((bf16[2,64,1024]{2,1,0:T(8,128)(2,1)S(1)}, bf16[2,64,1024]{2,1,0:T(8,128)(2,1)S(1)}, u32[]{:S(2)}, u32[]{:S(2)}) %collective-permute-start.3) | collective-permute-done | bytes 262176 | tf_op jit(solution)/shard_map/ppermute | solution.py:210
  73.4 7.1 %collective-permute-start.4 = (bf16[64,1024]{1,0:T(8,128)(2,1)S(1)}, bf16[64,1024]{1,0:T(8,128)(2,1)S(1)}, u32[]{:S(2)}, u32[]{:S(2)}) collective-permute-start(bf16[64,1024]{1,0:T(8,128)(2,1)S(1)} %get-tuple-element.30), channel_id=1, source_target_pairs={{0,6},{1,3},{2,4},{3,1},{4,2},{5,7},{6,0},{7,5},{8,14},{9,11},{10,... | collective-permute-start | bytes 393224 | tf_op jit(solution)/shard_map/ppermute | solution.py:210
  80.5 4.1 %collective-permute-done.4.after.got = bf16[64,1024]{1,0:T(8,128)(2,1)S(1)} collective-permute-done((bf16[64,1024]{1,0:T(8,128)(2,1)S(1)}, bf16[64,1024]{1,0:T(8,128)(2,1)S(1)}, u32[]{:S(2)}, u32[]{:S(2)}) %collective-permute-start.4) | collective-permute-done | bytes 131104 | tf_op jit(solution)/shard_map/ppermute | solution.py:210
  84.5 10.0 %all-to-all-done.2.value = bf16[16,80,512]{2,1,0:T(8,128)(2,1)S(1)} async-done(((bf16[16,80,512]{2,1,0:T(8,128)(2,1)}), bf16[16,80,512]{2,1,0:T(8,128)(2,1)S(1)}, u32[]{:S(2)}, u32[]{:S(2)}) %all-to-all-start.2) | async-done | bytes 1310752 | tf_op jit(solution)/shard_map/all_to_all | solution.py:198
  94.5 0.1 shard_map.82.weights
  94.6 2.6 %collective-permute-start.5 = (bf16[16,80,512]{2,1,0:T(8,128)(2,1)S(1)}, bf16[16,80,512]{2,1,0:T(8,128)(2,1)S(1)}, u32[]{:S(2)}, u32[]{:S(2)}) collective-permute-start(bf16[16,80,512]{2,1,0:T(8,128)(2,1)S(1)} %shard_map.82.weights), channel_id=1, source_target_pairs={{0,1},{1,0},{2,3},{3,2},{4,5},{5,4},{6,7},{7,6},{8,9},{9,8},{10,11... | collective-permute-start | bytes 3932168 | tf_op jit(solution)/shard_map/ppermute | solution.py:210
  97.3 2.6 %collective-permute-done.5.others = bf16[16,80,512]{2,1,0:T(8,128)(2,1)S(1)} collective-permute-done((bf16[16,80,512]{2,1,0:T(8,128)(2,1)S(1)}, bf16[16,80,512]{2,1,0:T(8,128)(2,1)S(1)}, u32[]{:S(2)}, u32[]{:S(2)}) %collective-permute-start.5) | collective-permute-done | bytes 1310752 | tf_op jit(solution)/shard_map/ppermute | solution.py:210
  99.9 1.1 shard_map.83
  101.0 1.9 %collective-permute-start.6 = (bf16[2,16,1024]{2,1,0:T(8,128)(2,1)S(1)}, bf16[2,16,1024]{2,1,0:T(8,128)(2,1)S(1)}, u32[]{:S(2)}, u32[]{:S(2)}) collective-permute-start(bf16[2,16,1024]{2,1,0:T(8,128)(2,1)S(1)} %get-tuple-element.34), channel_id=1, source_target_pairs={{0,2},{1,7},{2,0},{3,5},{4,6},{5,3},{6,4},{7,1},{8,10},{9,15},{10,... | collective-permute-start | bytes 196616 | tf_op jit(solution)/shard_map/ppermute | solution.py:210
  103.0 7.0 %collective-permute-done.6.got = bf16[2,16,1024]{2,1,0:T(8,128)(2,1)S(1)} collective-permute-done((bf16[2,16,1024]{2,1,0:T(8,128)(2,1)S(1)}, bf16[2,16,1024]{2,1,0:T(8,128)(2,1)S(1)}, u32[]{:S(2)}, u32[]{:S(2)}) %collective-permute-start.6) | collective-permute-done | bytes 65568 | tf_op jit(solution)/shard_map/ppermute | solution.py:210
  110.0 2.5 %collective-permute-start.7 = (bf16[16,1024]{1,0:T(8,128)(2,1)S(1)}, bf16[16,1024]{1,0:T(8,128)(2,1)S(1)}, u32[]{:S(2)}, u32[]{:S(2)}) collective-permute-start(bf16[16,1024]{1,0:T(8,128)(2,1)S(1)} %get-tuple-element.36), channel_id=1, source_target_pairs={{0,6},{1,3},{2,4},{3,1},{4,2},{5,7},{6,0},{7,5},{8,14},{9,11},{10,... | collective-permute-start | bytes 98312 | tf_op jit(solution)/shard_map/ppermute | solution.py:210
  112.4 6.3 %collective-permute-done.7.got = bf16[16,1024]{1,0:T(8,128)(2,1)S(1)} collective-permute-done((bf16[16,1024]{1,0:T(8,128)(2,1)S(1)}, bf16[16,1024]{1,0:T(8,128)(2,1)S(1)}, u32[]{:S(2)}, u32[]{:S(2)}) %collective-permute-start.7) | collective-permute-done | bytes 32800 | tf_op jit(solution)/shard_map/ppermute | solution.py:210
  118.7 0.6 shard_map.85
  (4 shorter events, 0.1 us)
Async XLA Ops:
  15.5 7.0 %copy-start.1 = (bf16[16,1024]{1,0:T(8,128)(2,1)S(1)}, bf16[16,1024]{1,0:T(8,128)(2,1)}, u32[]{:S(2)}) copy-start(bf16[16,1024]{1,0:T(8,128)(2,1)} %get-tuple-element.22.padded) | copy-start | bytes 98308
  15.5 18.7 %copy-start.2 = (s32[1,1,56]{2,1,0:T(1,128)S(1)}, s32[1,1,56]{2,1,0:T(1,128)}, u32[]{:S(2)}) copy-start(s32[1,1,56]{2,1,0:T(1,128)} %param.11) | copy-start | bytes 676
  15.5 18.7 %copy-start.3 = (s32[1,1,56]{2,1,0:T(1,128)S(1)}, s32[1,1,56]{2,1,0:T(1,128)}, u32[]{:S(2)}) copy-start(s32[1,1,56]{2,1,0:T(1,128)} %param.12) | copy-start | bytes 676
  15.5 32.1 %all-to-all-start.1 = ((bf16[16,64,768]{2,1,0:T(8,128)(2,1)}), bf16[16,64,768]{2,1,0:T(8,128)(2,1)S(1)}, u32[]{:S(2)}, u32[]{:S(2)}) async-start(bf16[16,64,768]{2,1,0:T(8,128)(2,1)} %broadcast_in_dim.9), calls=%async_computation.1 | async-start | bytes 3145728 | tf_op jit(solution)/shard_map/all_to_all | solution.py:198
  23.1 13.8 %collective-permute-start = (bf16[2,112,128]{2,1,0:T(8,128)(2,1)S(1)}, bf16[2,112,128]{2,1,0:T(8,128)(2,1)S(1)}, u32[]{:S(2)}, u32[]{:S(2)}) collective-permute-start(bf16[2,112,128]{2,1,0:T(8,128)(2,1)S(1)} %get-tuple-element.24), channel_id=1, source_target_pairs={{0,2},{1,7},{2,0},{3,5},{4,6},{5,3},{6,4},{7,1},{8,10},{9,15},{10,... | collective-permute-start | bytes 172040 | tf_op jit(solution)/shard_map/ppermute | solution.py:210
  34.2 1.5 %copy-start = (bf16[1,1,56,128,128]{4,3,2,1,0:T(8,128)(2,1)S(1)}, bf16[1,1,56,128,128]{4,3,2,1,0:T(8,128)(2,1)}, u32[]{:S(2)}) copy-start(bf16[1,1,56,128,128]{4,3,2,1,0:T(8,128)(2,1)} %param.10) | copy-start | bytes 5505028
  36.9 10.1 %collective-permute-start.1 = (bf16[2,112,128]{2,1,0:T(8,128)(2,1)S(1)}, bf16[2,112,128]{2,1,0:T(8,128)(2,1)S(1)}, u32[]{:S(2)}, u32[]{:S(2)}) collective-permute-start(bf16[2,112,128]{2,1,0:T(8,128)(2,1)S(1)} %shard_map.76), channel_id=1, source_target_pairs={{0,6},{1,3},{2,4},{3,1},{4,2},{5,7},{6,0},{7,5},{8,14},{9,11},{10,... | collective-permute-start | bytes 172040 | tf_op jit(solution)/shard_map/ppermute | solution.py:210
  48.9 7.1 %collective-permute-start.2 = (bf16[4,64,1024]{2,1,0:T(8,128)(2,1)S(1)}, bf16[4,64,1024]{2,1,0:T(8,128)(2,1)S(1)}, u32[]{:S(2)}, u32[]{:S(2)}) collective-permute-start(bf16[4,64,1024]{2,1,0:T(8,128)(2,1)S(1)} %shard_map.78.after), channel_id=1, source_target_pairs={{0,1},{1,0},{2,3},{3,2},{4,5},{5,4},{6,7},{7,6},{8,9},{9,8},{10,11... | collective-permute-start | bytes 1572872 | tf_op jit(solution)/shard_map/ppermute | solution.py:210
  56.0 17.3 %collective-permute-start.3 = (bf16[2,64,1024]{2,1,0:T(8,128)(2,1)S(1)}, bf16[2,64,1024]{2,1,0:T(8,128)(2,1)S(1)}, u32[]{:S(2)}, u32[]{:S(2)}) collective-permute-start(bf16[2,64,1024]{2,1,0:T(8,128)(2,1)S(1)} %get-tuple-element.28), channel_id=1, source_target_pairs={{0,2},{1,7},{2,0},{3,5},{4,6},{5,3},{6,4},{7,1},{8,10},{9,15},{10,... | collective-permute-start | bytes 786440 | tf_op jit(solution)/shard_map/ppermute | solution.py:210
  64.3 30.2 %all-to-all-start.2 = ((bf16[16,80,512]{2,1,0:T(8,128)(2,1)}), bf16[16,80,512]{2,1,0:T(8,128)(2,1)S(1)}, u32[]{:S(2)}, u32[]{:S(2)}) async-start(bf16[16,80,512]{2,1,0:T(8,128)(2,1)} %broadcast_in_dim.10), calls=%async_computation.2 | async-start | bytes 2621440 | tf_op jit(solution)/shard_map/all_to_all | solution.py:198
  73.4 11.2 %collective-permute-start.4 = (bf16[64,1024]{1,0:T(8,128)(2,1)S(1)}, bf16[64,1024]{1,0:T(8,128)(2,1)S(1)}, u32[]{:S(2)}, u32[]{:S(2)}) collective-permute-start(bf16[64,1024]{1,0:T(8,128)(2,1)S(1)} %get-tuple-element.30), channel_id=1, source_target_pairs={{0,6},{1,3},{2,4},{3,1},{4,2},{5,7},{6,0},{7,5},{8,14},{9,11},{10,... | collective-permute-start | bytes 393224 | tf_op jit(solution)/shard_map/ppermute | solution.py:210
  94.6 5.3 %collective-permute-start.5 = (bf16[16,80,512]{2,1,0:T(8,128)(2,1)S(1)}, bf16[16,80,512]{2,1,0:T(8,128)(2,1)S(1)}, u32[]{:S(2)}, u32[]{:S(2)}) collective-permute-start(bf16[16,80,512]{2,1,0:T(8,128)(2,1)S(1)} %shard_map.82.weights), channel_id=1, source_target_pairs={{0,1},{1,0},{2,3},{3,2},{4,5},{5,4},{6,7},{7,6},{8,9},{9,8},{10,11... | collective-permute-start | bytes 3932168 | tf_op jit(solution)/shard_map/ppermute | solution.py:210
  101.0 8.9 %collective-permute-start.6 = (bf16[2,16,1024]{2,1,0:T(8,128)(2,1)S(1)}, bf16[2,16,1024]{2,1,0:T(8,128)(2,1)S(1)}, u32[]{:S(2)}, u32[]{:S(2)}) collective-permute-start(bf16[2,16,1024]{2,1,0:T(8,128)(2,1)S(1)} %get-tuple-element.34), channel_id=1, source_target_pairs={{0,2},{1,7},{2,0},{3,5},{4,6},{5,3},{6,4},{7,1},{8,10},{9,15},{10,... | collective-permute-start | bytes 196616 | tf_op jit(solution)/shard_map/ppermute | solution.py:210
  110.0 8.7 %collective-permute-start.7 = (bf16[16,1024]{1,0:T(8,128)(2,1)S(1)}, bf16[16,1024]{1,0:T(8,128)(2,1)S(1)}, u32[]{:S(2)}, u32[]{:S(2)}) collective-permute-start(bf16[16,1024]{1,0:T(8,128)(2,1)S(1)} %get-tuple-element.36), channel_id=1, source_target_pairs={{0,6},{1,3},{2,4},{3,1},{4,2},{5,7},{6,0},{7,5},{8,14},{9,11},{10,... | collective-permute-start | bytes 98312 | tf_op jit(solution)/shard_map/ppermute | solution.py:210

commit v12 on v11

--- a/solution.py
+++ b/solution.py
@@ -168,16 +168,25 @@
     same[...] = value[...]
 
 
-def transform(place, hold, got, own, weights, others, send, rest, part):
+def product(value, own, block):
+    total = jnp.dot(own, block[:, 4 * ROWS :].reshape(PIECE, WIDE), preferred_element_type=F32)
+    for i in range(4):
+        part = block[:, i * ROWS : (i + 1) * ROWS].reshape(PIECE, WIDE)
+        total = total + jnp.dot(
+            value[:, i * PIECE : (i + 1) * PIECE], part, preferred_element_type=F32
+        )
+    return total
+
+
+def transform_own(hold, got, own, weights, msgs, half):
+    value = (hold[...] + got[...].astype(F32)).astype(BF)
+    msgs[...] = value
+    half[...] = product(value, own[...], weights)
+
+
+def transform(place, msgs, own, half, others, send, rest, part):
     core = place[1]
-    value = (hold[...] + got[...].astype(F32)).astype(BF)
-    for c, ref in ((core, weights), (1 - core, others)):
-        total = None
-        for i in range(PARTS):
-            block = ref[:, i * ROWS : (i + 1) * ROWS].reshape(PIECE, WIDE)
-            left = value[:, i * PIECE : (i + 1) * PIECE] if i < 4 else own[...]
-            term = jnp.dot(left, block, preferred_element_type=F32)
-            total = term if total is None else total + term
+    for c, total in ((core, half[...]), (1 - core, product(msgs[...], own[...], others))):
         for z in range(4):
             spot = pl.ds(pl.multiple_of((2 * z + c) * TILE, TILE), TILE)
             part[:, spot] = total[:, z * TILE : (z + 1) * TILE]
@@ -265,12 +274,16 @@
     )(rest, partner(send, 1))
     got = partner(send, 2)
     weights = call(hand, shape(BF, 16, 4 * QUART, WIDE), [ANY, VMEM])(got, spread(rows, YX))
+    others = partner(weights, 0)
+    msgs, half = call(transform_own, (shape(BF, *mid), shape(F32, 4 * ROWS, WIDE)), [VMEM] * 4)(
+        hold, got, own, weights
+    )
     send, rest = call(
         transform,
         (shape(BF, 2, ROWS, DOUT), shape(F32, 2, ROWS, DOUT)),
-        [SMEM] + [VMEM] * 5,
+        [SMEM] + [VMEM] * 4,
         [pltpu.VMEM((4 * ROWS, DOUT), F32)],
-    )(place, hold, got, own, weights, partner(weights, 0))
+    )(place, msgs, own, half, others)
     send, hold = call(second_half, (shape(BF, ROWS, DOUT), shape(F32, ROWS, DOUT)), [VMEM] * 2)(
         rest, partner(send, 1)
     )

time: 120 us -> 120 us (level)
  transfers between devices with their start and end apart: 10 -> 10, of which waited for: 8 -> 8; matrix products, arithmetic and copies ran while one was open for 1% -> 1% of each run, Pallas kernels for 3% -> 4%
where the time goes in v12:
time: 120 us; the launch traced here: 119 us
  starting transfers between devices  55.5 us (46%)
  waiting for transfers between devices  37.1 us (31%)
  blocking collectives  12.1 us (10%)
  Pallas kernels  9.52 us (8%)
  local copies, waits for them, and re-layouts  4.03 us (3%)
    ppermute x8, starting transfers between devices, partner(): return lax.ppermute(x, REL, [(i, 2 * z + c) for i, (z, c) in pairs])  41.6 us
    ppermute x8, waiting for transfers between devices, partner(): return lax.ppermute(x, REL, [(i, 2 * z + c) for i, (z, c) in pairs])  27.1 us
    all_to_all x2, starting transfers between devices, exchange(): return lax.all_to_all(x, axis, split_axis=0, concat_axis=0, tiled=True)  13.9 us
    all_to_all x1, blocking collectives, exchange(): return lax.all_to_all(x, axis, split_axis=0, concat_axis=0, tiled=True)  12.1 us
    all_to_all x2, waiting for transfers between devices, exchange(): return lax.all_to_all(x, axis, split_axis=0, concat_axis=0, tiled=True)  9.97 us
    broadcast_in_dim x2, local copies, waits for them, and re-layouts, spread(): return exchange(jnp.broadcast_to(x, (lax.axis_size(axis), *x.shape)), axis)  2.51 us
  transfers between devices with their start and end apart: 10, of which 8 were waited for; matrix products, arithmetic and copies ran while one was open for 1% of the time, Pallas kernels for 4%

profile of v12, /device:TPU:1, one launch (start us, length us, event | category | flops | bytes accessed | tf_op | source)
XLA Modules:
  0.0 119.1 jit_solution(13652219441610798550)
XLA Ops:
  0.0 2.1 %shard_map.74 = (bf16[16,1024]{1,0:T(8,128)(2,1)}, bf16[4,16,1408]{2,1,0:T(8,128)(2,1)}) custom-call(bf16[16,768]{1,0:T(8,128)(2,1)} %bitcast.19, f32[6,30]{1,0:T(8,128)} %coef_in.1, bf16[12,30,128]{2,1,0:T(8,128)(2,1)} %bitcast.18), custom_call_target="tpu_custom_call" | custom-call | tf_op jit(solution)/shard_map/pallas_call | solution.py:224
  2.1 12.1 %all_to_all.15.gathered = bf16[4,16,1408]{2,1,0:T(8,128)(2,1)S(1)} all-to-all(bf16[4,16,1408]{2,1,0:T(8,128)(2,1)} %get-tuple-element.23), channel_id=1, replica_groups=mesh['y'=4,'x'=4,'zl'=4,'zh'=4,'core'=2] {'zl'}, dimensions={0} | all-to-all | bytes 360448 | tf_op jit(solution)/shard_map/all_to_all | solution.py:207
  14.2 1.3 %broadcast_in_dim.9 = bf16[16,64,768]{2,1,0:T(8,128)(2,1)} broadcast(bf16[64,768]{1,0:T(8,128)(2,1)S(1)} %bitcast.17), dimensions={1,2} | broadcast | bytes 1671168 | tf_op jit(solution)/shard_map/broadcast_in_dim | solution.py:211
  15.5 0.0 copy-start.1
  15.5 0.0 copy-start.2
  15.5 0.0 copy-start.3
  15.5 6.9 %all-to-all-start.1 = ((bf16[16,64,768]{2,1,0:T(8,128)(2,1)}), bf16[16,64,768]{2,1,0:T(8,128)(2,1)S(1)}, u32[]{:S(2)}, u32[]{:S(2)}) async-start(bf16[16,64,768]{2,1,0:T(8,128)(2,1)} %broadcast_in_dim.9), calls=%async_computation.1 | async-start | bytes 3145728 | tf_op jit(solution)/shard_map/all_to_all | solution.py:207
  22.5 0.1 pad_add_fusion.place
  22.5 0.0 copy-done.1
  22.5 0.6 shard_map.75
  23.1 10.4 %collective-permute-start = (bf16[2,112,128]{2,1,0:T(8,128)(2,1)S(1)}, bf16[2,112,128]{2,1,0:T(8,128)(2,1)S(1)}, u32[]{:S(2)}, u32[]{:S(2)}) collective-permute-start(bf16[2,112,128]{2,1,0:T(8,128)(2,1)S(1)} %get-tuple-element.26), channel_id=1, source_target_pairs={{0,2},{1,7},{2,0},{3,5},{4,6},{5,3},{6,4},{7,1},{8,10},{9,15},{10,... | collective-permute-start | bytes 172040 | tf_op jit(solution)/shard_map/ppermute | solution.py:219
  34.2 0.0 copy-done.2
  34.2 0.0 copy-done.3
  34.2 0.0 copy-start
  34.2 1.5 %copy-done = bf16[1,1,56,128,128]{4,3,2,1,0:T(8,128)(2,1)S(1)} copy-done((bf16[1,1,56,128,128]{4,3,2,1,0:T(8,128)(2,1)S(1)}, bf16[1,1,56,128,128]{4,3,2,1,0:T(8,128)(2,1)}, u32[]{:S(2)}) %copy-start) | copy-done | bytes 1835032
  35.7 1.6 %shard_map.73.after.dense = bf16[5,128,1024]{2,1,0:T(8,128)(2,1)S(1)} custom-call(s32[1]{0:T(128)} %bitcast.11.count, s32[56]{0:T(128)S(1)} %bitcast.15, s32[56]{0:T(128)S(1)} %bitcast.16, bf16[56,128,128]{2,1,0:T(8,128)(2,1)S(1)} %bitcast.14), custom_call_target="tpu_custom_call" | custom-call | flops 1048576 | bytes 8388608 | tf_op jit(solution)/shard_map/pallas_call | solution.py:238
  37.3 0.0 collective-permute-done.got.first
  37.4 4.7 %collective-permute-start.1 = (bf16[2,112,128]{2,1,0:T(8,128)(2,1)S(1)}, bf16[2,112,128]{2,1,0:T(8,128)(2,1)S(1)}, u32[]{:S(2)}, u32[]{:S(2)}) collective-permute-start(bf16[2,112,128]{2,1,0:T(8,128)(2,1)S(1)} %shard_map.76), channel_id=1, source_target_pairs={{0,6},{1,3},{2,4},{3,1},{4,2},{5,7},{6,0},{7,5},{8,14},{9,11},{10,... | collective-permute-start | bytes 172040 | tf_op jit(solution)/shard_map/ppermute | solution.py:219
  42.1 5.2 %collective-permute-done.1.second = bf16[2,112,128]{2,1,0:T(8,128)(2,1)S(1)} collective-permute-done((bf16[2,112,128]{2,1,0:T(8,128)(2,1)S(1)}, bf16[2,112,128]{2,1,0:T(8,128)(2,1)S(1)}, u32[]{:S(2)}, u32[]{:S(2)}) %collective-permute-start.1) | collective-permute-done | bytes 57376 | tf_op jit(solution)/shard_map/ppermute | solution.py:219
  47.3 0.6 shard_map.77
  47.8 0.0 all-to-all-done.1
  47.8 1.3 %shard_map.78.after = bf16[4,64,1024]{2,1,0:T(8,128)(2,1)S(1)} custom-call(s32[2]{0:T(128)S(1)} %pad_add_fusion.place, bf16[5,128,1024]{2,1,0:T(8,128)(2,1)S(1)} %shard_map.73.after.dense, bf16[1024,768]{1,0:T(8,128)(2,1)S(1)} %bitcast.12, bf16[80,512]{1,0:T(8,128)(2,1)S(1)} %get-tuple-element.28.after.rows), custom_call_target="tpu_custom_call" | custom-call | tf_op jit(solution)/shard_map/pallas_call | solution.py:264
  49.1 5.3 %collective-permute-start.2 = (bf16[4,64,1024]{2,1,0:T(8,128)(2,1)S(1)}, bf16[4,64,1024]{2,1,0:T(8,128)(2,1)S(1)}, u32[]{:S(2)}, u32[]{:S(2)}) collective-permute-start(bf16[4,64,1024]{2,1,0:T(8,128)(2,1)S(1)} %shard_map.78.after), channel_id=1, source_target_pairs={{0,1},{1,0},{2,3},{3,2},{4,5},{5,4},{6,7},{7,6},{8,9},{9,8},{10,11... | collective-permute-start | bytes 1572872 | tf_op jit(solution)/shard_map/ppermute | solution.py:219
  54.4 1.3 %shard_map.79.keep = f32[4,64,1024]{2,1,0:T(8,128)S(1)} custom-call(s32[2]{0:T(128)S(1)} %pad_add_fusion.place, bf16[5,128,1024]{2,1,0:T(8,128)(2,1)S(1)} %shard_map.73.after.dense, bf16[1024,768]{1,0:T(8,128)(2,1)S(1)} %bitcast.13, bf16[4,64,1024]{2,1,0:T(8,128)(2,1)S(1)} %shard_map.78.after), custom_call_target="tpu_custom_call" | custom-call | tf_op jit(solution)/shard_map/pallas_call | solution.py:265
  55.7 0.2 collective-permute-done.2.got
  55.9 0.1 shard_map.80
  56.0 7.1 %collective-permute-start.3 = (bf16[2,64,1024]{2,1,0:T(8,128)(2,1)S(1)}, bf16[2,64,1024]{2,1,0:T(8,128)(2,1)S(1)}, u32[]{:S(2)}, u32[]{:S(2)}) collective-permute-start(bf16[2,64,1024]{2,1,0:T(8,128)(2,1)S(1)} %get-tuple-element.30), channel_id=1, source_target_pairs={{0,2},{1,7},{2,0},{3,5},{4,6},{5,3},{6,4},{7,1},{8,10},{9,15},{10,... | collective-permute-start | bytes 786440 | tf_op jit(solution)/shard_map/ppermute | solution.py:219
  63.1 1.2 %broadcast_in_dim.10 = bf16[16,80,512]{2,1,0:T(8,128)(2,1)} broadcast(bf16[80,512]{1,0:T(8,128)(2,1)S(1)} %get-tuple-element.34), dimensions={1,2} | broadcast | bytes 1392640 | tf_op jit(solution)/shard_map/broadcast_in_dim | solution.py:211
  64.3 6.9 %all-to-all-start.2 = ((bf16[16,80,512]{2,1,0:T(8,128)(2,1)}), bf16[16,80,512]{2,1,0:T(8,128)(2,1)S(1)}, u32[]{:S(2)}, u32[]{:S(2)}) async-start(bf16[16,80,512]{2,1,0:T(8,128)(2,1)} %broadcast_in_dim.10), calls=%async_computation.2 | async-start | bytes 2621440 | tf_op jit(solution)/shard_map/all_to_all | solution.py:207
  71.2 2.1 %collective-permute-done.3.got = bf16[2,64,1024]{2,1,0:T(8,128)(2,1)S(1)} collective-permute-done((bf16[2,64,1024]{2,1,0:T(8,128)(2,1)S(1)}, bf16[2,64,1024]{2,1,0:T(8,128)(2,1)S(1)}, u32[]{:S(2)}, u32[]{:S(2)}) %collective-permute-start.3) | collective-permute-done | bytes 262176 | tf_op jit(solution)/shard_map/ppermute | solution.py:219
  73.4 7.1 %collective-permute-start.4 = (bf16[64,1024]{1,0:T(8,128)(2,1)S(1)}, bf16[64,1024]{1,0:T(8,128)(2,1)S(1)}, u32[]{:S(2)}, u32[]{:S(2)}) collective-permute-start(bf16[64,1024]{1,0:T(8,128)(2,1)S(1)} %get-tuple-element.32), channel_id=1, source_target_pairs={{0,6},{1,3},{2,4},{3,1},{4,2},{5,7},{6,0},{7,5},{8,14},{9,11},{10,... | collective-permute-start | bytes 393224 | tf_op jit(solution)/shard_map/ppermute | solution.py:219
  80.5 4.1 %collective-permute-done.4.after.got = bf16[64,1024]{1,0:T(8,128)(2,1)S(1)} collective-permute-done((bf16[64,1024]{1,0:T(8,128)(2,1)S(1)}, bf16[64,1024]{1,0:T(8,128)(2,1)S(1)}, u32[]{:S(2)}, u32[]{:S(2)}) %collective-permute-start.4) | collective-permute-done | bytes 131104 | tf_op jit(solution)/shard_map/ppermute | solution.py:219
  84.6 10.0 %all-to-all-done.2.value = bf16[16,80,512]{2,1,0:T(8,128)(2,1)S(1)} async-done(((bf16[16,80,512]{2,1,0:T(8,128)(2,1)}), bf16[16,80,512]{2,1,0:T(8,128)(2,1)S(1)}, u32[]{:S(2)}, u32[]{:S(2)}) %all-to-all-start.2) | async-done | bytes 1310752 | tf_op jit(solution)/shard_map/all_to_all | solution.py:207
  94.5 0.1 shard_map.82.weights
  94.6 2.6 %collective-permute-start.5 = (bf16[16,80,512]{2,1,0:T(8,128)(2,1)S(1)}, bf16[16,80,512]{2,1,0:T(8,128)(2,1)S(1)}, u32[]{:S(2)}, u32[]{:S(2)}) collective-permute-start(bf16[16,80,512]{2,1,0:T(8,128)(2,1)S(1)} %shard_map.82.weights), channel_id=1, source_target_pairs={{0,1},{1,0},{2,3},{3,2},{4,5},{5,4},{6,7},{7,6},{8,9},{9,8},{10,11... | collective-permute-start | bytes 3932168 | tf_op jit(solution)/shard_map/ppermute | solution.py:219
  97.3 0.3 shard_map.83
  97.6 2.3 %collective-permute-done.5.others = bf16[16,80,512]{2,1,0:T(8,128)(2,1)S(1)} collective-permute-done((bf16[16,80,512]{2,1,0:T(8,128)(2,1)S(1)}, bf16[16,80,512]{2,1,0:T(8,128)(2,1)S(1)}, u32[]{:S(2)}, u32[]{:S(2)}) %collective-permute-start.5) | collective-permute-done | bytes 1310752 | tf_op jit(solution)/shard_map/ppermute | solution.py:219
  99.9 0.9 shard_map.84
  100.8 1.9 %collective-permute-start.6 = (bf16[2,16,1024]{2,1,0:T(8,128)(2,1)S(1)}, bf16[2,16,1024]{2,1,0:T(8,128)(2,1)S(1)}, u32[]{:S(2)}, u32[]{:S(2)}) collective-permute-start(bf16[2,16,1024]{2,1,0:T(8,128)(2,1)S(1)} %get-tuple-element.38), channel_id=1, source_target_pairs={{0,2},{1,7},{2,0},{3,5},{4,6},{5,3},{6,4},{7,1},{8,10},{9,15},{10,... | collective-permute-start | bytes 196616 | tf_op jit(solution)/shard_map/ppermute | solution.py:219
  102.7 7.0 %collective-permute-done.6.got = bf16[2,16,1024]{2,1,0:T(8,128)(2,1)S(1)} collective-permute-done((bf16[2,16,1024]{2,1,0:T(8,128)(2,1)S(1)}, bf16[2,16,1024]{2,1,0:T(8,128)(2,1)S(1)}, u32[]{:S(2)}, u32[]{:S(2)}) %collective-permute-start.6) | collective-permute-done | bytes 65568 | tf_op jit(solution)/shard_map/ppermute | solution.py:219
  109.8 2.5 %collective-permute-start.7 = (bf16[16,1024]{1,0:T(8,128)(2,1)S(1)}, bf16[16,1024]{1,0:T(8,128)(2,1)S(1)}, u32[]{:S(2)}, u32[]{:S(2)}) collective-permute-start(bf16[16,1024]{1,0:T(8,128)(2,1)S(1)} %get-tuple-element.40), channel_id=1, source_target_pairs={{0,6},{1,3},{2,4},{3,1},{4,2},{5,7},{6,0},{7,5},{8,14},{9,11},{10,... | collective-permute-start | bytes 98312 | tf_op jit(solution)/shard_map/ppermute | solution.py:219
  112.2 6.3 %collective-permute-done.7.got = bf16[16,1024]{1,0:T(8,128)(2,1)S(1)} collective-permute-done((bf16[16,1024]{1,0:T(8,128)(2,1)S(1)}, bf16[16,1024]{1,0:T(8,128)(2,1)S(1)}, u32[]{:S(2)}, u32[]{:S(2)}) %collective-permute-start.7) | collective-permute-done | bytes 32800 | tf_op jit(solution)/shard_map/ppermute | solution.py:219
  118.5 0.6 shard_map.86
  (4 shorter events, 0.1 us)
Async XLA Ops:
  15.5 7.0 %copy-start.1 = (bf16[16,1024]{1,0:T(8,128)(2,1)S(1)}, bf16[16,1024]{1,0:T(8,128)(2,1)}, u32[]{:S(2)}) copy-start(bf16[16,1024]{1,0:T(8,128)(2,1)} %get-tuple-element.24.padded) | copy-start | bytes 98308
  15.5 18.7 %copy-start.2 = (s32[1,1,56]{2,1,0:T(1,128)S(1)}, s32[1,1,56]{2,1,0:T(1,128)}, u32[]{:S(2)}) copy-start(s32[1,1,56]{2,1,0:T(1,128)} %param.11) | copy-start | bytes 676
  15.5 18.7 %copy-start.3 = (s32[1,1,56]{2,1,0:T(1,128)S(1)}, s32[1,1,56]{2,1,0:T(1,128)}, u32[]{:S(2)}) copy-start(s32[1,1,56]{2,1,0:T(1,128)} %param.12) | copy-start | bytes 676
  15.5 32.3 %all-to-all-start.1 = ((bf16[16,64,768]{2,1,0:T(8,128)(2,1)}), bf16[16,64,768]{2,1,0:T(8,128)(2,1)S(1)}, u32[]{:S(2)}, u32[]{:S(2)}) async-start(bf16[16,64,768]{2,1,0:T(8,128)(2,1)} %broadcast_in_dim.9), calls=%async_computation.1 | async-start | bytes 3145728 | tf_op jit(solution)/shard_map/all_to_all | solution.py:207
  23.1 14.2 %collective-permute-start = (bf16[2,112,128]{2,1,0:T(8,128)(2,1)S(1)}, bf16[2,112,128]{2,1,0:T(8,128)(2,1)S(1)}, u32[]{:S(2)}, u32[]{:S(2)}) collective-permute-start(bf16[2,112,128]{2,1,0:T(8,128)(2,1)S(1)} %get-tuple-element.26), channel_id=1, source_target_pairs={{0,2},{1,7},{2,0},{3,5},{4,6},{5,3},{6,4},{7,1},{8,10},{9,15},{10,... | collective-permute-start | bytes 172040 | tf_op jit(solution)/shard_map/ppermute | solution.py:219
  34.2 1.5 %copy-start = (bf16[1,1,56,128,128]{4,3,2,1,0:T(8,128)(2,1)S(1)}, bf16[1,1,56,128,128]{4,3,2,1,0:T(8,128)(2,1)}, u32[]{:S(2)}) copy-start(bf16[1,1,56,128,128]{4,3,2,1,0:T(8,128)(2,1)} %param.10) | copy-start | bytes 5505028
  37.4 9.9 %collective-permute-start.1 = (bf16[2,112,128]{2,1,0:T(8,128)(2,1)S(1)}, bf16[2,112,128]{2,1,0:T(8,128)(2,1)S(1)}, u32[]{:S(2)}, u32[]{:S(2)}) collective-permute-start(bf16[2,112,128]{2,1,0:T(8,128)(2,1)S(1)} %shard_map.76), channel_id=1, source_target_pairs={{0,6},{1,3},{2,4},{3,1},{4,2},{5,7},{6,0},{7,5},{8,14},{9,11},{10,... | collective-permute-start | bytes 172040 | tf_op jit(solution)/shard_map/ppermute | solution.py:219
  49.1 6.8 %collective-permute-start.2 = (bf16[4,64,1024]{2,1,0:T(8,128)(2,1)S(1)}, bf16[4,64,1024]{2,1,0:T(8,128)(2,1)S(1)}, u32[]{:S(2)}, u32[]{:S(2)}) collective-permute-start(bf16[4,64,1024]{2,1,0:T(8,128)(2,1)S(1)} %shard_map.78.after), channel_id=1, source_target_pairs={{0,1},{1,0},{2,3},{3,2},{4,5},{5,4},{6,7},{7,6},{8,9},{9,8},{10,11... | collective-permute-start | bytes 1572872 | tf_op jit(solution)/shard_map/ppermute | solution.py:219
  56.0 17.3 %collective-permute-start.3 = (bf16[2,64,1024]{2,1,0:T(8,128)(2,1)S(1)}, bf16[2,64,1024]{2,1,0:T(8,128)(2,1)S(1)}, u32[]{:S(2)}, u32[]{:S(2)}) collective-permute-start(bf16[2,64,1024]{2,1,0:T(8,128)(2,1)S(1)} %get-tuple-element.30), channel_id=1, source_target_pairs={{0,2},{1,7},{2,0},{3,5},{4,6},{5,3},{6,4},{7,1},{8,10},{9,15},{10,... | collective-permute-start | bytes 786440 | tf_op jit(solution)/shard_map/ppermute | solution.py:219
  64.3 30.2 %all-to-all-start.2 = ((bf16[16,80,512]{2,1,0:T(8,128)(2,1)}), bf16[16,80,512]{2,1,0:T(8,128)(2,1)S(1)}, u32[]{:S(2)}, u32[]{:S(2)}) async-start(bf16[16,80,512]{2,1,0:T(8,128)(2,1)} %broadcast_in_dim.10), calls=%async_computation.2 | async-start | bytes 2621440 | tf_op jit(solution)/shard_map/all_to_all | solution.py:207
  73.4 11.2 %collective-permute-start.4 = (bf16[64,1024]{1,0:T(8,128)(2,1)S(1)}, bf16[64,1024]{1,0:T(8,128)(2,1)S(1)}, u32[]{:S(2)}, u32[]{:S(2)}) collective-permute-start(bf16[64,1024]{1,0:T(8,128)(2,1)S(1)} %get-tuple-element.32), channel_id=1, source_target_pairs={{0,6},{1,3},{2,4},{3,1},{4,2},{5,7},{6,0},{7,5},{8,14},{9,11},{10,... | collective-permute-start | bytes 393224 | tf_op jit(solution)/shard_map/ppermute | solution.py:219
  94.6 5.3 %collective-permute-start.5 = (bf16[16,80,512]{2,1,0:T(8,128)(2,1)S(1)}, bf16[16,80,512]{2,1,0:T(8,128)(2,1)S(1)}, u32[]{:S(2)}, u32[]{:S(2)}) collective-permute-start(bf16[16,80,512]{2,1,0:T(8,128)(2,1)S(1)} %shard_map.82.weights), channel_id=1, source_target_pairs={{0,1},{1,0},{2,3},{3,2},{4,5},{5,4},{6,7},{7,6},{8,9},{9,8},{10,11... | collective-permute-start | bytes 3932168 | tf_op jit(solution)/shard_map/ppermute | solution.py:219
  100.8 8.9 %collective-permute-start.6 = (bf16[2,16,1024]{2,1,0:T(8,128)(2,1)S(1)}, bf16[2,16,1024]{2,1,0:T(8,128)(2,1)S(1)}, u32[]{:S(2)}, u32[]{:S(2)}) collective-permute-start(bf16[2,16,1024]{2,1,0:T(8,128)(2,1)S(1)} %get-tuple-element.38), channel_id=1, source_target_pairs={{0,2},{1,7},{2,0},{3,5},{4,6},{5,3},{6,4},{7,1},{8,10},{9,15},{10,... | collective-permute-start | bytes 196616 | tf_op jit(solution)/shard_map/ppermute | solution.py:219
  109.8 8.7 %collective-permute-start.7 = (bf16[16,1024]{1,0:T(8,128)(2,1)S(1)}, bf16[16,1024]{1,0:T(8,128)(2,1)S(1)}, u32[]{:S(2)}, u32[]{:S(2)}) collective-permute-start(bf16[16,1024]{1,0:T(8,128)(2,1)S(1)} %get-tuple-element.40), channel_id=1, source_target_pairs={{0,6},{1,3},{2,4},{3,1},{4,2},{5,7},{6,0},{7,5},{8,14},{9,11},{10,... | collective-permute-start | bytes 98312 | tf_op jit(solution)/shard_map/ppermute | solution.py:219
